TPU v7x, 32 devices: a whole 2x2x4 slice. The times are simulated.
32 devices in a mesh: groups: 2 (over x), seq: 16 (over z, y, core).
Axes of the slice: x: 2, y: 2, z: 4, core: 2. Of those that a mesh axis runs over, the one named last changes fastest.
Arguments:
- queries: bfloat16 [4096, 5120], P(('groups', 'seq')), parts along dimension 0, may hold values from -12 to 12
- keys: bfloat16 [4096, 5120], P(('groups', 'seq')), parts along dimension 0, may hold values from -12 to 12
- values: bfloat16 [4096, 5120], P(('groups', 'seq')), parts along dimension 0, may hold values from -6 to 6
- q_gain: float32 [5120], replicated, may hold values from 0.1 to 1.9
- k_gain: float32 [5120], replicated, may hold values from 0.1 to 1.9
- key_tiles: int32 [40, 16, 16], replicated, may hold values from 0 to 15, as said below
- key_count: int32 [40, 16], replicated, may hold values from 1 to 16
Outputs:
- attended: bfloat16 [4096, 5120], P(('groups', 'seq')), parts along dimension 0
There are 2 independent parts, one for each index of `groups`. A program takes and returns all parts, laid end to end along the dimension named above; an argument that names none is the same for every part. Nothing has to cross between parts.
Inputs may be any that keep to these rules, and one draw needn't show every extreme that they name: key_tiles[h, t] holds 16 distinct tiles and its first entry is t itself.
All inputs are finite; a program needn't handle non-finite values.
Results may differ from a plain program's by a relative error of at most 0.012.
The roundings to bfloat16 on the way count: a program that leaves them out, or rounds other values in their place, can miss the bound.
Values may be sent and summed in bfloat16 or wider, within the bound.
No kernel may reach another device: no remote copies, remote signals or barrier semaphores. Data moves between devices by JAX's collectives and lax.ppermute only.
A program may use at most 128 MiB of HBM per device.

v0:
```python
import math

import jax
import jax.numpy as jnp
from jax import lax
from jax.sharding import PartitionSpec as P

HEADS = 40
HEAD_DIM = 128
TILE = 128


group_size = 4


def normed(rows, gain):
    values32 = rows.astype(jnp.float32)
    factor = lax.rsqrt(jnp.mean(values32 * values32, axis=-1, keepdims=True) + 1e-06)
    return (values32 * factor * gain).astype(jnp.bfloat16)


def padded(entries, length):
    return jnp.pad(entries, (0, length - entries.shape[0]), mode="edge")


def attend_units(received, slot_index, tile_index, head_index, key_tiles, key_count):

    def one_group(unit_items):
        slot_part, tile_part, head_part = unit_items
        query_rows = received[tile_part, slot_part, 0]
        key_lists = key_tiles[head_part, tile_part]
        counts = key_count[head_part, tile_part]
        key_block = received[key_lists, slot_part[:, None], 1]
        value_block = received[key_lists, slot_part[:, None], 2]
        units = query_rows.shape[0]
        tile_rows = query_rows.shape[1]
        key_flat = key_block.reshape(units, -1, key_block.shape[-1])
        value_flat = value_block.reshape(units, -1, value_block.shape[-1])
        scores = jnp.einsum(
            "uqd,ukd->uqk", query_rows, key_flat, preferred_element_type=jnp.float32
        ) / math.sqrt(query_rows.shape[-1])
        list_place = jnp.arange(key_flat.shape[1]) // tile_rows
        valid = (list_place[None, :] < counts[:, None])[:, None, :]
        masked = jnp.where(valid, scores, -jnp.inf)
        peak = jnp.max(masked, axis=-1, keepdims=True)
        weights = jnp.where(valid, jnp.exp(masked - peak), jnp.float32(0.0))
        total = jnp.sum(weights, axis=-1, keepdims=True)
        probs = weights.astype(jnp.bfloat16)
        mixed = (
            jnp.einsum("uqk,ukd->uqd", probs, value_flat, preferred_element_type=jnp.float32)
            / total
        )
        return mixed.astype(jnp.bfloat16)

    grouped = (
        slot_index.reshape(-1, group_size),
        tile_index.reshape(-1, group_size),
        head_index.reshape(-1, group_size),
    )
    result = lax.map(one_group, grouped)
    return result.reshape(-1, result.shape[2], result.shape[3])


def local(queries, keys, values, q_gain, k_gain, key_tiles, key_count):
    devices = lax.axis_size("seq")
    my_index = lax.axis_index("seq")
    q_normed = normed(queries, q_gain)
    k_normed = normed(keys, k_gain)
    stacked = (
        jnp.stack([q_normed, k_normed, values])
        .reshape(3, TILE, HEADS, HEAD_DIM)
        .transpose(2, 0, 1, 3)
    )
    targets = jnp.arange(devices)
    per_device = (HEADS + devices - 1) // devices
    total_slots = devices * per_device
    fewest_slots = total_slots // HEADS
    most_units = (devices + fewest_slots - 1) // fewest_slots

    def slot_layout(slot_number):
        head_of = slot_number * HEADS // total_slots
        head_start = (head_of * total_slots + HEADS - 1) // HEADS
        head_end = ((head_of + 1) * total_slots + HEADS - 1) // HEADS
        sharers = head_end - head_start
        within = slot_number - head_start
        return (head_of, within * devices // sharers, (within + 1) * devices // sharers)

    all_slots = jnp.arange(total_slots).reshape(devices, per_device)
    send_heads = slot_layout(all_slots)[0]
    received = lax.all_to_all(stacked[send_heads], "seq", split_axis=0, concat_axis=0, tiled=True)
    own_heads, lower_tile, upper_tile = slot_layout(my_index * per_device + jnp.arange(per_device))
    offsets = jnp.arange(most_units)
    tile_grid = jnp.minimum(lower_tile[:, None] + offsets[None, :], devices - 1)
    slot_grid = jnp.broadcast_to(jnp.arange(per_device)[:, None], tile_grid.shape)
    head_grid = jnp.broadcast_to(own_heads[:, None], tile_grid.shape)
    unit_total = per_device * most_units
    length = (unit_total + group_size - 1) // group_size * group_size
    finished = attend_units(
        received,
        padded(slot_grid.reshape(-1), length),
        padded(tile_grid.reshape(-1), length),
        padded(head_grid.reshape(-1), length),
        key_tiles,
        key_count,
    )[:unit_total]
    finished = finished.reshape(per_device, most_units, TILE, HEAD_DIM)
    position = targets[:, None] - lower_tile[None, :]
    inside = (position >= 0) & (targets[:, None] < upper_tile[None, :])
    gathered = finished[jnp.arange(per_device)[None, :], jnp.clip(position, 0, most_units - 1)]
    outgoing = jnp.where(inside[:, :, None, None], gathered, jnp.zeros_like(gathered))
    returned = lax.all_to_all(outgoing, "seq", split_axis=0, concat_axis=0, tiled=True)
    head_list = jnp.arange(HEADS)
    head_start = (head_list * total_slots + HEADS - 1) // HEADS
    sharers = ((head_list + 1) * total_slots + HEADS - 1) // HEADS - head_start
    owner_slot = head_start + ((my_index + 1) * sharers - 1) // devices
    pieces = returned[owner_slot // per_device, owner_slot % per_device]
    return pieces.transpose(1, 0, 2).reshape(TILE, HEADS * HEAD_DIM)


def solution(mesh):
    in_specs = (
        P(("groups", "seq"), None),
        P(("groups", "seq"), None),
        P(("groups", "seq"), None),
        P(),
        P(),
        P(),
        P(),
    )
    out_specs = P(("groups", "seq"), None)
    return jax.shard_map(local, mesh=mesh, in_specs=in_specs, out_specs=out_specs, check_vma=False)
```

profile of v0, /device:TPU:0, one launch (start us, length us, event | category | flops | bytes accessed | tf_op | source)
XLA Modules:
  0.0 386.7 jit_solution(15004399506665328456)
XLA Ops:
  15.7 3.4 maximum_bitcast_fusion
  19.1 5.6 %gather_fusion.5 = bf16[48,3,128,128]{3,2,1,0:T(8,128)(2,1)} fusion(bf16[40,3,128,128]{3,2,1,0:T(8,128)(2,1)} %maximum_bitcast_fusion, s32[1024]{0:T(1024)S(1)} %pad_clamp_fusion), kind=kCustom, calls=%fused_computation.5 | custom fusion | bytes 9437376 | tf_op jit(solution)/shard_map/gather | solution.py:90
  24.7 7.6 %all-to-all-start = ((bf16[16,3,3,128,128]{4,3,2,1,0:T(8,128)(2,1)}), bf16[16,3,3,128,128]{4,3,2,1,0:T(8,128)(2,1)}, u32[]{:S(2)}, u32[]{:S(2)}) async-start(bf16[16,3,3,128,128]{4,3,2,1,0:T(8,128)(2,1)} %bitcast.90), calls=%async_computation | async-start | bytes 9437184 | tf_op jit(solution)/shard_map/all_to_all | solution.py:90
  33.4 85.7 %all-to-all-done = bf16[16,3,3,128,128]{4,3,2,1,0:T(8,128)(2,1)} async-done(((bf16[16,3,3,128,128]{4,3,2,1,0:T(8,128)(2,1)}), bf16[16,3,3,128,128]{4,3,2,1,0:T(8,128)(2,1)}, u32[]{:S(2)}, u32[]{:S(2)}) %all-to-all-start) | async-done | bytes 4718624 | tf_op jit(solution)/shard_map/all_to_all | solution.py:90
  119.2 206.7 %while.12 = (s32[]{:T(128)}, bf16[12,4,128,128]{3,2,1,0:T(8,128)(2,1)}, s32[12,4]{1,0:T(8,128)S(1)}, s32[12,4]{1,0:T(8,128)S(1)}, s32[40,16]{0,1:T(8,128)S(1)}, ...) while((s32[]{:T(128)}, ...), condition=%wide.region_5.6_spmd, body=%wide.region_2.5_spmd.sunk | while | flops 543320704 | bytes 17343108 | solution.py:60
  120.0 3.4 gather_fusion.4
  130.1 3.4 gather_fusion.1
  137.2 3.4 gather_fusion.4
  147.3 3.4 gather_fusion.1
  154.4 3.4 gather_fusion.4
  164.5 3.4 gather_fusion.1
  171.7 3.4 gather_fusion.4
  181.8 3.4 gather_fusion.1
  188.9 3.4 gather_fusion.4
  199.0 3.4 gather_fusion.1
  206.1 3.4 gather_fusion.4
  216.2 3.4 gather_fusion.1
  223.3 3.4 gather_fusion.4
  233.4 3.4 gather_fusion.1
  240.6 3.4 gather_fusion.4
  250.7 3.4 gather_fusion.1
  257.8 3.4 gather_fusion.4
  267.9 3.4 gather_fusion.1
  271.2 3.0 fusion.77
  275.0 3.4 gather_fusion.4
  285.1 3.4 gather_fusion.1
  292.3 3.4 gather_fusion.4
  302.4 3.4 gather_fusion.1
  309.5 3.4 gather_fusion.4
  319.6 3.4 gather_fusion.1
  329.7 21.7 %all-to-all-start.1 = ((bf16[16,3,128,128]{3,2,1,0:T(8,128)(2,1)}), bf16[16,3,128,128]{3,2,1,0:T(8,128)(2,1)S(1)}, u32[]{:S(2)}, u32[]{:S(2)}) async-start(bf16[16,3,128,128]{3,2,1,0:T(8,128)(2,1)} %broadcast_select_fusion), calls=%async_computation.1 | async-start | bytes 3145728 | tf_op jit(solution)/shard_map/all_to_all | solution.py:111
  351.5 31.9 %all-to-all-done.1 = bf16[16,3,128,128]{3,2,1,0:T(8,128)(2,1)S(1)} async-done(((bf16[16,3,128,128]{3,2,1,0:T(8,128)(2,1)}), bf16[16,3,128,128]{3,2,1,0:T(8,128)(2,1)S(1)}, u32[]{:S(2)}, u32[]{:S(2)}) %all-to-all-start.1) | async-done | bytes 1572896 | tf_op jit(solution)/shard_map/all_to_all | solution.py:111
  (194 shorter events, 146.8 us)
Async XLA Ops:
  0.0 2.5 copy-start.3
  6.2 2.5 copy-start.4
  12.3 3.4 copy-start.1
  24.7 8.3 %copy-start.2 = (s32[40,16,16]{0,2,1:T(8,128)S(1)}, s32[40,16,16]{0,2,1:T(8,128)}, u32[]{:S(2)}) copy-start(s32[40,16,16]{0,2,1:T(8,128)} %param.14) | copy-start | bytes 122884
  24.7 94.5 %copy-start = (s32[40,16]{0,1:T(8,128)S(1)}, s32[40,16]{0,1:T(8,128)}, u32[]{:S(2)}) copy-start(s32[40,16]{0,1:T(8,128)} %param.15) | copy-start | bytes 7684
  24.7 94.4 %all-to-all-start = ((bf16[16,3,3,128,128]{4,3,2,1,0:T(8,128)(2,1)}), bf16[16,3,3,128,128]{4,3,2,1,0:T(8,128)(2,1)}, u32[]{:S(2)}, u32[]{:S(2)}) async-start(bf16[16,3,3,128,128]{4,3,2,1,0:T(8,128)(2,1)} %bitcast.90), calls=%async_computation | async-start | bytes 9437184 | tf_op jit(solution)/shard_map/all_to_all | solution.py:90
  329.7 53.7 %all-to-all-start.1 = ((bf16[16,3,128,128]{3,2,1,0:T(8,128)(2,1)}), bf16[16,3,128,128]{3,2,1,0:T(8,128)(2,1)S(1)}, u32[]{:S(2)}, u32[]{:S(2)}) async-start(bf16[16,3,128,128]{3,2,1,0:T(8,128)(2,1)} %broadcast_select_fusion), calls=%async_computation.1 | async-start | bytes 3145728 | tf_op jit(solution)/shard_map/all_to_all | solution.py:111
where the time goes:
time: 392 us; the launch traced here: 387 us
  local copies, waits for them, and re-layouts  154 us (39%)
  waiting for transfers between devices  118 us (30%)
  matrix products  72.1 us (18%)
  starting transfers between devices  29.3 us (7%)
  other arithmetic  13 us (3%)
    all_to_all x1, waiting for transfers between devices, local(): lax.all_to_all(stacked[send_heads], 'seq', split_axis=0, concat_axis=0, t...  85.7 us
    gather x12, local copies, waits for them, and re-layouts, one_group(): key_block = received[key_lists, slot_part[:, None], 1]  40.2 us
    gather x12, local copies, waits for them, and re-layouts, one_group(): value_block = received[key_lists, slot_part[:, None], 2]  40.2 us
    sub x12, matrix products, one_group(): weights = jnp.where(valid, jnp.exp(masked - peak), jnp.float32(0.0))  36.1 us
    dot_general x12, matrix products, one_group(): jnp.einsum('uqk,ukd->uqd', probs, value_flat, preferred_element_type=jnp....  36 us
    gather x12, local copies, waits for them, and re-layouts, one_group(): query_rows = received[tile_part, slot_part, 0]  35 us
    all_to_all x1, waiting for transfers between devices, local(): lax.all_to_all(outgoing, 'seq', split_axis=0, concat_axis=0, tiled=True)  31.9 us
    all_to_all x1, starting transfers between devices, local(): lax.all_to_all(outgoing, 'seq', split_axis=0, concat_axis=0, tiled=True)  21.7 us
  transfers between devices with their start and end apart: 2, of which 2 were waited for; matrix products, arithmetic and copies ran while one was open for 0% of the time, Pallas kernels for 0%

commit v1 on v0

--- a/solution.py
+++ b/solution.py
@@ -1,8 +1,11 @@
+import functools
 import math
 
 import jax
 import jax.numpy as jnp
 from jax import lax
+from jax.experimental import pallas as pl
+from jax.experimental.pallas import tpu as pltpu
 from jax.sharding import PartitionSpec as P
 
 HEADS = 40
@@ -61,7 +64,7 @@
     return result.reshape(-1, result.shape[2], result.shape[3])
 
 
-def local(queries, keys, values, q_gain, k_gain, key_tiles, key_count):
+def local_general(queries, keys, values, q_gain, k_gain, key_tiles, key_count):
     devices = lax.axis_size("seq")
     my_index = lax.axis_index("seq")
     q_normed = normed(queries, q_gain)
@@ -117,6 +120,301 @@
     return pieces.transpose(1, 0, 2).reshape(TILE, HEADS * HEAD_DIM)
 
 
+HALF = TILE // 2
+VMEM_BYTES = 48 * 1024 * 1024
+
+
+def pair_layout(devices):
+    per_pair = 2 * HEADS // devices
+    full = per_pair // 2
+    places = []
+    for head in range(HEADS):
+        pair, within = divmod(head, per_pair)
+        if within < full:
+            places.append([(2 * pair, within)])
+        elif within >= per_pair - full:
+            places.append([(2 * pair + 1, within - (per_pair - full))])
+        else:
+            places.append([(2 * pair, full), (2 * pair + 1, full)])
+    return places, full
+
+
+def put_head(parts, places, head, block):
+    holders = places[head]
+    for which, (device, slot) in enumerate(holders):
+        if slot not in parts:
+            continue
+        ref, unit = parts[slot]
+        if len(holders) == 2:
+            ref[device, unit] = block[which * HALF : (which + 1) * HALF]
+        else:
+            ref[device, unit] = block[:HALF]
+            ref[device, unit + 1] = block[HALF:]
+
+
+def head_columns(head):
+    return slice(head * HEAD_DIM, (head + 1) * HEAD_DIM)
+
+
+def normed_blocks(rows_ref, gain_ref):
+    squares = jnp.zeros((TILE, HEAD_DIM), jnp.float32)
+    for head in range(HEADS):
+        block = rows_ref[:, head_columns(head)].astype(jnp.float32)
+        squares = squares + block * block
+    mean = jnp.sum(squares, axis=-1, keepdims=True) / (HEADS * HEAD_DIM)
+    factor = lax.rsqrt(mean + 1e-06)
+    for head in range(HEADS):
+        block = rows_ref[:, head_columns(head)].astype(jnp.float32)
+        yield head, (block * factor * gain_ref[:, head_columns(head)]).astype(jnp.bfloat16)
+
+
+def values_kernel(places, full, values_ref, out_ref):
+    parts = {slot: (out_ref, 2 * slot) for slot in range(full + 1)}
+    for head in range(HEADS):
+        put_head(parts, places, head, values_ref[:, head_columns(head)])
+
+
+def norm_kernel(
+    places, full, early, queries_ref, keys_ref, q_gain_ref, k_gain_ref, first_ref, second_ref
+):
+    query_parts = {
+        slot: (first_ref, 2 * slot) if slot < early else (second_ref, 2 * (slot - early))
+        for slot in range(full + 1)
+    }
+    key_parts = {slot: (first_ref, 2 * (early + slot)) for slot in range(full + 1)}
+    for head, block in normed_blocks(keys_ref, k_gain_ref):
+        put_head(key_parts, places, head, block)
+    for head, block in normed_blocks(queries_ref, q_gain_ref):
+        put_head(query_parts, places, head, block)
+
+
+def attend_rows(queries, keys, values, masks):
+    rows = queries[0].shape[0]
+    tiles = keys.shape[0] // TILE
+    stacked = jnp.concatenate(queries, axis=0)
+    scores = lax.dot_general(
+        stacked, keys, (((1,), (1,)), ((), ())), preferred_element_type=jnp.float32
+    )
+    scale = jnp.float32(math.log2(math.e) / math.sqrt(HEAD_DIM))
+    probs, totals = [], []
+    for i, mask in enumerate(masks):
+        parts = []
+        for tile in range(tiles):
+            offset = jnp.where((mask >> tile) & 1 == 1, jnp.float32(0.0), jnp.float32(-1e30))
+            part = scores[i * rows : (i + 1) * rows, tile * TILE : (tile + 1) * TILE]
+            parts.append(part + offset)
+        peak = jnp.max(functools.reduce(jnp.maximum, parts), axis=-1, keepdims=True)
+        weights = [jnp.exp2((part - peak) * scale) for part in parts]
+        totals.append(jnp.sum(functools.reduce(jnp.add, weights), axis=-1, keepdims=True))
+        probs.append(jnp.concatenate([w.astype(jnp.bfloat16) for w in weights], axis=1))
+    mixed = jnp.dot(jnp.concatenate(probs, axis=0), values, preferred_element_type=jnp.float32)
+    return [
+        (mixed[i * rows : (i + 1) * rows] / totals[i]).astype(jnp.bfloat16)
+        for i in range(len(masks))
+    ]
+
+
+def attend_head(mask_ref, mask_row, query_at, keys_at, values_at, store, tiles, together):
+    def step(index, carry):
+        first = index * together
+        out = attend_rows(
+            [query_at(first + i) for i in range(together)],
+            keys_at(),
+            values_at(),
+            [mask_ref[mask_row, first + i] for i in range(together)],
+        )
+        for i in range(together):
+            store(first + i, out[i])
+        return carry
+
+    lax.fori_loop(0, tiles // together, step, 0)
+
+
+def whole_head(ref, unit):
+    return ref[:, unit : unit + 2].reshape(-1, HEAD_DIM)
+
+
+def whole_heads(mask_ref, heads, query_ref, first_ref, value_ref, out_ref, query_slot, early):
+    tiles = query_ref.shape[0]
+    for row, slot in heads:
+        unit = 2 * (slot - query_slot)
+
+        def store(tile, block, unit=unit):
+            out_ref[tile, unit] = block[:HALF]
+            out_ref[tile, unit + 1] = block[HALF:]
+
+        attend_head(
+            mask_ref,
+            row,
+            lambda tile, unit=unit: query_ref[tile, unit : unit + 2].reshape(TILE, HEAD_DIM),
+            lambda slot=slot: whole_head(first_ref, 2 * (early + slot)),
+            lambda slot=slot: whole_head(value_ref, 2 * slot),
+            store,
+            tiles,
+            2,
+        )
+
+
+def early_kernel(early, mask_ref, first_ref, value_ref, out_ref):
+    heads = [(slot, slot) for slot in range(early)]
+    whole_heads(mask_ref, heads, first_ref, first_ref, value_ref, out_ref, 0, early)
+
+
+def late_kernel(
+    early,
+    full,
+    mask_ref,
+    second_ref,
+    first_ref,
+    value_ref,
+    other_key_ref,
+    other_value_ref,
+    out_ref,
+    key_scratch,
+    value_scratch,
+):
+    heads = [(slot, slot) for slot in range(early, full)]
+    whole_heads(mask_ref, heads, second_ref, first_ref, value_ref, out_ref, early, early)
+    key_scratch[:, 0] = first_ref[:, 2 * (early + full)]
+    key_scratch[:, 1] = other_key_ref[...]
+    value_scratch[:, 0] = value_ref[:, 2 * full]
+    value_scratch[:, 1] = other_value_ref[...]
+    unit = 2 * (full - early)
+
+    def store(tile, block):
+        out_ref[tile, unit] = block
+
+    attend_head(
+        mask_ref,
+        full,
+        lambda tile: second_ref[tile, unit],
+        lambda: whole_head(key_scratch, 0),
+        lambda: whole_head(value_scratch, 0),
+        store,
+        second_ref.shape[0],
+        4,
+    )
+
+
+def collect_kernel(places, early, early_ref, late_ref, out_ref):
+    for head in range(HEADS):
+        for which, (device, slot) in enumerate(places[head]):
+            ref, unit = (early_ref, 2 * slot) if slot < early else (late_ref, 2 * (slot - early))
+            columns = head_columns(head)
+            if len(places[head]) == 2:
+                out_ref[which * HALF : (which + 1) * HALF, columns] = ref[device, unit]
+            else:
+                out_ref[:HALF, columns] = ref[device, unit]
+                out_ref[HALF:, columns] = ref[device, unit + 1]
+
+
+def on_chip(kernel, name, out_shapes, *operands, smem=0, scratch=()):
+    in_vmem = pl.BlockSpec(memory_space=pltpu.VMEM)
+    in_smem = pl.BlockSpec(memory_space=pltpu.SMEM)
+    outs = [jax.ShapeDtypeStruct(shape, jnp.bfloat16) for shape in out_shapes]
+    return pl.pallas_call(
+        kernel,
+        name=name,
+        out_shape=outs,
+        in_specs=[in_smem] * smem + [in_vmem] * (len(operands) - smem),
+        out_specs=[in_vmem] * len(outs),
+        scratch_shapes=list(scratch),
+        compiler_params=pltpu.CompilerParams(vmem_limit_bytes=VMEM_BYTES),
+    )(*operands)
+
+
+def exchange(blocks):
+    return lax.all_to_all(blocks, "seq", split_axis=0, concat_axis=0, tiled=True)
+
+
+def after(value, *others):
+    return lax.optimization_barrier((value, *others))[0]
+
+
+def local_paired(queries, keys, values, q_gain, k_gain, key_tiles, key_count):
+    devices = lax.axis_size("seq")
+    my_index = lax.axis_index("seq")
+    places, full = pair_layout(devices)
+    early = full // 2
+    units = 2 * full + 1
+    swap = [(i, i ^ 1) for i in range(devices)]
+
+    def buffer(count):
+        return (devices, count, HALF, HEAD_DIM)
+
+    (value_send,) = on_chip(
+        functools.partial(values_kernel, places, full), "lay_out_values", [buffer(units)], values
+    )
+    value_here = exchange(value_send)
+    first_send, second_send = on_chip(
+        functools.partial(norm_kernel, places, full, early),
+        "norm",
+        [buffer(2 * early + units), buffer(units - 2 * early)],
+        queries,
+        keys,
+        q_gain.reshape(1, -1),
+        k_gain.reshape(1, -1),
+    )
+    allowed = jnp.arange(key_tiles.shape[-1]) < key_count[:, :, None]
+    masks = jnp.sum(jnp.where(allowed, jnp.left_shift(1, key_tiles), 0), axis=-1)
+    pair, core = my_index // 2, my_index % 2
+    slots = jnp.arange(full + 1)
+    within = jnp.where(slots < full, slots + core * (full + 1), full)
+    masks = masks[pair * (2 * full + 1) + within]
+
+    first_here = exchange(after(first_send, value_here))
+    other_values = lax.ppermute(value_here[:, 2 * full], "seq", swap)
+    second_here = exchange(after(second_send, first_here))
+    other_keys = lax.ppermute(first_here[:, 2 * (early + full)], "seq", swap)
+    (early_out,) = on_chip(
+        functools.partial(early_kernel, early),
+        "attend_early",
+        [buffer(2 * early)],
+        masks,
+        first_here,
+        value_here,
+        smem=1,
+    )
+    early_back = exchange(after(early_out, second_here))
+    shared = pltpu.VMEM((devices, 2, HALF, HEAD_DIM), jnp.bfloat16)
+    (late_out,) = on_chip(
+        functools.partial(late_kernel, early, full),
+        "attend_late",
+        [buffer(units - 2 * early)],
+        masks,
+        second_here,
+        first_here,
+        value_here,
+        other_keys,
+        other_values,
+        smem=1,
+        scratch=[shared, shared],
+    )
+    late_back = exchange(after(late_out, early_back))
+    (attended,) = on_chip(
+        functools.partial(collect_kernel, places, early),
+        "collect",
+        [queries.shape],
+        early_back,
+        late_back,
+    )
+    return attended
+
+
+def paired_fits(mesh, key_tiles_shape):
+    devices = mesh.shape["seq"]
+    per_pair, rest = divmod(2 * HEADS, devices)
+    return (
+        devices % 2 == 0
+        and rest == 0
+        and per_pair % 2 == 1
+        and per_pair >= 5
+        and devices % 4 == 0
+        and key_tiles_shape[1] == devices
+        and devices <= 31
+    )
+
+
 def solution(mesh):
     in_specs = (
         P(("groups", "seq"), None),
@@ -128,4 +426,12 @@
         P(),
     )
     out_specs = P(("groups", "seq"), None)
-    return jax.shard_map(local, mesh=mesh, in_specs=in_specs, out_specs=out_specs, check_vma=False)
+
+    def run(*operands):
+        paired = paired_fits(mesh, operands[5].shape)
+        body = local_paired if paired else local_general
+        return jax.shard_map(
+            body, mesh=mesh, in_specs=in_specs, out_specs=out_specs, check_vma=False
+        )(*operands)
+
+    return run

time: 392 us -> 164 us (0.42); the launches traced: 387 us -> 163 us
  local copies, waits for them, and re-layouts: 154 us -> 8.47 us
  waiting for transfers between devices: 118 us -> 30.6 us
  blocking collectives: 0 us -> 76.9 us
  matrix products: 72.1 us -> 0 us
  Pallas kernels: 0 us -> 28.5 us
  other arithmetic: 13 us -> 0.06 us
  starting transfers between devices: 29.3 us -> 18.1 us
    gather x63 -> x1, local copies, waits for them, and re-layouts: 139 us -> 0.56 us  [local_paired(): masks = masks[pair * (2 * full + 1) + within]]
    all_to_all x2 -> x3, waiting for transfers between devices: 118 us -> 29.2 us  [exchange(): lax.all_to_all(blocks, 'seq', split_axis=0, concat_axis=0, tiled=True)]
    all_to_all x0 -> x2, blocking collectives: none -> 76.9 us  [exchange(): lax.all_to_all(blocks, 'seq', split_axis=0, concat_axis=0, tiled=True)]
    sub x12 -> x0, matrix products: 36.1 us -> none  [one_group(): weights = jnp.where(valid, jnp.exp(masked - peak), jnp.float32(0.0))]
    dot_general x12 -> x0, matrix products: 36 us -> none  [one_group(): jnp.einsum('uqk,ukd->uqd', probs, value_flat, preferred_element_type=jnp....]
    pallas_call x0 -> x5, Pallas kernels: none -> 28.5 us  [on_chip(): pl.pallas_call(kernel, name=name, out_shape=outs, in_specs=[in_smem] * sm...]
    all_to_all x2 -> x3, starting transfers between devices: 29.3 us -> 17.4 us  [exchange(): lax.all_to_all(blocks, 'seq', split_axis=0, concat_axis=0, tiled=True)]
    convert_element_type x2 -> x0, other arithmetic: 4.38 us -> none  [normed(): return (values32 * factor * gain).astype(jnp.bfloat16)]
  transfers between devices with their start and end apart: 2 -> 5, of which waited for: 2 -> 4; matrix products, arithmetic and copies ran while one was open for 0% -> 0% of each run, Pallas kernels for 0% -> 15%
where the time goes in v1:
time: 164 us; the launch traced here: 163 us
  blocking collectives  76.9 us (47%)
  waiting for transfers between devices  30.6 us (19%)
  Pallas kernels  28.5 us (17%)
  starting transfers between devices  18.1 us (11%)
  local copies, waits for them, and re-layouts  8.47 us (5%)
    all_to_all x2, blocking collectives, exchange(): lax.all_to_all(blocks, 'seq', split_axis=0, concat_axis=0, tiled=True)  76.9 us
    all_to_all x3, waiting for transfers between devices, exchange(): lax.all_to_all(blocks, 'seq', split_axis=0, concat_axis=0, tiled=True)  29.2 us
    pallas_call x5, Pallas kernels, on_chip(): pl.pallas_call(kernel, name=name, out_shape=outs, in_specs=[in_smem] * sm...  28.5 us
    all_to_all x3, starting transfers between devices, exchange(): lax.all_to_all(blocks, 'seq', split_axis=0, concat_axis=0, tiled=True)  17.4 us
    unnamed x22, local copies, waits for them, and re-layouts  7.8 us
  transfers between devices with their start and end apart: 5, of which 4 were waited for; matrix products, arithmetic and copies ran while one was open for 0% of the time, Pallas kernels for 15%

profile of v1, /device:TPU:0, one launch (start us, length us, event | category | flops | bytes accessed | tf_op | source)
XLA Modules:
  0.0 162.8 jit_solution(14139571293072564371)
XLA Ops:
  0.0 1.3 copy-done.3
  1.3 1.3 lay_out_values.1
  2.6 7.5 %all-to-all-start = ((bf16[16,5,64,128]{3,2,1,0:T(8,128)(2,1)}), bf16[16,5,64,128]{3,2,1,0:T(8,128)(2,1)S(1)}, u32[]{:S(2)}, u32[]{:S(2)}) async-start(bf16[16,5,64,128]{3,2,1,0:T(8,128)(2,1)} %lay_out_values.1), calls=%async_computation | async-start | bytes 2621440 | tf_op jit(solution)/shard_map/all_to_all | solution.py:327
  10.1 0.0 copy-done.7
  10.1 0.0 copy-done.8
  10.1 0.0 copy-start.4
  10.2 1.3 copy-done.4
  11.5 1.3 copy-done.5
  12.8 1.1 norm.1
  13.9 1.3 copy-done.2
  15.2 0.9 copy-done.6
  16.1 21.5 %all-to-all-done.value_ref = bf16[16,5,64,128]{3,2,1,0:T(8,128)(2,1)S(1)} async-done(((bf16[16,5,64,128]{3,2,1,0:T(8,128)(2,1)}), bf16[16,5,64,128]{3,2,1,0:T(8,128)(2,1)S(1)}, u32[]{:S(2)}, u32[]{:S(2)}) %all-to-all-start) | async-done | bytes 1310752 | tf_op jit(solution)/shard_map/all_to_all | solution.py:327
  37.5 50.8 %all_to_all.25.first_ref = bf16[16,7,64,128]{3,2,1,0:T(8,128)(2,1)S(1)} all-to-all(bf16[16,7,64,128]{3,2,1,0:T(8,128)(2,1)} %copy-done.2), channel_id=1, replica_groups=mesh['groups'=2,'seq'=16] {'seq'}, dimensions={0} | all-to-all | bytes 3670016 | tf_op jit(solution)/shard_map/all_to_all | solution.py:327
  88.3 4.4 %all-to-all-start.2 = ((bf16[16,3,64,128]{3,2,1,0:T(8,128)(2,1)}), bf16[16,3,64,128]{3,2,1,0:T(8,128)(2,1)}, u32[]{:S(2)}, u32[]{:S(2)}) async-start(bf16[16,3,64,128]{3,2,1,0:T(8,128)(2,1)} %copy-done.6), calls=%async_computation.2 | async-start | bytes 1572864 | tf_op jit(solution)/shard_map/all_to_all | solution.py:327
  92.8 0.0 copy-done.9
  92.8 0.0 copy-done.10
  92.8 0.1 copy.14
  92.9 0.6 gather_fusion
  93.5 9.4 %attend_early.1 = bf16[16,2,64,128]{3,2,1,0:T(8,128)(2,1)S(1)} custom-call(s32[3,16]{1,0:T(4,128)S(1)} %gather_fusion, bf16[16,7,64,128]{3,2,1,0:T(8,128)(2,1)S(1)} %all_to_all.25.first_ref, bf16[16,5,64,128]{3,2,1,0:T(8,128)(2,1)S(1)} %all-to-all-done.value_ref), custom_call_target="tpu_custom_call" | custom-call | tf_op jit(solution)/shard_map/attend_early/pallas_call | solution.py:315
  102.9 0.8 copy-done.1
  103.7 7.7 %all-to-all-done.2.second_ref = bf16[16,3,64,128]{3,2,1,0:T(8,128)(2,1)} async-done(((bf16[16,3,64,128]{3,2,1,0:T(8,128)(2,1)}), bf16[16,3,64,128]{3,2,1,0:T(8,128)(2,1)}, u32[]{:S(2)}, u32[]{:S(2)}) %all-to-all-start.2) | async-done | bytes 786464 | tf_op jit(solution)/shard_map/all_to_all | solution.py:327
  111.5 5.5 %all-to-all-start.3 = ((bf16[16,2,64,128]{3,2,1,0:T(8,128)(2,1)}), bf16[16,2,64,128]{3,2,1,0:T(8,128)(2,1)}, u32[]{:S(2)}, u32[]{:S(2)}) async-start(bf16[16,2,64,128]{3,2,1,0:T(8,128)(2,1)} %copy-done.1), calls=%async_computation.3 | async-start | bytes 1048576 | tf_op jit(solution)/shard_map/all_to_all | solution.py:327
  117.0 0.4 collective-permute-start.1
  117.4 0.2 collective-permute-start
  117.6 0.9 collective-permute-done.1.other_value_ref
  118.6 0.4 collective-permute-done.other_key_ref
  119.0 14.3 %attend_late.1 = bf16[16,3,64,128]{3,2,1,0:T(8,128)(2,1)S(1)} custom-call(s32[3,16]{1,0:T(4,128)S(1)} %gather_fusion, bf16[16,3,64,128]{3,2,1,0:T(8,128)(2,1)} %all-to-all-done.2.second_ref, bf16[16,7,64,128]{3,2,1,0:T(8,128)(2,1)S(1)} %all_to_all.25.first_ref, bf16[16,5,64,128]{3,2,1,0:T(8,128)(2,1)S(1)} %all-to-all-done.value_ref, ...), custom_call_target="tpu_custom_call" | custom-call | tf_op jit(solution)/shard_map/attend_late/pallas_call | solution.py:315
  133.3 0.0 copy-start
  133.3 0.9 copy-done
  134.2 0.0 all-to-all-done.3.early_ref
  134.2 26.2 %all_to_all.26.late_ref = bf16[16,3,64,128]{3,2,1,0:T(8,128)(2,1)S(1)} all-to-all(bf16[16,3,64,128]{3,2,1,0:T(8,128)(2,1)} %copy-done), channel_id=1, replica_groups=mesh['groups'=2,'seq'=16] {'seq'}, dimensions={0} | all-to-all | bytes 1572864 | tf_op jit(solution)/shard_map/all_to_all | solution.py:327
  160.3 2.4 %collect.1 = bf16[128,5120]{1,0:T(8,128)(2,1)} custom-call(bf16[16,2,64,128]{3,2,1,0:T(8,128)(2,1)} %all-to-all-done.3.early_ref, bf16[16,3,64,128]{3,2,1,0:T(8,128)(2,1)S(1)} %all_to_all.26.late_ref), custom_call_target="tpu_custom_call" | custom-call | tf_op jit(solution)/shard_map/collect/pallas_call | solution.py:315
  (14 shorter events, 0.1 us)
Async XLA Ops:
  0.0 1.3 copy-start.3
  2.6 7.5 %copy-start.7 = (f32[5120]{0:T(1024)S(1)}, f32[5120]{0:T(1024)}, u32[]{:S(2)}) copy-start(f32[5120]{0:T(1024)} %param.10) | copy-start | bytes 61444
  2.6 7.5 %copy-start.8 = (f32[5120]{0:T(1024)S(1)}, f32[5120]{0:T(1024)}, u32[]{:S(2)}) copy-start(f32[5120]{0:T(1024)} %param.11) | copy-start | bytes 61444
  2.6 34.9 %all-to-all-start = ((bf16[16,5,64,128]{3,2,1,0:T(8,128)(2,1)}), bf16[16,5,64,128]{3,2,1,0:T(8,128)(2,1)S(1)}, u32[]{:S(2)}, u32[]{:S(2)}) async-start(bf16[16,5,64,128]{3,2,1,0:T(8,128)(2,1)} %lay_out_values.1), calls=%async_computation | async-start | bytes 2621440 | tf_op jit(solution)/shard_map/all_to_all | solution.py:327
  10.1 1.3 copy-start.4
  11.5 1.3 copy-start.5
  13.9 1.3 copy-start.2
  15.2 0.9 copy-start.6
  88.3 4.4 %copy-start.9 = (s32[40,16,16]{0,2,1:T(8,128)S(1)}, s32[40,16,16]{0,2,1:T(8,128)}, u32[]{:S(2)}) copy-start(s32[40,16,16]{0,2,1:T(8,128)} %param.12) | copy-start | bytes 122884
  88.3 4.5 %copy-start.10 = (s32[40,16]{0,1:T(8,128)S(1)}, s32[40,16]{0,1:T(8,128)}, u32[]{:S(2)}) copy-start(s32[40,16]{0,1:T(8,128)} %param.13) | copy-start | bytes 7684
  88.3 23.1 %all-to-all-start.2 = ((bf16[16,3,64,128]{3,2,1,0:T(8,128)(2,1)}), bf16[16,3,64,128]{3,2,1,0:T(8,128)(2,1)}, u32[]{:S(2)}, u32[]{:S(2)}) async-start(bf16[16,3,64,128]{3,2,1,0:T(8,128)(2,1)} %copy-done.6), calls=%async_computation.2 | async-start | bytes 1572864 | tf_op jit(solution)/shard_map/all_to_all | solution.py:327
  102.9 0.8 copy-start.1
  111.5 22.7 %all-to-all-start.3 = ((bf16[16,2,64,128]{3,2,1,0:T(8,128)(2,1)}), bf16[16,2,64,128]{3,2,1,0:T(8,128)(2,1)}, u32[]{:S(2)}, u32[]{:S(2)}) async-start(bf16[16,2,64,128]{3,2,1,0:T(8,128)(2,1)} %copy-done.1), calls=%async_computation.3 | async-start | bytes 1048576 | tf_op jit(solution)/shard_map/all_to_all | solution.py:327
  117.0 1.6 collective-permute-start.1
  117.4 1.6 collective-permute-start
  133.3 0.9 copy-start

commit v2 on v0

--- a/solution.py
+++ b/solution.py
@@ -1,8 +1,11 @@
+import functools
 import math
 
 import jax
 import jax.numpy as jnp
 from jax import lax
+from jax.experimental import pallas as pl
+from jax.experimental.pallas import tpu as pltpu
 from jax.sharding import PartitionSpec as P
 
 HEADS = 40
@@ -61,7 +64,7 @@
     return result.reshape(-1, result.shape[2], result.shape[3])
 
 
-def local(queries, keys, values, q_gain, k_gain, key_tiles, key_count):
+def local_general(queries, keys, values, q_gain, k_gain, key_tiles, key_count):
     devices = lax.axis_size("seq")
     my_index = lax.axis_index("seq")
     q_normed = normed(queries, q_gain)
@@ -117,6 +120,332 @@
     return pieces.transpose(1, 0, 2).reshape(TILE, HEADS * HEAD_DIM)
 
 
+HALF = TILE // 2
+VMEM_BYTES = 48 * 1024 * 1024
+
+
+def pair_layout(devices):
+    per_pair = 2 * HEADS // devices
+    full = per_pair // 2
+    places = []
+    for head in range(HEADS):
+        pair, within = divmod(head, per_pair)
+        if within < full:
+            places.append([(2 * pair, within)])
+        elif within >= per_pair - full:
+            places.append([(2 * pair + 1, within - (per_pair - full))])
+        else:
+            places.append([(2 * pair, full), (2 * pair + 1, full)])
+    return places, full
+
+
+def slot_rows(slots, full, pieces):
+    rows, at = {}, 0
+    for slot in slots:
+        rows[slot] = at
+        at += pieces * (HALF if slot == full else TILE)
+    return rows, at
+
+
+def head_columns(head):
+    return slice(head * HEAD_DIM, (head + 1) * HEAD_DIM)
+
+
+def prepare_kernel(
+    places,
+    full,
+    slots,
+    queries_ref,
+    keys_ref,
+    values_ref,
+    q_gain_ref,
+    k_gain_ref,
+    out_ref,
+    query_rows,
+    key_rows,
+    staged,
+    in_sems,
+    value_sems,
+    out_sems,
+):
+    base, _ = slot_rows(slots, full, 3)
+    halves = [slice(0, HALF), slice(HALF, TILE)]
+    loads = {}
+    for i, (source, rows) in enumerate([(keys_ref, key_rows), (queries_ref, query_rows)]):
+        for half in range(2):
+            loads[i, half] = pltpu.make_async_copy(
+                source.at[halves[half]], rows.at[halves[half]], in_sems.at[2 * i + half]
+            )
+            loads[i, half].start()
+    copies = []
+    for head in range(HEADS):
+        for which, (device, slot) in enumerate(places[head]):
+            if slot not in base:
+                continue
+            if slot == full:
+                source = values_ref.at[halves[which], head_columns(head)]
+                target = out_ref.at[device, pl.ds(base[slot] + 2 * HALF, HALF)]
+            else:
+                source = values_ref.at[:, head_columns(head)]
+                target = out_ref.at[device, pl.ds(base[slot] + 2 * TILE, TILE)]
+            copies.append(pltpu.make_async_copy(source, target, value_sems.at[len(copies)]))
+            copies[-1].start()
+    sent = 0
+    for i, (rows, gain_ref, piece) in enumerate(
+        [(key_rows, k_gain_ref, 1), (query_rows, q_gain_ref, 0)]
+    ):
+        for half in range(2):
+            loads[i, half].wait()
+            squares = jnp.zeros((HALF, HEAD_DIM), jnp.float32)
+            for head in range(HEADS):
+                block = rows[halves[half], head_columns(head)].astype(jnp.float32)
+                squares = squares + block * block
+            mean = jnp.sum(squares, axis=-1, keepdims=True) / (HEADS * HEAD_DIM)
+            factor = lax.rsqrt(mean + 1e-06)
+            for head in range(HEADS):
+                for which, (device, slot) in enumerate(places[head]):
+                    if slot not in base or (slot == full and which != half):
+                        continue
+                    block = rows[halves[half], head_columns(head)].astype(jnp.float32)
+                    gain = gain_ref[head_columns(head)][None, :]
+                    done = (block * factor * gain).astype(jnp.bfloat16)
+                    if slot == full:
+                        first = base[slot] + piece * HALF
+                    else:
+                        first = base[slot] + piece * TILE + half * HALF
+                    staged[device, first : first + HALF] = done
+            for slot in slots:
+                if slot == full and half == 0:
+                    continue
+                if slot == full:
+                    here = pl.ds(base[slot] + piece * HALF, HALF)
+                else:
+                    here = pl.ds(base[slot] + piece * TILE + half * HALF, HALF)
+                copies.append(
+                    pltpu.make_async_copy(
+                        staged.at[:, here], out_ref.at[:, here], out_sems.at[sent]
+                    )
+                )
+                copies[-1].start()
+                sent += 1
+    for copy in copies:
+        copy.wait()
+
+
+def prepare(places, full, slots, devices, queries, keys, values, q_gain, k_gain):
+    rows = slot_rows(slots, full, 3)[1]
+    value_copies = sum(slot in slots for holders in places for _, slot in holders)
+    out_copies = sum(2 if slot == full else 4 for slot in slots)
+    anywhere = pl.BlockSpec(memory_space=pl.ANY)
+    in_vmem = pl.BlockSpec(memory_space=pltpu.VMEM)
+    return pl.pallas_call(
+        functools.partial(prepare_kernel, places, full, slots),
+        name="prepare",
+        out_shape=jax.ShapeDtypeStruct((devices, rows, HEAD_DIM), jnp.bfloat16),
+        in_specs=[anywhere] * 3 + [in_vmem] * 2,
+        out_specs=anywhere,
+        scratch_shapes=[
+            pltpu.VMEM(queries.shape, jnp.bfloat16),
+            pltpu.VMEM(keys.shape, jnp.bfloat16),
+            pltpu.VMEM((devices, rows, HEAD_DIM), jnp.bfloat16),
+            pltpu.SemaphoreType.DMA((4,)),
+            pltpu.SemaphoreType.DMA((value_copies,)),
+            pltpu.SemaphoreType.DMA((out_copies,)),
+        ],
+        compiler_params=pltpu.CompilerParams(vmem_limit_bytes=VMEM_BYTES),
+    )(queries, keys, values, q_gain, k_gain)
+
+
+def attend_rows(queries, keys, values, masks):
+    rows = queries[0].shape[0]
+    tiles = keys.shape[0] // TILE
+    stacked = jnp.concatenate(queries, axis=0)
+    scores = lax.dot_general(
+        stacked, keys, (((1,), (1,)), ((), ())), preferred_element_type=jnp.float32
+    )
+    scale = jnp.float32(math.log2(math.e) / math.sqrt(HEAD_DIM))
+    probs, totals = [], []
+    for i, mask in enumerate(masks):
+        parts = []
+        for tile in range(tiles):
+            offset = jnp.where((mask >> tile) & 1 == 1, jnp.float32(0.0), jnp.float32(-1e30))
+            part = scores[i * rows : (i + 1) * rows, tile * TILE : (tile + 1) * TILE]
+            parts.append(part + offset)
+        peak = jnp.max(functools.reduce(jnp.maximum, parts), axis=-1, keepdims=True)
+        weights = [jnp.exp2((part - peak) * scale) for part in parts]
+        totals.append(jnp.sum(functools.reduce(jnp.add, weights), axis=-1, keepdims=True))
+        probs.append(jnp.concatenate([w.astype(jnp.bfloat16) for w in weights], axis=1))
+    mixed = jnp.dot(jnp.concatenate(probs, axis=0), values, preferred_element_type=jnp.float32)
+    return [
+        (mixed[i * rows : (i + 1) * rows] / totals[i]).astype(jnp.bfloat16)
+        for i in range(len(masks))
+    ]
+
+
+def attend_head(mask_ref, slot, here_ref, first, keys_at, values_at, out_ref, out_first, rows):
+    tiles = here_ref.shape[0]
+    together = 2 * TILE // rows
+
+    def step(index, carry):
+        at = index * together
+        out = attend_rows(
+            [here_ref[at + i, first : first + rows] for i in range(together)],
+            keys_at(),
+            values_at(),
+            [mask_ref[slot, at + i] for i in range(together)],
+        )
+        for i in range(together):
+            out_ref[at + i, out_first : out_first + rows] = out[i]
+        return carry
+
+    lax.fori_loop(0, tiles // together, step, 0)
+
+
+def attend_kernel(full, slots, mask_ref, here_ref, *refs):
+    base, _ = slot_rows(slots, full, 3)
+    out_base, _ = slot_rows(slots, full, 1)
+    if full in slots:
+        other_ref, out_ref, shared_keys, shared_values = refs
+    else:
+        (out_ref,) = refs
+    for slot in slots:
+        first = base[slot]
+        if slot == full:
+            shared_keys[:, :HALF] = here_ref[:, first + HALF : first + 2 * HALF]
+            shared_keys[:, HALF:] = other_ref[:, :HALF]
+            shared_values[:, :HALF] = here_ref[:, first + 2 * HALF : first + 3 * HALF]
+            shared_values[:, HALF:] = other_ref[:, HALF:]
+            attend_head(
+                mask_ref,
+                slot,
+                here_ref,
+                first,
+                lambda: shared_keys[...].reshape(-1, HEAD_DIM),
+                lambda: shared_values[...].reshape(-1, HEAD_DIM),
+                out_ref,
+                out_base[slot],
+                HALF,
+            )
+        else:
+            keys, values = (slice(first + i * TILE, first + (i + 1) * TILE) for i in (1, 2))
+            attend_head(
+                mask_ref,
+                slot,
+                here_ref,
+                first,
+                lambda keys=keys: here_ref[:, keys].reshape(-1, HEAD_DIM),
+                lambda values=values: here_ref[:, values].reshape(-1, HEAD_DIM),
+                out_ref,
+                out_base[slot],
+                TILE,
+            )
+
+
+def attend_slots(full, slots, masks, here, *other):
+    in_vmem = pl.BlockSpec(memory_space=pltpu.VMEM)
+    in_smem = pl.BlockSpec(memory_space=pltpu.SMEM)
+    devices = here.shape[0]
+    rows = slot_rows(slots, full, 1)[1]
+    shared = pltpu.VMEM((devices, TILE, HEAD_DIM), jnp.bfloat16)
+    return pl.pallas_call(
+        functools.partial(attend_kernel, full, slots),
+        name="attend",
+        out_shape=jax.ShapeDtypeStruct((devices, rows, HEAD_DIM), jnp.bfloat16),
+        in_specs=[in_smem] + [in_vmem] * (1 + len(other)),
+        out_specs=in_vmem,
+        scratch_shapes=[shared, shared] if other else [],
+        compiler_params=pltpu.CompilerParams(vmem_limit_bytes=VMEM_BYTES),
+    )(masks, here, *other)
+
+
+def collect_kernel(places, full, slots, here_ref, *refs):
+    out_ref, sems = refs[-2:]
+    base, _ = slot_rows(slots, full, 1)
+    copies = []
+    for head in range(HEADS):
+        for which, (device, slot) in enumerate(places[head]):
+            if slot not in base:
+                continue
+            rows = pl.ds(which * HALF, HALF) if slot == full else pl.ds(0, TILE)
+            copies.append(
+                pltpu.make_async_copy(
+                    here_ref.at[device, pl.ds(base[slot], HALF if slot == full else TILE)],
+                    out_ref.at[rows, head_columns(head)],
+                    sems.at[len(copies)],
+                )
+            )
+            copies[-1].start()
+    for copy in copies:
+        copy.wait()
+
+
+def collect(places, full, slots, shape, here, *so_far):
+    anywhere = pl.BlockSpec(memory_space=pl.ANY)
+    count = sum(slot in slots for holders in places for _, slot in holders)
+    return pl.pallas_call(
+        functools.partial(collect_kernel, places, full, slots),
+        name="collect",
+        out_shape=jax.ShapeDtypeStruct(shape, jnp.bfloat16),
+        in_specs=[anywhere] * (1 + len(so_far)),
+        out_specs=anywhere,
+        scratch_shapes=[pltpu.SemaphoreType.DMA((count,))],
+        input_output_aliases={1: 0} if so_far else {},
+        compiler_params=pltpu.CompilerParams(vmem_limit_bytes=VMEM_BYTES),
+    )(here, *so_far)
+
+
+def exchange(blocks):
+    return lax.all_to_all(blocks, "seq", split_axis=0, concat_axis=0, tiled=True)
+
+
+def after(value, *others):
+    return lax.optimization_barrier((value, *others))[0]
+
+
+def local_paired(queries, keys, values, q_gain, k_gain, key_tiles, key_count):
+    devices = lax.axis_size("seq")
+    my_index = lax.axis_index("seq")
+    places, full = pair_layout(devices)
+    late = tuple(range(full - full // 2, full))
+    early = tuple(range(full - full // 2)) + (full,)
+    swap = [(i, i ^ 1) for i in range(devices)]
+
+    operands = (queries, keys, values, q_gain, k_gain)
+    early_here = exchange(prepare(places, full, early, devices, *operands))
+    late_send = prepare(places, full, late, devices, *operands)
+
+    allowed = jnp.arange(key_tiles.shape[-1]) < key_count[:, :, None]
+    masks = jnp.sum(jnp.where(allowed, jnp.left_shift(1, key_tiles), 0), axis=-1)
+    pair, core = my_index // 2, my_index % 2
+    slots = jnp.arange(full + 1)
+    within = jnp.where(slots < full, slots + core * (full + 1), full)
+    masks = masks[pair * (2 * full + 1) + within]
+
+    late_here = exchange(after(late_send, early_here))
+    shared_first = slot_rows(early, full, 3)[0][full]
+    own = early_here[:, shared_first + HALF : shared_first + 3 * HALF]
+    other = lax.ppermute(own, "seq", swap)
+    early_out = attend_slots(full, early, masks, early_here, other)
+    early_back = exchange(after(early_out, late_here))
+    late_out = attend_slots(full, late, masks, late_here)
+    late_back = exchange(after(late_out, early_back))
+    so_far = collect(places, full, early, queries.shape, early_back)
+    return collect(places, full, late, queries.shape, late_back, so_far)
+
+
+def paired_fits(mesh, key_tiles_shape):
+    devices = mesh.shape["seq"]
+    per_pair, rest = divmod(2 * HEADS, devices)
+    return (
+        rest == 0
+        and per_pair % 2 == 1
+        and per_pair >= 5
+        and devices % 4 == 0
+        and key_tiles_shape[1] == devices
+        and devices <= 31
+    )
+
+
 def solution(mesh):
     in_specs = (
         P(("groups", "seq"), None),
@@ -128,4 +457,12 @@
         P(),
     )
     out_specs = P(("groups", "seq"), None)
-    return jax.shard_map(local, mesh=mesh, in_specs=in_specs, out_specs=out_specs, check_vma=False)
+
+    def run(*operands):
+        paired = paired_fits(mesh, operands[5].shape)
+        body = local_paired if paired else local_general
+        return jax.shard_map(
+            body, mesh=mesh, in_specs=in_specs, out_specs=out_specs, check_vma=False
+        )(*operands)
+
+    return run

time: 392 us -> 155 us (0.40); the launches traced: 387 us -> 155 us
  local copies, waits for them, and re-layouts: 154 us -> 11.2 us
  matrix products: 72.1 us -> 0 us
  waiting for transfers between devices: 118 us -> 75.2 us
  Pallas kernels: 0 us -> 33.3 us
  other arithmetic: 13 us -> 0.06 us
  starting transfers between devices: 29.3 us -> 34.7 us
    gather x63 -> x1, local copies, waits for them, and re-layouts: 139 us -> 0.56 us  [local_paired(): masks = masks[pair * (2 * full + 1) + within]]
    all_to_all x2 -> x4, waiting for transfers between devices: 118 us -> 74.4 us  [exchange(): lax.all_to_all(blocks, 'seq', split_axis=0, concat_axis=0, tiled=True)]
    sub x12 -> x0, matrix products: 36.1 us -> none  [one_group(): weights = jnp.where(valid, jnp.exp(masked - peak), jnp.float32(0.0))]
    dot_general x12 -> x0, matrix products: 36 us -> none  [one_group(): jnp.einsum('uqk,ukd->uqd', probs, value_flat, preferred_element_type=jnp....]
    pallas_call x0 -> x6, Pallas kernels: none -> 33.3 us  [the longest x2 26 us: attend_slots(): pl.pallas_call(functools.partial(attend_kernel, full, slots), name='atten...]
    unnamed x13 -> x26, local copies, waits for them, and re-layouts: 5.42 us -> 10.5 us
    all_to_all x2 -> x4, starting transfers between devices: 29.3 us -> 34.3 us  [exchange(): lax.all_to_all(blocks, 'seq', split_axis=0, concat_axis=0, tiled=True)]
    convert_element_type x2 -> x0, other arithmetic: 4.38 us -> none  [normed(): return (values32 * factor * gain).astype(jnp.bfloat16)]
  transfers between devices with their start and end apart: 2 -> 5, of which waited for: 2 -> 5; matrix products, arithmetic and copies ran while one was open for 0% -> 0% of each run, Pallas kernels for 0% -> 19%
where the time goes in v2:
time: 155 us
  waiting for transfers between devices  75.2 us (49%)
  starting transfers between devices  34.7 us (22%)
  Pallas kernels  33.3 us (21%)
  local copies, waits for them, and re-layouts  11.2 us (7%)
    all_to_all x4, waiting for transfers between devices, exchange(): lax.all_to_all(blocks, 'seq', split_axis=0, concat_axis=0, tiled=True)  74.4 us
    all_to_all x4, starting transfers between devices, exchange(): lax.all_to_all(blocks, 'seq', split_axis=0, concat_axis=0, tiled=True)  34.3 us
    pallas_call x2, Pallas kernels, attend_slots(): pl.pallas_call(functools.partial(attend_kernel, full, slots), name='atten...  26 us
    unnamed x26, local copies, waits for them, and re-layouts  10.5 us
    pallas_call x2, Pallas kernels, prepare(): pl.pallas_call(functools.partial(prepare_kernel, places, full, slots), na...  5.29 us
  transfers between devices with their start and end apart: 5, of which 5 were waited for; matrix products, arithmetic and copies ran while one was open for 0% of the time, Pallas kernels for 19%

profile of v2, /device:TPU:0, one launch (start us, length us, event | category | flops | bytes accessed | tf_op | source)
XLA Modules:
  0.0 154.6 jit_solution(13161452849447487402)
XLA Ops:
  0.0 1.3 copy-done.1
  1.3 1.3 copy-done.3
  2.6 1.3 copy-done.5
  4.0 0.7 copy-done.7
  4.7 0.7 copy-done.9
  5.4 3.1 %prepare.3 = bf16[16,576,128]{2,1,0:T(8,128)(2,1)} custom-call(bf16[128,5120]{1,0:T(8,128)(2,1)S(1)} %copy-done.1, bf16[128,5120]{1,0:T(8,128)(2,1)S(1)} %copy-done.3, bf16[128,5120]{1,0:T(8,128)(2,1)S(1)} %copy-done.5, f32[5120]{0:T(1024)S(1)} %copy-done.7, f32[5120]{0:T(1024)S(1)} %copy-done.9), custom_call_target="tpu_custom_call" | custom-call | tf_op jit(solution)/shard_map/prepare/pallas_call | solution.py:241
  8.5 0.0 copy-start.8
  8.5 0.0 copy-start.10
  8.5 7.4 %all-to-all-start = ((bf16[16,576,128]{2,1,0:T(8,128)(2,1)}), bf16[16,576,128]{2,1,0:T(8,128)(2,1)S(1)}, u32[]{:S(2)}, u32[]{:S(2)}) async-start(bf16[16,576,128]{2,1,0:T(8,128)(2,1)} %prepare.3), calls=%async_computation | async-start | bytes 4718592 | tf_op jit(solution)/shard_map/all_to_all | solution.py:398
  15.9 0.0 copy-done.8
  15.9 0.0 copy-done.10
  15.9 0.0 copy-start.2
  15.9 1.3 copy-done.2
  17.3 1.3 copy-done.4
  18.6 1.3 copy-done.6
  19.9 2.2 %prepare.2 = bf16[16,384,128]{2,1,0:T(8,128)(2,1)S(1)} custom-call(bf16[128,5120]{1,0:T(8,128)(2,1)S(1)} %copy-done.2, bf16[128,5120]{1,0:T(8,128)(2,1)S(1)} %copy-done.4, bf16[128,5120]{1,0:T(8,128)(2,1)S(1)} %copy-done.6, f32[5120]{0:T(1024)S(1)} %copy-done.8, f32[5120]{0:T(1024)S(1)} %copy-done.10), custom_call_target="tpu_custom_call" | custom-call | tf_op jit(solution)/shard_map/prepare/pallas_call | solution.py:241
  22.1 1.1 copy-done
  23.3 38.3 %all-to-all-done.here_ref = bf16[16,576,128]{2,1,0:T(8,128)(2,1)S(1)} async-done(((bf16[16,576,128]{2,1,0:T(8,128)(2,1)}), bf16[16,576,128]{2,1,0:T(8,128)(2,1)S(1)}, u32[]{:S(2)}, u32[]{:S(2)}) %all-to-all-start) | async-done | bytes 2359328 | tf_op jit(solution)/shard_map/all_to_all | solution.py:398
  61.6 12.3 %all-to-all-start.1 = ((bf16[16,384,128]{2,1,0:T(8,128)(2,1)}), bf16[16,384,128]{2,1,0:T(8,128)(2,1)}, u32[]{:S(2)}, u32[]{:S(2)}) async-start(bf16[16,384,128]{2,1,0:T(8,128)(2,1)} %copy-done), calls=%async_computation.1 | async-start | bytes 3145728 | tf_op jit(solution)/shard_map/all_to_all | solution.py:398
  73.9 0.4 collective-permute-start
  74.4 0.1 copy.9
  74.5 0.6 gather_fusion
  75.1 0.8 collective-permute-done.refs_0_
  75.9 14.8 %attend.3 = bf16[16,192,128]{2,1,0:T(8,128)(2,1)} custom-call(s32[3,16]{1,0:T(4,128)S(1)} %gather_fusion, bf16[16,576,128]{2,1,0:T(8,128)(2,1)S(1)} %all-to-all-done.here_ref, bf16[16,128,128]{2,1,0:T(8,128)(2,1)S(1)} %collective-permute-done.refs_0_), custom_call_target="tpu_custom_call" | custom-call | tf_op jit(solution)/shard_map/attend/pallas_call | solution.py:350
  90.8 15.2 %all-to-all-done.1.here_ref = bf16[16,384,128]{2,1,0:T(8,128)(2,1)} async-done(((bf16[16,384,128]{2,1,0:T(8,128)(2,1)}), bf16[16,384,128]{2,1,0:T(8,128)(2,1)}, u32[]{:S(2)}, u32[]{:S(2)}) %all-to-all-start.1) | async-done | bytes 1572896 | tf_op jit(solution)/shard_map/all_to_all | solution.py:398
  105.9 9.1 %all-to-all-start.2 = ((bf16[16,192,128]{2,1,0:T(8,128)(2,1)}), bf16[16,192,128]{2,1,0:T(8,128)(2,1)S(1)}, u32[]{:S(2)}, u32[]{:S(2)}) async-start(bf16[16,192,128]{2,1,0:T(8,128)(2,1)} %attend.3), calls=%async_computation.2 | async-start | bytes 1572864 | tf_op jit(solution)/shard_map/all_to_all | solution.py:398
  115.1 11.1 %attend.2 = bf16[16,128,128]{2,1,0:T(8,128)(2,1)} custom-call(s32[3,16]{1,0:T(4,128)S(1)} %gather_fusion, bf16[16,384,128]{2,1,0:T(8,128)(2,1)} %all-to-all-done.1.here_ref), custom_call_target="tpu_custom_call" | custom-call | tf_op jit(solution)/shard_map/attend/pallas_call | solution.py:350
  126.2 7.6 %all-to-all-done.2.here_ref = bf16[16,192,128]{2,1,0:T(8,128)(2,1)S(1)} async-done(((bf16[16,192,128]{2,1,0:T(8,128)(2,1)}), bf16[16,192,128]{2,1,0:T(8,128)(2,1)S(1)}, u32[]{:S(2)}, u32[]{:S(2)}) %all-to-all-start.2) | async-done | bytes 786464 | tf_op jit(solution)/shard_map/all_to_all | solution.py:398
  133.8 5.5 %all-to-all-start.3 = ((bf16[16,128,128]{2,1,0:T(8,128)(2,1)}), bf16[16,128,128]{2,1,0:T(8,128)(2,1)S(1)}, u32[]{:S(2)}, u32[]{:S(2)}) async-start(bf16[16,128,128]{2,1,0:T(8,128)(2,1)} %attend.2), calls=%async_computation.3 | async-start | bytes 1048576 | tf_op jit(solution)/shard_map/all_to_all | solution.py:398
  139.2 1.1 collect.2.refs_0_
  140.4 13.3 %all-to-all-done.3.here_ref = bf16[16,128,128]{2,1,0:T(8,128)(2,1)S(1)} async-done(((bf16[16,128,128]{2,1,0:T(8,128)(2,1)}), bf16[16,128,128]{2,1,0:T(8,128)(2,1)S(1)}, u32[]{:S(2)}, u32[]{:S(2)}) %all-to-all-start.3) | async-done | bytes 524320 | tf_op jit(solution)/shard_map/all_to_all | solution.py:398
  153.7 0.9 collect.3
  (16 shorter events, 0.1 us)
Async XLA Ops:
  0.0 1.3 copy-start.1
  1.3 1.3 copy-start.3
  2.6 1.3 copy-start.5
  4.0 0.7 copy-start.7
  4.7 0.7 copy-start.9
  8.5 7.4 %copy-start.8 = (f32[5120]{0:T(1024)S(1)}, f32[5120]{0:T(1024)}, u32[]{:S(2)}) copy-start(f32[5120]{0:T(1024)} %q_gain_ref.3) | copy-start | bytes 61444
  8.5 7.4 %copy-start.10 = (f32[5120]{0:T(1024)S(1)}, f32[5120]{0:T(1024)}, u32[]{:S(2)}) copy-start(f32[5120]{0:T(1024)} %k_gain_ref.3) | copy-start | bytes 61444
  8.5 53.1 %all-to-all-start = ((bf16[16,576,128]{2,1,0:T(8,128)(2,1)}), bf16[16,576,128]{2,1,0:T(8,128)(2,1)S(1)}, u32[]{:S(2)}, u32[]{:S(2)}) async-start(bf16[16,576,128]{2,1,0:T(8,128)(2,1)} %prepare.3), calls=%async_computation | async-start | bytes 4718592 | tf_op jit(solution)/shard_map/all_to_all | solution.py:398
  15.9 1.3 copy-start.2
  17.2 1.3 copy-start.4
  18.6 1.3 copy-start.6
  22.1 1.1 copy-start
  23.3 51.1 %copy-start.11 = (s32[40,16,16]{0,2,1:T(8,128)S(1)}, s32[40,16,16]{0,2,1:T(8,128)}, u32[]{:S(2)}) copy-start(s32[40,16,16]{0,2,1:T(8,128)} %param.12) | copy-start | bytes 122884
  23.3 51.1 %copy-start.12 = (s32[40,16]{0,1:T(8,128)S(1)}, s32[40,16]{0,1:T(8,128)}, u32[]{:S(2)}) copy-start(s32[40,16]{0,1:T(8,128)} %param.13) | copy-start | bytes 7684
  61.6 44.4 %all-to-all-start.1 = ((bf16[16,384,128]{2,1,0:T(8,128)(2,1)}), bf16[16,384,128]{2,1,0:T(8,128)(2,1)}, u32[]{:S(2)}, u32[]{:S(2)}) async-start(bf16[16,384,128]{2,1,0:T(8,128)(2,1)} %copy-done), calls=%async_computation.1 | async-start | bytes 3145728 | tf_op jit(solution)/shard_map/all_to_all | solution.py:398
  73.9 2.0 %collective-permute-start = (bf16[16,128,128]{2,1,0:T(8,128)(2,1)S(1)}, bf16[16,128,128]{2,1,0:T(8,128)(2,1)S(1)}, u32[]{:S(2)}, u32[]{:S(2)}) collective-permute-start(bf16[16,128,128]{2,1,0:T(8,128)(2,1)S(1)} %slice.6), channel_id=1, source_target_pairs={{0,1},{1,0},{2,3},{3,2},{4,5},{5,4},{6,7},{7,6},{8,9},{9,8},{10,11... | collective-permute-start | bytes 1572872 | tf_op jit(solution)/shard_map/ppermute | solution.py:427
  105.9 27.8 %all-to-all-start.2 = ((bf16[16,192,128]{2,1,0:T(8,128)(2,1)}), bf16[16,192,128]{2,1,0:T(8,128)(2,1)S(1)}, u32[]{:S(2)}, u32[]{:S(2)}) async-start(bf16[16,192,128]{2,1,0:T(8,128)(2,1)} %attend.3), calls=%async_computation.2 | async-start | bytes 1572864 | tf_op jit(solution)/shard_map/all_to_all | solution.py:398
  133.8 20.0 %all-to-all-start.3 = ((bf16[16,128,128]{2,1,0:T(8,128)(2,1)}), bf16[16,128,128]{2,1,0:T(8,128)(2,1)S(1)}, u32[]{:S(2)}, u32[]{:S(2)}) async-start(bf16[16,128,128]{2,1,0:T(8,128)(2,1)} %attend.2), calls=%async_computation.3 | async-start | bytes 1048576 | tf_op jit(solution)/shard_map/all_to_all | solution.py:398

commit v3 on v0

--- a/solution.py
+++ b/solution.py
@@ -1,8 +1,11 @@
+import functools
 import math
 
 import jax
 import jax.numpy as jnp
 from jax import lax
+from jax.experimental import pallas as pl
+from jax.experimental.pallas import tpu as pltpu
 from jax.sharding import PartitionSpec as P
 
 HEADS = 40
@@ -61,7 +64,7 @@
     return result.reshape(-1, result.shape[2], result.shape[3])
 
 
-def local(queries, keys, values, q_gain, k_gain, key_tiles, key_count):
+def local_general(queries, keys, values, q_gain, k_gain, key_tiles, key_count):
     devices = lax.axis_size("seq")
     my_index = lax.axis_index("seq")
     q_normed = normed(queries, q_gain)
@@ -117,6 +120,408 @@
     return pieces.transpose(1, 0, 2).reshape(TILE, HEADS * HEAD_DIM)
 
 
+ALL_VMEM_BYTES = 60 * 1024 * 1024
+IN_HBM = pl.BlockSpec(memory_space=pltpu.HBM)
+ANYWHERE = pl.BlockSpec(memory_space=pl.ANY)
+IN_SMEM = pl.BlockSpec(memory_space=pltpu.SMEM)
+IN_VMEM = pl.BlockSpec(memory_space=pltpu.VMEM)
+PARAMS = pltpu.CompilerParams(vmem_limit_bytes=ALL_VMEM_BYTES)
+LEAVE_ROOM = pltpu.CompilerParams(vmem_limit_bytes=40 * 1024 * 1024)
+LOADS = 2
+
+
+def head_of(pair, core, slot, full):
+    return pair * (2 * full + 1) + (full if slot == full else slot + core * (full + 1))
+
+
+def columns_of(head):
+    return slice(head * HEAD_DIM, (head + 1) * HEAD_DIM)
+
+
+def traced_columns(head):
+    return pl.ds(pl.multiple_of(head * HEAD_DIM, HEAD_DIM), HEAD_DIM)
+
+
+def bf16(*shape):
+    return jax.ShapeDtypeStruct(shape, jnp.bfloat16)
+
+
+def copy_list(sems):
+    return sems, []
+
+
+def start_copy(copies, source, target):
+    sems, started = copies
+    started.append(pltpu.make_async_copy(source, target, sems.at[len(started)]))
+    started[-1].start()
+    return started[-1]
+
+
+def wait_copies(copies):
+    for copy in copies[1]:
+        copy.wait()
+
+
+def norm_in_place(rows, gain, loads, gain_load):
+    count = TILE // len(loads)
+    for part, load in enumerate(loads):
+        here = slice(part * count, (part + 1) * count)
+        load.wait()
+        squares = jnp.zeros((count, HEAD_DIM), jnp.float32)
+        for head in range(HEADS):
+            block = rows[here, columns_of(head)].astype(jnp.float32)
+            squares = squares + block * block
+        mean = jnp.sum(squares, axis=-1, keepdims=True) / (HEADS * HEAD_DIM)
+        factor = lax.rsqrt(mean + 1e-06)
+        if part == 0:
+            gain_load.wait()
+        for head in range(HEADS):
+            block = rows[here, columns_of(head)].astype(jnp.float32)
+            scaled = block * factor * gain[columns_of(head)][None, :]
+            rows[here, columns_of(head)] = scaled.astype(jnp.bfloat16)
+
+
+def prepare_kernel(send, queries, keys, values, q_gain, k_gain, scratch):
+    q_rows, k_rows, v_rows, q_scale, k_scale, in_sems = scratch
+    loading = copy_list(in_sems)
+
+    def load(source, target):
+        parts = [pl.ds(i * TILE // LOADS, TILE // LOADS) for i in range(LOADS)]
+        return [start_copy(loading, source.at[part], target.at[part]) for part in parts]
+
+    k_scale_load = start_copy(loading, k_gain, k_scale)
+    q_scale_load = start_copy(loading, q_gain, q_scale)
+    k_loads, v_loads, q_loads = load(keys, k_rows), load(values, v_rows), load(queries, q_rows)
+    norm_in_place(k_rows, k_scale, k_loads, k_scale_load)
+    send(k_rows, 1)
+    for part in v_loads:
+        part.wait()
+    send(v_rows, 2)
+    norm_in_place(q_rows, q_scale, q_loads, q_scale_load)
+    send(q_rows, 0)
+
+
+def prepare_whole_kernel(full, *refs):
+    operands, out, scratch, out_sems = refs[:5], refs[5], refs[6:-1], refs[-1]
+    copies = copy_list(out_sems)
+
+    def send(rows, tensor):
+        for device in range(out.shape[0]):
+            for slot in range(full):
+                head = head_of(device // 2, device % 2, slot, full)
+                target = out.at[device, pl.ds((3 * slot + tensor) * TILE, TILE)]
+                start_copy(copies, rows.at[:, pl.ds(head * HEAD_DIM, HEAD_DIM)], target)
+
+    prepare_kernel(send, *operands, scratch)
+    wait_copies(copies)
+
+
+def prepare_shared_kernel(full, pairs, me_ref, *refs):
+    operands, outs, scratch, out_sems = refs[:5], refs[5 : 5 + pairs], refs[5 + pairs : -1], refs[-1]
+    copies = copy_list(out_sems)
+
+    def send(rows, tensor):
+        for partner, out in enumerate(outs):
+            head = head_of(jnp.bitwise_xor(me_ref[0] // 2, partner), 0, full, full)
+            target = out.at[pl.ds(tensor * TILE, TILE)]
+            start_copy(copies, rows.at[:, traced_columns(head)], target)
+
+    prepare_kernel(send, *operands, scratch)
+    wait_copies(copies)
+
+
+def prepare_scratch(queries, q_gain, copies):
+    rows = pltpu.VMEM(queries.shape, jnp.bfloat16)
+    scale = pltpu.VMEM(q_gain.shape, jnp.float32)
+    sems = pltpu.SemaphoreType.DMA
+    return [rows, rows, rows, scale, scale, sems((3 * LOADS + 2,)), sems((copies,))]
+
+
+def prepare_whole(full, devices, *operands):
+    return pl.pallas_call(
+        functools.partial(prepare_whole_kernel, full),
+        name="prepare_whole",
+        out_shape=bf16(devices, 3 * full * TILE, HEAD_DIM),
+        in_specs=[IN_HBM] * 5,
+        out_specs=ANYWHERE,
+        scratch_shapes=prepare_scratch(operands[0], operands[3], 3 * full * devices),
+        compiler_params=PARAMS,
+    )(*operands)
+
+
+def prepare_shared(full, pairs, me, *operands):
+    return pl.pallas_call(
+        functools.partial(prepare_shared_kernel, full, pairs),
+        name="prepare_shared",
+        out_shape=[bf16(3 * TILE, HEAD_DIM)] * pairs,
+        in_specs=[IN_SMEM] + [IN_HBM] * 5,
+        out_specs=[ANYWHERE] * pairs,
+        scratch_shapes=prepare_scratch(operands[0], operands[3], 3 * pairs),
+        compiler_params=PARAMS,
+    )(me, *operands)
+
+
+TOGETHER = 2
+UNROLL = 4
+
+
+def key_marks(keys):
+    shape = (keys.shape[0], HEAD_DIM)
+    tile = lax.broadcasted_iota(jnp.int32, shape, 0) // TILE
+    marks = jnp.where(lax.broadcasted_iota(jnp.int32, shape, 1) == tile, 1.0, 0.0)
+    return jnp.concatenate([keys, marks.astype(jnp.bfloat16)], axis=1)
+
+
+def query_masks(queries, mask):
+    bit = jnp.minimum(lax.broadcasted_iota(jnp.int32, queries.shape, 1), 31)
+    offsets = jnp.where((mask >> bit) & 1 == 1, jnp.float32(0.0), jnp.float32(-1e30))
+    return jnp.concatenate([queries, offsets.astype(jnp.bfloat16)], axis=1)
+
+
+def attend_rows(queries, keys, values, masks):
+    tiles = keys.shape[0] // TILE
+    marked = [query_masks(tile, mask) for tile, mask in zip(queries, masks)]
+    scores = lax.dot_general(
+        jnp.concatenate(marked, axis=0),
+        keys,
+        (((1,), (1,)), ((), ())),
+        preferred_element_type=jnp.float32,
+    )
+    scale = jnp.float32(math.log2(math.e) / math.sqrt(HEAD_DIM))
+    probs, totals = [], []
+    for i in range(len(masks)):
+        rows = slice(i * TILE, (i + 1) * TILE)
+        parts = [scores[rows, tile * TILE : (tile + 1) * TILE] for tile in range(tiles)]
+        peak = jnp.max(functools.reduce(jnp.maximum, parts), axis=-1, keepdims=True)
+        weights = [jnp.exp2((part - peak) * scale) for part in parts]
+        totals.append(jnp.sum(functools.reduce(jnp.add, weights), axis=-1, keepdims=True))
+        probs.append(jnp.concatenate([w.astype(jnp.bfloat16) for w in weights], axis=1))
+    mixed = jnp.dot(jnp.concatenate(probs, axis=0), values, preferred_element_type=jnp.float32)
+    return [
+        (mixed[i * TILE : (i + 1) * TILE] / total).astype(jnp.bfloat16)
+        for i, total in enumerate(totals)
+    ]
+
+
+def attend_slot(mask_ref, slot, here, first, out, out_first, stride, marked):
+    def part(tile, tensor):
+        return here[tile, first + tensor * TILE : first + (tensor + 1) * TILE]
+
+    marked[...] = key_marks(part(slice(None), 1).reshape(-1, HEAD_DIM))
+
+    def step(index, carry):
+        for product in range(UNROLL):
+            at = (index * UNROLL + product) * TOGETHER
+            tiles = [(at + i) * stride for i in range(TOGETHER)]
+            values = part(slice(None), 2).reshape(-1, HEAD_DIM)
+            masks = [mask_ref[slot, tile] for tile in tiles]
+            blocks = attend_rows([part(tile, 0) for tile in tiles], marked[...], values, masks)
+            for tile, block in zip(tiles, blocks):
+                out[tile, out_first : out_first + TILE] = block
+        return carry
+
+    lax.fori_loop(0, here.shape[0] // (stride * TOGETHER * UNROLL), step, 0)
+
+
+def marked_keys(devices):
+    return pltpu.VMEM((devices * TILE, 2 * HEAD_DIM), jnp.bfloat16)
+
+
+def attend_whole_kernel(full, mask_ref, here, out, marked):
+    for slot in range(full):
+        attend_slot(mask_ref, slot, here, 3 * slot * TILE, out, slot * TILE, 1, marked)
+
+
+def attend_whole(full, masks, here):
+    return pl.pallas_call(
+        functools.partial(attend_whole_kernel, full),
+        name="attend_whole",
+        out_shape=bf16(here.shape[0], full * TILE, HEAD_DIM),
+        in_specs=[IN_SMEM, IN_VMEM],
+        out_specs=IN_VMEM,
+        scratch_shapes=[marked_keys(here.shape[0])],
+        compiler_params=LEAVE_ROOM,
+    )(masks, here)
+
+
+def attend_shared_kernel(full, pairs, mask_ref, *refs):
+    blocks, other, outs = refs[:pairs], refs[pairs], refs[pairs + 1 : 2 * pairs + 1]
+    here, out, marked, in_sems, out_sems = refs[2 * pairs + 1 :]
+    loads, stores = copy_list(in_sems), copy_list(out_sems)
+    for partner, block in enumerate(blocks):
+        start_copy(loads, block, here.at[2 * partner])
+        start_copy(loads, other.at[partner], here.at[2 * partner + 1, pl.ds(TILE, 2 * TILE)])
+    wait_copies(loads)
+    attend_slot(mask_ref, full, here, 0, out, 0, 2, marked)
+    for partner, target in enumerate(outs):
+        start_copy(stores, out.at[2 * partner], target)
+    wait_copies(stores)
+
+
+def attend_shared(full, masks, blocks, other):
+    pairs = len(blocks)
+    return pl.pallas_call(
+        functools.partial(attend_shared_kernel, full, pairs),
+        name="attend_shared",
+        out_shape=[bf16(TILE, HEAD_DIM)] * pairs,
+        in_specs=[IN_SMEM] + [ANYWHERE] * (pairs + 1),
+        out_specs=[ANYWHERE] * pairs,
+        scratch_shapes=[
+            pltpu.VMEM((2 * pairs, 3 * TILE, HEAD_DIM), jnp.bfloat16),
+            pltpu.VMEM((2 * pairs, TILE, HEAD_DIM), jnp.bfloat16),
+            marked_keys(2 * pairs),
+            pltpu.SemaphoreType.DMA((2 * pairs,)),
+            pltpu.SemaphoreType.DMA((pairs,)),
+        ],
+        compiler_params=PARAMS,
+    )(masks, *blocks, other)
+
+
+def join_kernel(*refs):
+    blocks, (out, rows, in_sems, out_sems) = refs[:-4], refs[-4:]
+    loads, stores = copy_list(in_sems), copy_list(out_sems)
+    for index, block in enumerate(blocks):
+        start_copy(loads, block.at[pl.ds(TILE, 2 * TILE)], rows.at[index])
+    for index, load in enumerate(loads[1]):
+        load.wait()
+        start_copy(stores, rows.at[index], out.at[index])
+    wait_copies(stores)
+
+
+def join_keys_values(blocks):
+    shape = (len(blocks), 2 * TILE, HEAD_DIM)
+    sems = pltpu.SemaphoreType.DMA((len(blocks),))
+    return pl.pallas_call(
+        join_kernel,
+        name="join_keys_values",
+        out_shape=bf16(*shape),
+        in_specs=[ANYWHERE] * len(blocks),
+        out_specs=ANYWHERE,
+        scratch_shapes=[pltpu.VMEM(shape, jnp.bfloat16), sems, sems],
+        compiler_params=PARAMS,
+    )(*blocks)
+
+
+def collect_shared_kernel(full, me_ref, *refs):
+    blocks, (out, rows, in_sems, out_sems) = refs[:-4], refs[-4:]
+    loads, stores = copy_list(in_sems), copy_list(out_sems)
+    for partner, block in enumerate(blocks):
+        start_copy(loads, block, rows.at[partner])
+    for partner, load in enumerate(loads[1]):
+        load.wait()
+        head = head_of(jnp.bitwise_xor(me_ref[0] // 2, partner), 0, full, full)
+        start_copy(stores, rows.at[partner], out.at[:, traced_columns(head)])
+    wait_copies(stores)
+
+
+def collect_shared(full, shape, me, blocks):
+    sems = pltpu.SemaphoreType.DMA((len(blocks),))
+    return pl.pallas_call(
+        functools.partial(collect_shared_kernel, full),
+        name="collect_shared",
+        out_shape=bf16(*shape),
+        in_specs=[IN_SMEM] + [ANYWHERE] * len(blocks),
+        out_specs=IN_HBM,
+        scratch_shapes=[pltpu.VMEM((len(blocks), TILE, HEAD_DIM), jnp.bfloat16), sems, sems],
+        compiler_params=PARAMS,
+    )(me, *blocks)
+
+
+def collect_whole_kernel(full, here, _, out, sems):
+    stores = copy_list(sems)
+    for device in range(here.shape[0]):
+        for slot in range(full):
+            head = head_of(device // 2, device % 2, slot, full)
+            target = out.at[:, pl.ds(head * HEAD_DIM, HEAD_DIM)]
+            start_copy(stores, here.at[device, pl.ds(slot * TILE, TILE)], target)
+    wait_copies(stores)
+
+
+def collect_whole(full, here, so_far):
+    return pl.pallas_call(
+        functools.partial(collect_whole_kernel, full),
+        name="collect_whole",
+        out_shape=bf16(*so_far.shape),
+        in_specs=[IN_VMEM, IN_HBM],
+        out_specs=IN_HBM,
+        scratch_shapes=[pltpu.SemaphoreType.DMA((full * here.shape[0],))],
+        input_output_aliases={1: 0},
+        compiler_params=LEAVE_ROOM,
+    )(here, so_far)
+
+
+def with_all(blocks):
+    return lax.all_to_all(blocks, "seq", split_axis=0, concat_axis=0, tiled=True)
+
+
+def with_partner(block, k):
+    devices = lax.axis_size("seq")
+    return lax.ppermute(block, "seq", [(i, i ^ (2 * k)) for i in range(devices)]) if k else block
+
+
+def with_sibling(block):
+    return lax.ppermute(block, "seq", [(i, i ^ 1) for i in range(lax.axis_size("seq"))])
+
+
+def after(value, *others):
+    return lax.optimization_barrier((value, *others))[0]
+
+
+def all_after(values, *others):
+    return list(lax.optimization_barrier((*values, *others))[: len(values)])
+
+
+def tile_masks(full, my_index, key_tiles, key_count):
+    slots = jnp.arange(full + 1)
+    within = jnp.where(slots < full, slots + my_index % 2 * (full + 1), full)
+    heads = my_index // 2 * (2 * full + 1) + within
+    tiles, counts = key_tiles[heads], key_count[heads]
+    flip = jnp.where(slots < full, 0, my_index)
+    bits = jnp.left_shift(1, jnp.bitwise_xor(tiles, flip[:, None, None]))
+    allowed = jnp.arange(tiles.shape[-1]) < counts[:, :, None]
+    masks = jnp.sum(jnp.where(allowed, bits, 0), axis=-1)
+    order = jnp.bitwise_xor(jnp.arange(tiles.shape[1])[None, :], flip[:, None])
+    return jnp.take_along_axis(masks, order, axis=1)
+
+
+def local_paired(queries, keys, values, q_gain, k_gain, key_tiles, key_count):
+    devices = lax.axis_size("seq")
+    pairs = devices // 2
+    full = HEADS // devices
+    my_index = lax.axis_index("seq")
+    me = my_index.reshape(1)
+    rest = (keys, values, q_gain, k_gain)
+
+    whole = prepare_whole(full, devices, queries, *rest)
+    masks = tile_masks(full, my_index, key_tiles, key_count)
+    shared = prepare_shared(full, pairs, me, after(queries, masks, whole), *rest)
+    whole = with_all(whole)
+    shared = [with_partner(block, k) for k, block in enumerate(shared)]
+    near, far = shared[: pairs // 2], shared[pairs // 2 :]
+    whole_out = attend_whole(full, masks, after(whole, *near))
+    shared = all_after(near + far, whole_out)
+    whole_back = with_all(after(whole_out, *shared))
+    other = with_sibling(join_keys_values(shared))
+    shared_out = attend_shared(full, masks, shared, other)
+    shared_back = [with_partner(block, k) for k, block in enumerate(shared_out)]
+    so_far = collect_shared(full, queries.shape, me, shared_back)
+    return collect_whole(full, whole_back, so_far)
+
+
+def paired_fits(mesh, key_tiles_shape):
+    devices = mesh.shape["seq"]
+    per_pair, rest = divmod(2 * HEADS, devices)
+    return (
+        rest == 0
+        and per_pair % 2 == 1
+        and per_pair >= 3
+        and devices >= 16
+        and devices & (devices - 1) == 0
+        and key_tiles_shape[1] == devices
+        and devices <= 31
+    )
+
+
 def solution(mesh):
     in_specs = (
         P(("groups", "seq"), None),
@@ -128,4 +533,12 @@
         P(),
     )
     out_specs = P(("groups", "seq"), None)
-    return jax.shard_map(local, mesh=mesh, in_specs=in_specs, out_specs=out_specs, check_vma=False)
+
+    def run(*operands):
+        paired = paired_fits(mesh, operands[5].shape)
+        body = local_paired if paired else local_general
+        return jax.shard_map(
+            body, mesh=mesh, in_specs=in_specs, out_specs=out_specs, check_vma=False
+        )(*operands)
+
+    return run

time: 392 us -> 147 us (0.38); the launches traced: 387 us -> 147 us
  local copies, waits for them, and re-layouts: 154 us -> 5.9 us
  matrix products: 72.1 us -> 0 us
  waiting for transfers between devices: 118 us -> 57.8 us
  Pallas kernels: 0 us -> 33.4 us
  starting transfers between devices: 29.3 us -> 48.8 us
  other arithmetic: 13 us -> 0.38 us
    gather x63 -> x5, local copies, waits for them, and re-layouts: 139 us -> 2.34 us  [the longest x3 1.24 us: tile_masks(): return jnp.take_along_axis(masks, order, axis=1)]
    all_to_all x2, waiting for transfers between devices: 118 us -> 0.45 us  [with_all(): lax.all_to_all(blocks, 'seq', split_axis=0, concat_axis=0, tiled=True)]
    ppermute x0 -> x15, waiting for transfers between devices: none -> 57.4 us  [the longest x14 55.6 us: with_partner(): lax.ppermute(block, 'seq', [(i, i ^ 2 * k) for i in range(devices)])]
    sub x12 -> x0, matrix products: 36.1 us -> none  [one_group(): weights = jnp.where(valid, jnp.exp(masked - peak), jnp.float32(0.0))]
    dot_general x12 -> x0, matrix products: 36 us -> none  [one_group(): jnp.einsum('uqk,ukd->uqd', probs, value_flat, preferred_element_type=jnp....]
    pallas_call x0 -> x7, Pallas kernels: none -> 33.4 us  [the longest x1 14.2 us: attend_whole(): pl.pallas_call(functools.partial(attend_whole_kernel, full), name='attend...]
    ppermute x0 -> x15, starting transfers between devices: none -> 28.3 us  [the longest x14 27.8 us: with_partner(): lax.ppermute(block, 'seq', [(i, i ^ 2 * k) for i in range(devices)])]
    all_to_all x2, starting transfers between devices: 29.3 us -> 20.5 us  [with_all(): lax.all_to_all(blocks, 'seq', split_axis=0, concat_axis=0, tiled=True)]
  transfers between devices with their start and end apart: 2 -> 17, of which waited for: 2 -> 8; matrix products, arithmetic and copies ran while one was open for 0% -> 3% of each run, Pallas kernels for 0% -> 19%
where the time goes in v3:
time: 147 us
  waiting for transfers between devices  57.8 us (39%)
  starting transfers between devices  48.8 us (33%)
  Pallas kernels  33.4 us (23%)
  local copies, waits for them, and re-layouts  5.9 us (4%)
    ppermute x14, waiting for transfers between devices, with_partner(): lax.ppermute(block, 'seq', [(i, i ^ 2 * k) for i in range(devices)])  55.6 us
    ppermute x14, starting transfers between devices, with_partner(): lax.ppermute(block, 'seq', [(i, i ^ 2 * k) for i in range(devices)])  27.8 us
    all_to_all x2, starting transfers between devices, with_all(): lax.all_to_all(blocks, 'seq', split_axis=0, concat_axis=0, tiled=True)  20.5 us
    pallas_call x1, Pallas kernels, attend_whole(): pl.pallas_call(functools.partial(attend_whole_kernel, full), name='attend...  14.2 us
    pallas_call x1, Pallas kernels, attend_shared(): pl.pallas_call(functools.partial(attend_shared_kernel, full, pairs), name...  6.31 us
    pallas_call x1, Pallas kernels, prepare_whole(): pl.pallas_call(functools.partial(prepare_whole_kernel, full), name='prepa...  4.59 us
    pallas_call x1, Pallas kernels, prepare_shared(): pl.pallas_call(functools.partial(prepare_shared_kernel, full, pairs), nam...  3.63 us
    unnamed x32, local copies, waits for them, and re-layouts  3.55 us
  transfers between devices with their start and end apart: 17, of which 8 were waited for; matrix products, arithmetic and copies ran while one was open for 3% of the time, Pallas kernels for 19%

profile of v3, /device:TPU:0, one launch (start us, length us, event | category | flops | bytes accessed | tf_op | source)
XLA Modules:
  0.0 146.7 jit_solution(10573133389456607762)
XLA Ops:
  0.0 4.6 %prepare_whole.1 = bf16[16,768,128]{2,1,0:T(8,128)(2,1)} custom-call(bf16[128,5120]{1,0:T(8,128)(2,1)} %refs_0_.2, bf16[128,5120]{1,0:T(8,128)(2,1)} %refs_1_.3, bf16[128,5120]{1,0:T(8,128)(2,1)} %refs_2_.3, f32[5120]{0:T(1024)} %refs_3_.3, f32[5120]{0:T(1024)} %refs_4_.3), custom_call_target="tpu_custom_call" | custom-call | tf_op jit(solution)/shard_map/prepare_whole/pallas_call | solution.py:241
  4.6 7.4 %all-to-all-start = ((bf16[16,768,128]{2,1,0:T(8,128)(2,1)}), bf16[16,768,128]{2,1,0:T(8,128)(2,1)S(1)}, u32[]{:S(2)}, u32[]{:S(2)}) async-start(bf16[16,768,128]{2,1,0:T(8,128)(2,1)} %prepare_whole.1), calls=%async_computation | async-start | bytes 6291456 | tf_op jit(solution)/shard_map/all_to_all | solution.py:454
  12.3 1.1 copy.12
  14.8 1.1 gather_fusion.2
  16.0 3.6 %prepare_shared.1 = (bf16[384,128]{1,0:T(8,128)(2,1)}, bf16[384,128]{1,0:T(8,128)(2,1)}, bf16[384,128]{1,0:T(8,128)(2,1)}, bf16[384,128]{1,0:T(8,128)(2,1)}, bf1...) custom-call(s32[1]{0:T(128)} %bitcast.1.me_ref, ...), custom_call_target="tpu_custom_call" | custom-call | tf_op jit(solution)/shard_map/prepare_shared/pallas_call | solution.py:253
  19.6 2.0 %collective-permute-start = (bf16[384,128]{1,0:T(8,128)(2,1)}, bf16[384,128]{1,0:T(8,128)(2,1)S(1)}, u32[]{:S(2)}, u32[]{:S(2)}) collective-permute-start(bf16[384,128]{1,0:T(8,128)(2,1)} %get-tuple-element.34), channel_id=1, source_target_pairs={{0,2},{1,3},{2,0},{3,1},{4,6},{5,7},{6,4},{7,5},{8,10},{9,11},{10,... | collective-permute-start | bytes 294920 | tf_op jit(solution)/shard_map/ppermute | solution.py:459
  21.6 1.5 collective-permute-start.1
  23.2 2.8 %collective-permute-start.3 = (bf16[384,128]{1,0:T(8,128)(2,1)}, bf16[384,128]{1,0:T(8,128)(2,1)S(1)}, u32[]{:S(2)}, u32[]{:S(2)}) collective-permute-start(bf16[384,128]{1,0:T(8,128)(2,1)} %get-tuple-element.38), channel_id=1, source_target_pairs={{0,8},{1,9},{2,10},{3,11},{4,12},{5,13},{6,14},{7,15},{8,0},{9,1},... | collective-permute-start | bytes 294920 | tf_op jit(solution)/shard_map/ppermute | solution.py:459
  26.0 1.5 collective-permute-start.4
  27.5 7.6 %collective-permute-done.refs_1_ = bf16[384,128]{1,0:T(8,128)(2,1)S(1)} collective-permute-done((bf16[384,128]{1,0:T(8,128)(2,1)}, bf16[384,128]{1,0:T(8,128)(2,1)S(1)}, u32[]{:S(2)}, u32[]{:S(2)}) %collective-permute-start) | collective-permute-done | bytes 98336 | tf_op jit(solution)/shard_map/ppermute | solution.py:459
  35.1 2.7 %collective-permute-start.5 = (bf16[384,128]{1,0:T(8,128)(2,1)}, bf16[384,128]{1,0:T(8,128)(2,1)}, u32[]{:S(2)}, u32[]{:S(2)}) collective-permute-start(bf16[384,128]{1,0:T(8,128)(2,1)} %get-tuple-element.40), channel_id=1, source_target_pairs={{0,12},{1,13},{2,14},{3,15},{4,8},{5,9},{6,10},{7,11},{8,4},{9,5},... | collective-permute-start | bytes 294920 | tf_op jit(solution)/shard_map/ppermute | solution.py:459
  37.9 28.4 %collective-permute-done.1.refs_2_ = bf16[384,128]{1,0:T(8,128)(2,1)S(1)} collective-permute-done((bf16[384,128]{1,0:T(8,128)(2,1)}, bf16[384,128]{1,0:T(8,128)(2,1)S(1)}, u32[]{:S(2)}, u32[]{:S(2)}) %collective-permute-start.1) | collective-permute-done | bytes 98336 | tf_op jit(solution)/shard_map/ppermute | solution.py:459
  66.2 4.8 %collective-permute-start.6 = (bf16[384,128]{1,0:T(8,128)(2,1)}, bf16[384,128]{1,0:T(8,128)(2,1)}, u32[]{:S(2)}, u32[]{:S(2)}) collective-permute-start(bf16[384,128]{1,0:T(8,128)(2,1)} %get-tuple-element.41), channel_id=1, source_target_pairs={{0,14},{1,15},{2,12},{3,13},{4,10},{5,11},{6,8},{7,9},{8,6},{9,7},... | collective-permute-start | bytes 294920 | tf_op jit(solution)/shard_map/ppermute | solution.py:459
  71.4 14.2 %attend_whole.1 = bf16[16,256,128]{2,1,0:T(8,128)(2,1)S(1)} custom-call(s32[3,16]{1,0:T(4,128)S(1)} %fusion.6.mask_ref, bf16[16,768,128]{2,1,0:T(8,128)(2,1)S(1)} %all-to-all-done.here), custom_call_target="tpu_custom_call" | custom-call | tf_op jit(solution)/shard_map/attend_whole/pallas_call | solution.py:336
  85.7 1.0 copy-done
  86.6 8.0 %collective-permute-done.3.refs_4_ = bf16[384,128]{1,0:T(8,128)(2,1)S(1)} collective-permute-done((bf16[384,128]{1,0:T(8,128)(2,1)}, bf16[384,128]{1,0:T(8,128)(2,1)S(1)}, u32[]{:S(2)}, u32[]{:S(2)}) %collective-permute-start.3) | collective-permute-done | bytes 98336 | tf_op jit(solution)/shard_map/ppermute | solution.py:459
  94.6 3.2 %collective-permute-done.4.refs_5_ = bf16[384,128]{1,0:T(8,128)(2,1)} collective-permute-done((bf16[384,128]{1,0:T(8,128)(2,1)}, bf16[384,128]{1,0:T(8,128)(2,1)}, u32[]{:S(2)}, u32[]{:S(2)}) %collective-permute-start.4) | collective-permute-done | bytes 98336 | tf_op jit(solution)/shard_map/ppermute | solution.py:459
  97.8 13.1 %all-to-all-start.1 = ((bf16[16,256,128]{2,1,0:T(8,128)(2,1)}), bf16[16,256,128]{2,1,0:T(8,128)(2,1)S(1)}, u32[]{:S(2)}, u32[]{:S(2)}) async-start(bf16[16,256,128]{2,1,0:T(8,128)(2,1)} %copy-done), calls=%async_computation.1 | async-start | bytes 2097152 | tf_op jit(solution)/shard_map/all_to_all | solution.py:454
  110.9 1.8 %join_keys_values.1 = bf16[8,256,128]{2,1,0:T(8,128)(2,1)} custom-call(bf16[384,128]{1,0:T(8,128)(2,1)} %get-tuple-element.42.refs_0_, bf16[384,128]{1,0:T(8,128)(2,1)} %copy-done.3, bf16[384,128]{1,0:T(8,128)(2,1)} %copy-done.4, bf16[384,128]{1,0:T(8,128)(2,1)} %copy-done.5, bf16[384,128]{1,0:T(8,128)(2,1)} %copy-done.6, ...), custom_call_target="tpu_custom_call" | custom-call | tf_op jit(solution)/shard_map/join_keys_values/pallas_call | solution.py:394
  113.2 1.7 %collective-permute-done.7.refs_8_ = bf16[8,256,128]{2,1,0:T(8,128)(2,1)S(1)} collective-permute-done((bf16[8,256,128]{2,1,0:T(8,128)(2,1)}, bf16[8,256,128]{2,1,0:T(8,128)(2,1)S(1)}, u32[]{:S(2)}, u32[]{:S(2)}) %collective-permute-start.7) | collective-permute-done | bytes 524320 | tf_op jit(solution)/shard_map/ppermute | solution.py:463
  115.0 0.8 copy-done.2
  115.8 6.3 %attend_shared.1 = (bf16[128,128]{1,0:T(8,128)(2,1)}, bf16[128,128]{1,0:T(8,128)(2,1)}, bf16[128,128]{1,0:T(8,128)(2,1)}, bf16[128,128]{1,0:T(8,128)(2,1)}, bf16...) custom-call(s32[3,16]{1,0:T(4,128)} %copy-done.1, ...), custom_call_target="tpu_custom_call" | custom-call | tf_op jit(solution)/shard_map/attend_shared/pallas_call | solution.py:363
  122.1 2.0 %collective-permute-start.8 = (bf16[128,128]{1,0:T(8,128)(2,1)}, bf16[128,128]{1,0:T(8,128)(2,1)S(1)}, u32[]{:S(2)}, u32[]{:S(2)}) collective-permute-start(bf16[128,128]{1,0:T(8,128)(2,1)} %get-tuple-element.52), channel_id=1, source_target_pairs={{0,2},{1,3},{2,0},{3,1},{4,6},{5,7},{6,4},{7,5},{8,10},{9,11},{10,... | collective-permute-start | bytes 98312 | tf_op jit(solution)/shard_map/ppermute | solution.py:459
  124.1 1.5 collective-permute-start.9
  125.7 2.8 %collective-permute-start.11 = (bf16[128,128]{1,0:T(8,128)(2,1)}, bf16[128,128]{1,0:T(8,128)(2,1)S(1)}, u32[]{:S(2)}, u32[]{:S(2)}) collective-permute-start(bf16[128,128]{1,0:T(8,128)(2,1)} %get-tuple-element.55), channel_id=1, source_target_pairs={{0,8},{1,9},{2,10},{3,11},{4,12},{5,13},{6,14},{7,15},{8,0},{9,1},... | collective-permute-start | bytes 98312 | tf_op jit(solution)/shard_map/ppermute | solution.py:459
  128.4 1.5 collective-permute-start.12
  129.9 3.3 %collective-permute-start.13 = (bf16[128,128]{1,0:T(8,128)(2,1)}, bf16[128,128]{1,0:T(8,128)(2,1)S(1)}, u32[]{:S(2)}, u32[]{:S(2)}) collective-permute-start(bf16[128,128]{1,0:T(8,128)(2,1)} %get-tuple-element.57), channel_id=1, source_target_pairs={{0,12},{1,13},{2,14},{3,15},{4,8},{5,9},{6,10},{7,11},{8,4},{9,5},... | collective-permute-start | bytes 98312 | tf_op jit(solution)/shard_map/ppermute | solution.py:459
  133.2 1.4 collective-permute-start.14
  134.6 6.9 %collective-permute-done.11.refs_4_ = bf16[128,128]{1,0:T(8,128)(2,1)S(1)} collective-permute-done((bf16[128,128]{1,0:T(8,128)(2,1)}, bf16[128,128]{1,0:T(8,128)(2,1)S(1)}, u32[]{:S(2)}, u32[]{:S(2)}) %collective-permute-start.11) | collective-permute-done | bytes 32800 | tf_op jit(solution)/shard_map/ppermute | solution.py:459
  141.5 1.6 %collective-permute-done.12.refs_5_ = bf16[128,128]{1,0:T(8,128)(2,1)S(1)} collective-permute-done((bf16[128,128]{1,0:T(8,128)(2,1)}, bf16[128,128]{1,0:T(8,128)(2,1)S(1)}, u32[]{:S(2)}, u32[]{:S(2)}) %collective-permute-start.12) | collective-permute-done | bytes 32800 | tf_op jit(solution)/shard_map/ppermute | solution.py:459
  143.7 1.6 %collect_shared.1._ = bf16[128,5120]{1,0:T(8,128)(2,1)} custom-call(s32[1]{0:T(128)} %bitcast.1.me_ref, bf16[128,128]{1,0:T(8,128)(2,1)} %get-tuple-element.51.refs_0_, bf16[128,128]{1,0:T(8,128)(2,1)} %copy-done.7, bf16[128,128]{1,0:T(8,128)(2,1)} %copy-done.8, bf16[128,128]{1,0:T(8,128)(2,1)} %copy-done.9, bf16[128,128]{1,0:T(8,128)(2,1)} %copy-done.10, ...), custom_call_target="tpu_custom_call" | custom-call | tf_op jit(solution)/shard_map/collect_shared/pallas_call | solution.py:419
  145.3 1.2 collect_whole.1
  (52 shorter events, 3.6 us)
Async XLA Ops:
  4.6 7.6 %copy-start.14 = (s32[40,16]{0,1:T(8,128)S(1)}, s32[40,16]{0,1:T(8,128)}, u32[]{:S(2)}) copy-start(s32[40,16]{0,1:T(8,128)} %param.13) | copy-start | bytes 7684
  4.6 66.8 %all-to-all-start = ((bf16[16,768,128]{2,1,0:T(8,128)(2,1)}), bf16[16,768,128]{2,1,0:T(8,128)(2,1)S(1)}, u32[]{:S(2)}, u32[]{:S(2)}) async-start(bf16[16,768,128]{2,1,0:T(8,128)(2,1)} %prepare_whole.1), calls=%async_computation | async-start | bytes 6291456 | tf_op jit(solution)/shard_map/all_to_all | solution.py:454
  16.0 55.4 %copy-start.1 = (s32[3,16]{1,0:T(4,128)}, s32[3,16]{1,0:T(4,128)S(1)}, u32[]{:S(2)}) copy-start(s32[3,16]{1,0:T(4,128)S(1)} %fusion.6.mask_ref) | copy-start | bytes 580
  19.6 15.5 %collective-permute-start = (bf16[384,128]{1,0:T(8,128)(2,1)}, bf16[384,128]{1,0:T(8,128)(2,1)S(1)}, u32[]{:S(2)}, u32[]{:S(2)}) collective-permute-start(bf16[384,128]{1,0:T(8,128)(2,1)} %get-tuple-element.34), channel_id=1, source_target_pairs={{0,2},{1,3},{2,0},{3,1},{4,6},{5,7},{6,4},{7,5},{8,10},{9,11},{10,... | collective-permute-start | bytes 294920 | tf_op jit(solution)/shard_map/ppermute | solution.py:459
  21.6 44.6 %collective-permute-start.1 = (bf16[384,128]{1,0:T(8,128)(2,1)}, bf16[384,128]{1,0:T(8,128)(2,1)S(1)}, u32[]{:S(2)}, u32[]{:S(2)}) collective-permute-start(bf16[384,128]{1,0:T(8,128)(2,1)} %get-tuple-element.35), channel_id=1, source_target_pairs={{0,4},{1,5},{2,6},{3,7},{4,0},{5,1},{6,2},{7,3},{8,12},{9,13},{10,... | collective-permute-start | bytes 294920 | tf_op jit(solution)/shard_map/ppermute | solution.py:459
  23.1 47.9 %collective-permute-start.2 = (bf16[384,128]{1,0:T(8,128)(2,1)}, bf16[384,128]{1,0:T(8,128)(2,1)S(1)}, u32[]{:S(2)}, u32[]{:S(2)}) collective-permute-start(bf16[384,128]{1,0:T(8,128)(2,1)} %get-tuple-element.36), channel_id=1, source_target_pairs={{0,6},{1,7},{2,4},{3,5},{4,2},{5,3},{6,0},{7,1},{8,14},{9,15},{10,... | collective-permute-start | bytes 294920 | tf_op jit(solution)/shard_map/ppermute | solution.py:459
  23.2 71.4 %collective-permute-start.3 = (bf16[384,128]{1,0:T(8,128)(2,1)}, bf16[384,128]{1,0:T(8,128)(2,1)S(1)}, u32[]{:S(2)}, u32[]{:S(2)}) collective-permute-start(bf16[384,128]{1,0:T(8,128)(2,1)} %get-tuple-element.38), channel_id=1, source_target_pairs={{0,8},{1,9},{2,10},{3,11},{4,12},{5,13},{6,14},{7,15},{8,0},{9,1},... | collective-permute-start | bytes 294920 | tf_op jit(solution)/shard_map/ppermute | solution.py:459
  26.0 71.8 %collective-permute-start.4 = (bf16[384,128]{1,0:T(8,128)(2,1)}, bf16[384,128]{1,0:T(8,128)(2,1)}, u32[]{:S(2)}, u32[]{:S(2)}) collective-permute-start(bf16[384,128]{1,0:T(8,128)(2,1)} %get-tuple-element.39), channel_id=1, source_target_pairs={{0,10},{1,11},{2,8},{3,9},{4,14},{5,15},{6,12},{7,13},{8,2},{9,3},... | collective-permute-start | bytes 294920 | tf_op jit(solution)/shard_map/ppermute | solution.py:459
  35.1 50.5 %copy-start.3 = (bf16[384,128]{1,0:T(8,128)(2,1)}, bf16[384,128]{1,0:T(8,128)(2,1)S(1)}, u32[]{:S(2)}) copy-start(bf16[384,128]{1,0:T(8,128)(2,1)S(1)} %collective-permute-done.refs_1_) | copy-start | bytes 294916
  35.1 62.7 %collective-permute-start.5 = (bf16[384,128]{1,0:T(8,128)(2,1)}, bf16[384,128]{1,0:T(8,128)(2,1)}, u32[]{:S(2)}, u32[]{:S(2)}) collective-permute-start(bf16[384,128]{1,0:T(8,128)(2,1)} %get-tuple-element.40), channel_id=1, source_target_pairs={{0,12},{1,13},{2,14},{3,15},{4,8},{5,9},{6,10},{7,11},{8,4},{9,5},... | collective-permute-start | bytes 294920 | tf_op jit(solution)/shard_map/ppermute | solution.py:459
  66.2 19.4 %copy-start.4 = (bf16[384,128]{1,0:T(8,128)(2,1)}, bf16[384,128]{1,0:T(8,128)(2,1)S(1)}, u32[]{:S(2)}) copy-start(bf16[384,128]{1,0:T(8,128)(2,1)S(1)} %collective-permute-done.1.refs_2_) | copy-start | bytes 294916
  66.2 31.6 %collective-permute-start.6 = (bf16[384,128]{1,0:T(8,128)(2,1)}, bf16[384,128]{1,0:T(8,128)(2,1)}, u32[]{:S(2)}, u32[]{:S(2)}) collective-permute-start(bf16[384,128]{1,0:T(8,128)(2,1)} %get-tuple-element.41), channel_id=1, source_target_pairs={{0,14},{1,15},{2,12},{3,13},{4,10},{5,11},{6,8},{7,9},{8,6},{9,7},... | collective-permute-start | bytes 294920 | tf_op jit(solution)/shard_map/ppermute | solution.py:459
  71.0 14.7 %copy-start.5 = (bf16[384,128]{1,0:T(8,128)(2,1)}, bf16[384,128]{1,0:T(8,128)(2,1)S(1)}, u32[]{:S(2)}) copy-start(bf16[384,128]{1,0:T(8,128)(2,1)S(1)} %collective-permute-done.2.refs_3_) | copy-start | bytes 294916
  85.7 1.0 copy-start
  94.6 16.3 %copy-start.6 = (bf16[384,128]{1,0:T(8,128)(2,1)}, bf16[384,128]{1,0:T(8,128)(2,1)S(1)}, u32[]{:S(2)}) copy-start(bf16[384,128]{1,0:T(8,128)(2,1)S(1)} %collective-permute-done.3.refs_4_) | copy-start | bytes 294916
  97.8 47.6 %all-to-all-start.1 = ((bf16[16,256,128]{2,1,0:T(8,128)(2,1)}), bf16[16,256,128]{2,1,0:T(8,128)(2,1)S(1)}, u32[]{:S(2)}, u32[]{:S(2)}) async-start(bf16[16,256,128]{2,1,0:T(8,128)(2,1)} %copy-done), calls=%async_computation.1 | async-start | bytes 2097152 | tf_op jit(solution)/shard_map/all_to_all | solution.py:454
  112.8 2.2 %collective-permute-start.7 = (bf16[8,256,128]{2,1,0:T(8,128)(2,1)}, bf16[8,256,128]{2,1,0:T(8,128)(2,1)S(1)}, u32[]{:S(2)}, u32[]{:S(2)}) collective-permute-start(bf16[8,256,128]{2,1,0:T(8,128)(2,1)} %join_keys_values.1), channel_id=1, source_target_pairs={{0,1},{1,0},{2,3},{3,2},{4,5},{5,4},{6,7},{7,6},{8,9},{9,8},{10,11... | collective-permute-start | bytes 1572872 | tf_op jit(solution)/shard_map/ppermute | solution.py:463
  115.0 0.8 copy-start.2
  122.1 7.8 %collective-permute-start.8 = (bf16[128,128]{1,0:T(8,128)(2,1)}, bf16[128,128]{1,0:T(8,128)(2,1)S(1)}, u32[]{:S(2)}, u32[]{:S(2)}) collective-permute-start(bf16[128,128]{1,0:T(8,128)(2,1)} %get-tuple-element.52), channel_id=1, source_target_pairs={{0,2},{1,3},{2,0},{3,1},{4,6},{5,7},{6,4},{7,5},{8,10},{9,11},{10,... | collective-permute-start | bytes 98312 | tf_op jit(solution)/shard_map/ppermute | solution.py:459
  124.1 9.1 %collective-permute-start.9 = (bf16[128,128]{1,0:T(8,128)(2,1)}, bf16[128,128]{1,0:T(8,128)(2,1)S(1)}, u32[]{:S(2)}, u32[]{:S(2)}) collective-permute-start(bf16[128,128]{1,0:T(8,128)(2,1)} %get-tuple-element.53), channel_id=1, source_target_pairs={{0,4},{1,5},{2,6},{3,7},{4,0},{5,1},{6,2},{7,3},{8,12},{9,13},{10,... | collective-permute-start | bytes 98312 | tf_op jit(solution)/shard_map/ppermute | solution.py:459
  125.5 9.1 %collective-permute-start.10 = (bf16[128,128]{1,0:T(8,128)(2,1)}, bf16[128,128]{1,0:T(8,128)(2,1)S(1)}, u32[]{:S(2)}, u32[]{:S(2)}) collective-permute-start(bf16[128,128]{1,0:T(8,128)(2,1)} %get-tuple-element.54), channel_id=1, source_target_pairs={{0,6},{1,7},{2,4},{3,5},{4,2},{5,3},{6,0},{7,1},{8,14},{9,15},{10,... | collective-permute-start | bytes 98312 | tf_op jit(solution)/shard_map/ppermute | solution.py:459
  125.7 15.8 %collective-permute-start.11 = (bf16[128,128]{1,0:T(8,128)(2,1)}, bf16[128,128]{1,0:T(8,128)(2,1)S(1)}, u32[]{:S(2)}, u32[]{:S(2)}) collective-permute-start(bf16[128,128]{1,0:T(8,128)(2,1)} %get-tuple-element.55), channel_id=1, source_target_pairs={{0,8},{1,9},{2,10},{3,11},{4,12},{5,13},{6,14},{7,15},{8,0},{9,1},... | collective-permute-start | bytes 98312 | tf_op jit(solution)/shard_map/ppermute | solution.py:459
  128.4 14.6 %collective-permute-start.12 = (bf16[128,128]{1,0:T(8,128)(2,1)}, bf16[128,128]{1,0:T(8,128)(2,1)S(1)}, u32[]{:S(2)}, u32[]{:S(2)}) collective-permute-start(bf16[128,128]{1,0:T(8,128)(2,1)} %get-tuple-element.56), channel_id=1, source_target_pairs={{0,10},{1,11},{2,8},{3,9},{4,14},{5,15},{6,12},{7,13},{8,2},{9,3},... | collective-permute-start | bytes 98312 | tf_op jit(solution)/shard_map/ppermute | solution.py:459
  129.9 13.2 %copy-start.7 = (bf16[128,128]{1,0:T(8,128)(2,1)}, bf16[128,128]{1,0:T(8,128)(2,1)S(1)}, u32[]{:S(2)}) copy-start(bf16[128,128]{1,0:T(8,128)(2,1)S(1)} %collective-permute-done.8.refs_1_) | copy-start | bytes 98308
  129.9 13.2 %collective-permute-start.13 = (bf16[128,128]{1,0:T(8,128)(2,1)}, bf16[128,128]{1,0:T(8,128)(2,1)S(1)}, u32[]{:S(2)}, u32[]{:S(2)}) collective-permute-start(bf16[128,128]{1,0:T(8,128)(2,1)} %get-tuple-element.57), channel_id=1, source_target_pairs={{0,12},{1,13},{2,14},{3,15},{4,8},{5,9},{6,10},{7,11},{8,4},{9,5},... | collective-permute-start | bytes 98312 | tf_op jit(solution)/shard_map/ppermute | solution.py:459
  133.2 9.9 %copy-start.8 = (bf16[128,128]{1,0:T(8,128)(2,1)}, bf16[128,128]{1,0:T(8,128)(2,1)S(1)}, u32[]{:S(2)}) copy-start(bf16[128,128]{1,0:T(8,128)(2,1)S(1)} %collective-permute-done.9.refs_2_) | copy-start | bytes 98308
  133.2 9.9 %collective-permute-start.14 = (bf16[128,128]{1,0:T(8,128)(2,1)}, bf16[128,128]{1,0:T(8,128)(2,1)S(1)}, u32[]{:S(2)}, u32[]{:S(2)}) collective-permute-start(bf16[128,128]{1,0:T(8,128)(2,1)} %get-tuple-element.58), channel_id=1, source_target_pairs={{0,14},{1,15},{2,12},{3,13},{4,10},{5,11},{6,8},{7,9},{8,6},{9,7},... | collective-permute-start | bytes 98312 | tf_op jit(solution)/shard_map/ppermute | solution.py:459
  134.6 8.5 %copy-start.9 = (bf16[128,128]{1,0:T(8,128)(2,1)}, bf16[128,128]{1,0:T(8,128)(2,1)S(1)}, u32[]{:S(2)}) copy-start(bf16[128,128]{1,0:T(8,128)(2,1)S(1)} %collective-permute-done.10.refs_3_) | copy-start | bytes 98308
  141.5 1.7 %copy-start.10 = (bf16[128,128]{1,0:T(8,128)(2,1)}, bf16[128,128]{1,0:T(8,128)(2,1)S(1)}, u32[]{:S(2)}) copy-start(bf16[128,128]{1,0:T(8,128)(2,1)S(1)} %collective-permute-done.11.refs_4_) | copy-start | bytes 98308
  143.1 0.6 copy-start.11
  143.1 0.6 copy-start.12
  143.1 0.6 copy-start.13

commit v4 on v3

--- a/solution.py
+++ b/solution.py
@@ -216,15 +216,17 @@
     wait_copies(copies)
 
 
-def prepare_shared_kernel(full, pairs, me_ref, *refs):
-    operands, outs, scratch, out_sems = refs[:5], refs[5 : 5 + pairs], refs[5 + pairs : -1], refs[-1]
+def prepare_shared_kernel(full, me_ref, *refs):
+    operands, outs, scratch, out_sems = refs[:5], refs[5:7], refs[7:-1], refs[-1]
     copies = copy_list(out_sems)
 
     def send(rows, tensor):
-        for partner, out in enumerate(outs):
-            head = head_of(jnp.bitwise_xor(me_ref[0] // 2, partner), 0, full, full)
-            target = out.at[pl.ds(tensor * TILE, TILE)]
-            start_copy(copies, rows.at[:, traced_columns(head)], target)
+        for odd, out in enumerate(outs):
+            for flip in range(out.shape[0]):
+                pair = jnp.bitwise_xor(me_ref[0] // 2, 2 * flip + odd)
+                target = out.at[flip, pl.ds(tensor * TILE, TILE)]
+                source = rows.at[:, traced_columns(head_of(pair, 0, full, full))]
+                start_copy(copies, source, target)
 
     prepare_kernel(send, *operands, scratch)
     wait_copies(copies)
@@ -251,18 +253,49 @@
 
 def prepare_shared(full, pairs, me, *operands):
     return pl.pallas_call(
-        functools.partial(prepare_shared_kernel, full, pairs),
+        functools.partial(prepare_shared_kernel, full),
         name="prepare_shared",
-        out_shape=[bf16(3 * TILE, HEAD_DIM)] * pairs,
+        out_shape=[bf16(pairs // 2, 3 * TILE, HEAD_DIM)] * 2,
         in_specs=[IN_SMEM] + [IN_HBM] * 5,
-        out_specs=[ANYWHERE] * pairs,
+        out_specs=[ANYWHERE] * 2,
         scratch_shapes=prepare_scratch(operands[0], operands[3], 3 * pairs),
         compiler_params=PARAMS,
     )(me, *operands)
 
 
+def join_columns_kernel(own, other, *refs):
+    outs, (rows, in_sems, out_sems) = refs[:-3], refs[-3:]
+    count = own.shape[1]
+    loads, stores = copy_list(in_sems), copy_list(out_sems)
+    for flip in range(len(outs)):
+        start_copy(loads, own.at[flip], rows.at[flip, pl.ds(0, count)])
+        start_copy(loads, other.at[flip], rows.at[flip, pl.ds(count, count)])
+    for flip, out in enumerate(outs):
+        loads[1][2 * flip].wait()
+        loads[1][2 * flip + 1].wait()
+        start_copy(stores, rows.at[flip], out)
+    wait_copies(stores)
+
+
+def join_columns(own, other):
+    flips, count = own.shape[:2]
+    return pl.pallas_call(
+        join_columns_kernel,
+        name="join_columns",
+        out_shape=[bf16(2 * count, HEAD_DIM)] * flips,
+        in_specs=[ANYWHERE] * 2,
+        out_specs=[ANYWHERE] * flips,
+        scratch_shapes=[
+            pltpu.VMEM((flips, 2 * count, HEAD_DIM), jnp.bfloat16),
+            pltpu.SemaphoreType.DMA((2 * flips,)),
+            pltpu.SemaphoreType.DMA((flips,)),
+        ],
+        compiler_params=LEAVE_ROOM,
+    )(own, other)
+
+
 TOGETHER = 2
-UNROLL = 4
+UNROLL = 8
 
 
 def key_marks(keys):
@@ -309,9 +342,12 @@
 
     marked[...] = key_marks(part(slice(None), 1).reshape(-1, HEAD_DIM))
 
+    products = here.shape[0] // (stride * TOGETHER)
+    unroll = math.gcd(products, UNROLL)
+
     def step(index, carry):
-        for product in range(UNROLL):
-            at = (index * UNROLL + product) * TOGETHER
+        for product in range(unroll):
+            at = (index * unroll + product) * TOGETHER
             tiles = [(at + i) * stride for i in range(TOGETHER)]
             values = part(slice(None), 2).reshape(-1, HEAD_DIM)
             masks = [mask_ref[slot, tile] for tile in tiles]
@@ -320,110 +356,130 @@
                 out[tile, out_first : out_first + TILE] = block
         return carry
 
-    lax.fori_loop(0, here.shape[0] // (stride * TOGETHER * UNROLL), step, 0)
+    lax.fori_loop(0, products // unroll, step, 0)
 
 
 def marked_keys(devices):
     return pltpu.VMEM((devices * TILE, 2 * HEAD_DIM), jnp.bfloat16)
 
 
-def attend_whole_kernel(full, mask_ref, here, out, marked):
+def attend_whole_kernel(full, mask_ref, here, outs, out, marked, sems):
+    stores = copy_list(sems)
     for slot in range(full):
         attend_slot(mask_ref, slot, here, 3 * slot * TILE, out, slot * TILE, 1, marked)
+        rows = pl.ds(slot * TILE, TILE)
+        start_copy(stores, out.at[:, rows], outs.at[:, rows])
+    wait_copies(stores)
 
 
 def attend_whole(full, masks, here):
+    shape = (here.shape[0], full * TILE, HEAD_DIM)
     return pl.pallas_call(
         functools.partial(attend_whole_kernel, full),
         name="attend_whole",
-        out_shape=bf16(here.shape[0], full * TILE, HEAD_DIM),
+        out_shape=bf16(*shape),
         in_specs=[IN_SMEM, IN_VMEM],
-        out_specs=IN_VMEM,
-        scratch_shapes=[marked_keys(here.shape[0])],
+        out_specs=IN_HBM,
+        scratch_shapes=[
+            pltpu.VMEM(shape, jnp.bfloat16),
+            marked_keys(here.shape[0]),
+            pltpu.SemaphoreType.DMA((full,)),
+        ],
         compiler_params=LEAVE_ROOM,
     )(masks, here)
 
 
-def attend_shared_kernel(full, pairs, mask_ref, *refs):
-    blocks, other, outs = refs[:pairs], refs[pairs], refs[pairs + 1 : 2 * pairs + 1]
-    here, out, marked, in_sems, out_sems = refs[2 * pairs + 1 :]
+def attend_shared_kernel(full, mask_ref, *refs):
+    blocks, (other, *outs), scratch = refs[:-8], refs[-8:-5], refs[-5:]
+    here, out, marked, in_sems, out_sems = scratch
     loads, stores = copy_list(in_sems), copy_list(out_sems)
-    for partner, block in enumerate(blocks):
-        start_copy(loads, block, here.at[2 * partner])
-        start_copy(loads, other.at[partner], here.at[2 * partner + 1, pl.ds(TILE, 2 * TILE)])
+    for flip, block in enumerate(blocks):
+        for odd in range(2):
+            partner = 2 * flip + odd
+            start_copy(loads, block.at[pl.ds(3 * odd * TILE, 3 * TILE)], here.at[2 * partner])
+            target = here.at[2 * partner + 1, pl.ds(TILE, 2 * TILE)]
+            start_copy(loads, other.at[partner], target)
     wait_copies(loads)
     attend_slot(mask_ref, full, here, 0, out, 0, 2, marked)
-    for partner, target in enumerate(outs):
-        start_copy(stores, out.at[2 * partner], target)
+    for flip in range(len(blocks)):
+        for odd in range(2):
+            start_copy(stores, out.at[2 * (2 * flip + odd)], outs[odd].at[flip])
     wait_copies(stores)
 
 
 def attend_shared(full, masks, blocks, other):
-    pairs = len(blocks)
-    return pl.pallas_call(
-        functools.partial(attend_shared_kernel, full, pairs),
+    flips = len(blocks)
+    return pl.pallas_call(
+        functools.partial(attend_shared_kernel, full),
         name="attend_shared",
-        out_shape=[bf16(TILE, HEAD_DIM)] * pairs,
-        in_specs=[IN_SMEM] + [ANYWHERE] * (pairs + 1),
-        out_specs=[ANYWHERE] * pairs,
+        out_shape=[bf16(flips, TILE, HEAD_DIM)] * 2,
+        in_specs=[IN_SMEM] + [ANYWHERE] * (flips + 1),
+        out_specs=[ANYWHERE] * 2,
         scratch_shapes=[
-            pltpu.VMEM((2 * pairs, 3 * TILE, HEAD_DIM), jnp.bfloat16),
-            pltpu.VMEM((2 * pairs, TILE, HEAD_DIM), jnp.bfloat16),
-            marked_keys(2 * pairs),
-            pltpu.SemaphoreType.DMA((2 * pairs,)),
-            pltpu.SemaphoreType.DMA((pairs,)),
+            pltpu.VMEM((4 * flips, 3 * TILE, HEAD_DIM), jnp.bfloat16),
+            pltpu.VMEM((4 * flips, TILE, HEAD_DIM), jnp.bfloat16),
+            marked_keys(4 * flips),
+            pltpu.SemaphoreType.DMA((4 * flips,)),
+            pltpu.SemaphoreType.DMA((2 * flips,)),
         ],
-        compiler_params=PARAMS,
+        compiler_params=LEAVE_ROOM,
     )(masks, *blocks, other)
 
 
-def join_kernel(*refs):
+def join_keys_values_kernel(*refs):
     blocks, (out, rows, in_sems, out_sems) = refs[:-4], refs[-4:]
     loads, stores = copy_list(in_sems), copy_list(out_sems)
-    for index, block in enumerate(blocks):
-        start_copy(loads, block.at[pl.ds(TILE, 2 * TILE)], rows.at[index])
-    for index, load in enumerate(loads[1]):
+    for partner in range(2 * len(blocks)):
+        source = blocks[partner // 2].at[pl.ds((3 * (partner % 2) + 1) * TILE, 2 * TILE)]
+        start_copy(loads, source, rows.at[partner])
+    for partner, load in enumerate(loads[1]):
         load.wait()
-        start_copy(stores, rows.at[index], out.at[index])
+        start_copy(stores, rows.at[partner], out.at[partner])
     wait_copies(stores)
 
 
 def join_keys_values(blocks):
-    shape = (len(blocks), 2 * TILE, HEAD_DIM)
-    sems = pltpu.SemaphoreType.DMA((len(blocks),))
-    return pl.pallas_call(
-        join_kernel,
+    shape = (2 * len(blocks), 2 * TILE, HEAD_DIM)
+    sems = pltpu.SemaphoreType.DMA((2 * len(blocks),))
+    return pl.pallas_call(
+        join_keys_values_kernel,
         name="join_keys_values",
         out_shape=bf16(*shape),
         in_specs=[ANYWHERE] * len(blocks),
         out_specs=ANYWHERE,
         scratch_shapes=[pltpu.VMEM(shape, jnp.bfloat16), sems, sems],
-        compiler_params=PARAMS,
+        compiler_params=LEAVE_ROOM,
     )(*blocks)
 
 
 def collect_shared_kernel(full, me_ref, *refs):
     blocks, (out, rows, in_sems, out_sems) = refs[:-4], refs[-4:]
     loads, stores = copy_list(in_sems), copy_list(out_sems)
-    for partner, block in enumerate(blocks):
-        start_copy(loads, block, rows.at[partner])
-    for partner, load in enumerate(loads[1]):
+    for flip, block in enumerate(blocks):
+        start_copy(loads, block, rows.at[flip])
+    for flip, load in enumerate(loads[1]):
         load.wait()
-        head = head_of(jnp.bitwise_xor(me_ref[0] // 2, partner), 0, full, full)
-        start_copy(stores, rows.at[partner], out.at[:, traced_columns(head)])
+        for odd in range(2):
+            pair = jnp.bitwise_xor(me_ref[0] // 2, 2 * flip + odd)
+            target = out.at[:, traced_columns(head_of(pair, 0, full, full))]
+            start_copy(stores, rows.at[flip, pl.ds(odd * TILE, TILE)], target)
     wait_copies(stores)
 
 
 def collect_shared(full, shape, me, blocks):
-    sems = pltpu.SemaphoreType.DMA((len(blocks),))
+    flips = len(blocks)
     return pl.pallas_call(
         functools.partial(collect_shared_kernel, full),
         name="collect_shared",
         out_shape=bf16(*shape),
-        in_specs=[IN_SMEM] + [ANYWHERE] * len(blocks),
+        in_specs=[IN_SMEM] + [ANYWHERE] * flips,
         out_specs=IN_HBM,
-        scratch_shapes=[pltpu.VMEM((len(blocks), TILE, HEAD_DIM), jnp.bfloat16), sems, sems],
-        compiler_params=PARAMS,
+        scratch_shapes=[
+            pltpu.VMEM((flips, 2 * TILE, HEAD_DIM), jnp.bfloat16),
+            pltpu.SemaphoreType.DMA((flips,)),
+            pltpu.SemaphoreType.DMA((2 * flips,)),
+        ],
+        compiler_params=LEAVE_ROOM,
     )(me, *blocks)
 
 
@@ -494,16 +550,21 @@
 
     whole = prepare_whole(full, devices, queries, *rest)
     masks = tile_masks(full, my_index, key_tiles, key_count)
-    shared = prepare_shared(full, pairs, me, after(queries, masks, whole), *rest)
+    even, odd = prepare_shared(full, pairs, me, after(queries, masks, whole), *rest)
     whole = with_all(whole)
-    shared = [with_partner(block, k) for k, block in enumerate(shared)]
-    near, far = shared[: pairs // 2], shared[pairs // 2 :]
-    whole_out = attend_whole(full, masks, after(whole, *near))
+    shared = join_columns(even, with_partner(odd, 1))
+    near, far = shared[: pairs // 4], shared[pairs // 4 :]
+    near = [with_partner(block, 2 * flip) for flip, block in enumerate(near)]
+    whole = after(whole, *near, *far)
+    far = all_after(far, whole)
+    far = [with_partner(block, 2 * flip + pairs // 2) for flip, block in enumerate(far)]
+    whole_out = attend_whole(full, masks, whole)
     shared = all_after(near + far, whole_out)
     whole_back = with_all(after(whole_out, *shared))
     other = with_sibling(join_keys_values(shared))
-    shared_out = attend_shared(full, masks, shared, other)
-    shared_back = [with_partner(block, k) for k, block in enumerate(shared_out)]
+    even, odd = attend_shared(full, masks, shared, other)
+    shared_back = join_columns(even, with_partner(odd, 1))
+    shared_back = [with_partner(block, 2 * flip) for flip, block in enumerate(shared_back)]
     so_far = collect_shared(full, queries.shape, me, shared_back)
     return collect_whole(full, whole_back, so_far)
 

time: 147 us -> 141 us (0.959)
  starting transfers between devices: 48.8 us -> 35.8 us
  local copies, waits for them, and re-layouts: 5.9 us -> 9.14 us
  waiting for transfers between devices: 57.8 us -> 60 us
    all_to_all x2, starting transfers between devices: 20.5 us -> 13.1 us  [with_all(): lax.all_to_all(blocks, 'seq', split_axis=0, concat_axis=0, tiled=True)]
    ppermute x14 -> x8, starting transfers between devices: 27.8 us -> 22.3 us  [with_partner(): lax.ppermute(block, 'seq', [(i, i ^ 2 * k) for i in range(devices)])]
    unnamed x32 -> x20, local copies, waits for them, and re-layouts: 3.55 us -> 6.79 us
    all_to_all x2, waiting for transfers between devices: 0.45 us -> 3.36 us  [with_all(): lax.all_to_all(blocks, 'seq', split_axis=0, concat_axis=0, tiled=True)]
    pallas_call x3 -> x5, Pallas kernels: 11.8 us -> 14.2 us  [the longest x1 6.21 us: attend_shared(): pl.pallas_call(functools.partial(attend_shared_kernel, full), name='atten...]
    ppermute x14 -> x8, waiting for transfers between devices: 55.6 us -> 55.1 us  [with_partner(): lax.ppermute(block, 'seq', [(i, i ^ 2 * k) for i in range(devices)])]
  transfers between devices with their start and end apart: 17 -> 11, of which waited for: 8 -> 7; matrix products, arithmetic and copies ran while one was open for 3% -> 3% of each run, Pallas kernels for 19% -> 21%
where the time goes in v4:
time: 141 us; the launch traced here: 140 us
  waiting for transfers between devices  60 us (43%)
  starting transfers between devices  35.8 us (25%)
  Pallas kernels  34.7 us (25%)
  local copies, waits for them, and re-layouts  9.14 us (6%)
    ppermute x8, waiting for transfers between devices, with_partner(): lax.ppermute(block, 'seq', [(i, i ^ 2 * k) for i in range(devices)])  55.1 us
    ppermute x8, starting transfers between devices, with_partner(): lax.ppermute(block, 'seq', [(i, i ^ 2 * k) for i in range(devices)])  22.3 us
    pallas_call x1, Pallas kernels, attend_whole(): pl.pallas_call(functools.partial(attend_whole_kernel, full), name='attend...  13.5 us
    all_to_all x2, starting transfers between devices, with_all(): lax.all_to_all(blocks, 'seq', split_axis=0, concat_axis=0, tiled=True)  13.1 us
    unnamed x20, local copies, waits for them, and re-layouts  6.79 us
    pallas_call x1, Pallas kernels, attend_shared(): pl.pallas_call(functools.partial(attend_shared_kernel, full), name='atten...  6.21 us
    pallas_call x1, Pallas kernels, prepare_whole(): pl.pallas_call(functools.partial(prepare_whole_kernel, full), name='prepa...  4.57 us
    pallas_call x1, Pallas kernels, prepare_shared(): pl.pallas_call(functools.partial(prepare_shared_kernel, full), name='prep...  3.64 us
  transfers between devices with their start and end apart: 11, of which 7 were waited for; matrix products, arithmetic and copies ran while one was open for 3% of the time, Pallas kernels for 21%

profile of v4, /device:TPU:0, one launch (start us, length us, event | category | flops | bytes accessed | tf_op | source)
XLA Modules:
  0.0 140.4 jit_solution(7927350988079208149)
XLA Ops:
  0.0 4.6 %prepare_whole.1 = bf16[16,768,128]{2,1,0:T(8,128)(2,1)} custom-call(bf16[128,5120]{1,0:T(8,128)(2,1)} %refs_0_.2, bf16[128,5120]{1,0:T(8,128)(2,1)} %refs_1_.3, bf16[128,5120]{1,0:T(8,128)(2,1)} %refs_2_.3, f32[5120]{0:T(1024)} %refs_3_.3, f32[5120]{0:T(1024)} %refs_4_.3), custom_call_target="tpu_custom_call" | custom-call | tf_op jit(solution)/shard_map/prepare_whole/pallas_call | solution.py:243
  4.6 7.4 %all-to-all-start = ((bf16[16,768,128]{2,1,0:T(8,128)(2,1)}), bf16[16,768,128]{2,1,0:T(8,128)(2,1)S(1)}, u32[]{:S(2)}, u32[]{:S(2)}) async-start(bf16[16,768,128]{2,1,0:T(8,128)(2,1)} %prepare_whole.1), calls=%async_computation | async-start | bytes 6291456 | tf_op jit(solution)/shard_map/all_to_all | solution.py:510
  12.3 1.1 copy.12
  14.8 1.1 gather_fusion.2
  16.0 3.6 %prepare_shared.1 = (bf16[4,384,128]{2,1,0:T(8,128)(2,1)}, bf16[4,384,128]{2,1,0:T(8,128)(2,1)}) custom-call(s32[1]{0:T(128)} %bitcast.1.me_ref, bf16[128,5120]{1,0:T(8,128)(2,1)} %refs_0_.2, bf16[128,5120]{1,0:T(8,128)(2,1)} %refs_1_.3, bf16[128,5120]{1,0:T(8,128)(2,1)} %refs_2_.3, f32[5120]{0:T(1024)} %refs_3_.3, f32[5120]{0:T(1024)} %refs_4_.3), custom_call_target="tpu_custom_call" | custom-call | tf_op jit(solution)/shard_map/prepare_shared/pallas_call | solution.py:255
  19.6 2.0 %collective-permute-start = (bf16[4,384,128]{2,1,0:T(8,128)(2,1)}, bf16[4,384,128]{2,1,0:T(8,128)(2,1)S(1)}, u32[]{:S(2)}, u32[]{:S(2)}) collective-permute-start(bf16[4,384,128]{2,1,0:T(8,128)(2,1)} %get-tuple-element.28), channel_id=1, source_target_pairs={{0,2},{1,3},{2,0},{3,1},{4,6},{5,7},{6,4},{7,5},{8,10},{9,11},{10,... | collective-permute-start | bytes 1179656 | tf_op jit(solution)/shard_map/ppermute | solution.py:515
  21.6 25.0 %collective-permute-done.other = bf16[4,384,128]{2,1,0:T(8,128)(2,1)S(1)} collective-permute-done((bf16[4,384,128]{2,1,0:T(8,128)(2,1)}, bf16[4,384,128]{2,1,0:T(8,128)(2,1)S(1)}, u32[]{:S(2)}, u32[]{:S(2)}) %collective-permute-start) | collective-permute-done | bytes 393248 | tf_op jit(solution)/shard_map/ppermute | solution.py:515
  46.6 1.0 copy-done.5
  47.6 2.1 %join_columns.2 = (bf16[768,128]{1,0:T(8,128)(2,1)S(1)}, bf16[768,128]{1,0:T(8,128)(2,1)S(1)}, bf16[768,128]{1,0:T(8,128)(2,1)S(1)}, bf16[768,128]{1,0:T(8,128)(2,1)S(1)}) custom-call(bf16[4,384,128]{2,1,0:T(8,128)(2,1)S(1)} %copy-done.5, bf16[4,384,128]{2,1,0:T(8,128)(2,1)S(1)} %collective-permute-done.other), custom_call_target="tpu_custom_call" | custom-call | tf_op jit(solution)/shard_map/join_columns/pallas_call | solution.py:282
  49.7 0.7 copy-done.6
  50.4 0.7 copy-done.7
  51.0 17.0 %collective-permute-done.1.refs_1_ = bf16[768,128]{1,0:T(8,128)(2,1)S(1)} collective-permute-done((bf16[768,128]{1,0:T(8,128)(2,1)S(1)}, bf16[768,128]{1,0:T(8,128)(2,1)S(1)}, u32[]{:S(2)}, u32[]{:S(2)}) %collective-permute-start.1) | collective-permute-done | bytes 196640 | tf_op jit(solution)/shard_map/ppermute | solution.py:515
  68.0 3.4 %all-to-all-done.here = bf16[16,768,128]{2,1,0:T(8,128)(2,1)S(1)} async-done(((bf16[16,768,128]{2,1,0:T(8,128)(2,1)}), bf16[16,768,128]{2,1,0:T(8,128)(2,1)S(1)}, u32[]{:S(2)}, u32[]{:S(2)}) %all-to-all-start) | async-done | bytes 3145760 | tf_op jit(solution)/shard_map/all_to_all | solution.py:510
  71.4 13.5 %collective-permute-start.2 = (bf16[768,128]{1,0:T(8,128)(2,1)}, bf16[768,128]{1,0:T(8,128)(2,1)S(1)}, u32[]{:S(2)}, u32[]{:S(2)}) collective-permute-start(bf16[768,128]{1,0:T(8,128)(2,1)} %copy-done.7), channel_id=1, source_target_pairs={{0,8},{1,9},{2,10},{3,11},{4,12},{5,13},{6,14},{7,15},{8,0},{9,1},... | collective-permute-start | bytes 589832 | tf_op jit(solution)/shard_map/ppermute | solution.py:515
  85.0 13.5 %attend_whole.1 = bf16[16,256,128]{2,1,0:T(8,128)(2,1)S(1)} custom-call(s32[3,16]{1,0:T(4,128)S(1)} %fusion.6.mask_ref, bf16[16,768,128]{2,1,0:T(8,128)(2,1)S(1)} %all-to-all-done.here), custom_call_target="tpu_custom_call" | custom-call | tf_op jit(solution)/shard_map/attend_whole/pallas_call | solution.py:377
  98.5 1.0 copy-done
  99.5 0.7 copy-done.1
  100.2 0.7 copy-done.3
  100.9 5.7 %all-to-all-start.1 = ((bf16[16,256,128]{2,1,0:T(8,128)(2,1)}), bf16[16,256,128]{2,1,0:T(8,128)(2,1)S(1)}, u32[]{:S(2)}, u32[]{:S(2)}) async-start(bf16[16,256,128]{2,1,0:T(8,128)(2,1)} %copy-done), calls=%async_computation.1 | async-start | bytes 2097152 | tf_op jit(solution)/shard_map/all_to_all | solution.py:510
  106.6 0.9 copy-done.4
  107.5 1.5 %join_keys_values.1 = bf16[8,256,128]{2,1,0:T(8,128)(2,1)S(1)} custom-call(bf16[768,128]{1,0:T(8,128)(2,1)S(1)} %get-tuple-element.36.refs_0_, bf16[768,128]{1,0:T(8,128)(2,1)S(1)} %collective-permute-done.1.refs_1_, bf16[768,128]{1,0:T(8,128)(2,1)S(1)} %copy-done.2, bf16[768,128]{1,0:T(8,128)(2,1)S(1)} %copy-done.4), custom_call_target="tpu_custom_call" | custom-call | tf_op jit(solution)/shard_map/join_keys_values/pallas_call | solution.py:444
  109.5 1.5 %collective-permute-done.4.refs_4_ = bf16[8,256,128]{2,1,0:T(8,128)(2,1)S(1)} collective-permute-done((bf16[8,256,128]{2,1,0:T(8,128)(2,1)S(1)}, bf16[8,256,128]{2,1,0:T(8,128)(2,1)S(1)}, u32[]{:S(2)}, u32[]{:S(2)}) %collective-permute-start.4) | collective-permute-done | bytes 524320 | tf_op jit(solution)/shard_map/ppermute | solution.py:519
  111.0 6.2 %attend_shared.1 = (bf16[4,128,128]{2,1,0:T(8,128)(2,1)S(1)}, bf16[4,128,128]{2,1,0:T(8,128)(2,1)S(1)}) custom-call(s32[3,16]{1,0:T(4,128)S(1)} %fusion.6.mask_ref, bf16[768,128]{1,0:T(8,128)(2,1)S(1)} %get-tuple-element.36.refs_0_, bf16[768,128]{1,0:T(8,128)(2,1)S(1)} %collective-permute-done.1.refs_1_, bf16[768,128]{1,0:T(8,128)(2,1)S(1)} %copy-done.2, ...), custom_call_target="tpu_custom_call" | custom-call | tf_op jit(solution)/shard_map/attend_shared/pallas_call | solution.py:412
  117.2 2.0 %collective-permute-start.5 = (bf16[4,128,128]{2,1,0:T(8,128)(2,1)S(1)}, bf16[4,128,128]{2,1,0:T(8,128)(2,1)S(1)}, u32[]{:S(2)}, u32[]{:S(2)}) collective-permute-start(bf16[4,128,128]{2,1,0:T(8,128)(2,1)S(1)} %get-tuple-element.42), channel_id=1, source_target_pairs={{0,2},{1,3},{2,0},{3,1},{4,6},{5,7},{6,4},{7,5},{8,10},{9,11},{10,... | collective-permute-start | bytes 393224 | tf_op jit(solution)/shard_map/ppermute | solution.py:515
  119.2 5.4 %collective-permute-done.5.other = bf16[4,128,128]{2,1,0:T(8,128)(2,1)S(1)} collective-permute-done((bf16[4,128,128]{2,1,0:T(8,128)(2,1)S(1)}, bf16[4,128,128]{2,1,0:T(8,128)(2,1)S(1)}, u32[]{:S(2)}, u32[]{:S(2)}) %collective-permute-start.5) | collective-permute-done | bytes 131104 | tf_op jit(solution)/shard_map/ppermute | solution.py:515
  124.6 0.8 join_columns.3
  125.4 2.3 %collective-permute-start.6 = (bf16[256,128]{1,0:T(8,128)(2,1)S(1)}, bf16[256,128]{1,0:T(8,128)(2,1)S(1)}, u32[]{:S(2)}, u32[]{:S(2)}) collective-permute-start(bf16[256,128]{1,0:T(8,128)(2,1)S(1)} %get-tuple-element.44), channel_id=1, source_target_pairs={{0,4},{1,5},{2,6},{3,7},{4,0},{5,1},{6,2},{7,3},{8,12},{9,13},{10,... | collective-permute-start | bytes 196616 | tf_op jit(solution)/shard_map/ppermute | solution.py:515
  127.7 1.9 %collective-permute-start.7 = (bf16[256,128]{1,0:T(8,128)(2,1)S(1)}, bf16[256,128]{1,0:T(8,128)(2,1)S(1)}, u32[]{:S(2)}, u32[]{:S(2)}) collective-permute-start(bf16[256,128]{1,0:T(8,128)(2,1)S(1)} %get-tuple-element.45), channel_id=1, source_target_pairs={{0,8},{1,9},{2,10},{3,11},{4,12},{5,13},{6,14},{7,15},{8,0},{9,1},... | collective-permute-start | bytes 196616 | tf_op jit(solution)/shard_map/ppermute | solution.py:515
  130.1 1.3 collective-permute-done.6.refs_1_
  131.5 6.4 %collective-permute-done.7.refs_2_ = bf16[256,128]{1,0:T(8,128)(2,1)S(1)} collective-permute-done((bf16[256,128]{1,0:T(8,128)(2,1)S(1)}, bf16[256,128]{1,0:T(8,128)(2,1)S(1)}, u32[]{:S(2)}, u32[]{:S(2)}) %collective-permute-start.7) | collective-permute-done | bytes 65568 | tf_op jit(solution)/shard_map/ppermute | solution.py:515
  137.9 1.1 collect_shared.1._
  139.0 1.2 collect_whole.1
  (30 shorter events, 2.8 us)
Async XLA Ops:
  4.6 7.6 %copy-start.8 = (s32[40,16]{0,1:T(8,128)S(1)}, s32[40,16]{0,1:T(8,128)}, u32[]{:S(2)}) copy-start(s32[40,16]{0,1:T(8,128)} %param.13) | copy-start | bytes 7684
  4.6 66.8 %all-to-all-start = ((bf16[16,768,128]{2,1,0:T(8,128)(2,1)}), bf16[16,768,128]{2,1,0:T(8,128)(2,1)S(1)}, u32[]{:S(2)}, u32[]{:S(2)}) async-start(bf16[16,768,128]{2,1,0:T(8,128)(2,1)} %prepare_whole.1), calls=%async_computation | async-start | bytes 6291456 | tf_op jit(solution)/shard_map/all_to_all | solution.py:510
  19.6 27.0 %collective-permute-start = (bf16[4,384,128]{2,1,0:T(8,128)(2,1)}, bf16[4,384,128]{2,1,0:T(8,128)(2,1)S(1)}, u32[]{:S(2)}, u32[]{:S(2)}) collective-permute-start(bf16[4,384,128]{2,1,0:T(8,128)(2,1)} %get-tuple-element.28), channel_id=1, source_target_pairs={{0,2},{1,3},{2,0},{3,1},{4,6},{5,7},{6,4},{7,5},{8,10},{9,11},{10,... | collective-permute-start | bytes 1179656 | tf_op jit(solution)/shard_map/ppermute | solution.py:515
  46.6 1.0 copy-start.5
  49.7 0.7 copy-start.6
  50.4 0.7 copy-start.7
  51.0 17.0 %collective-permute-start.1 = (bf16[768,128]{1,0:T(8,128)(2,1)S(1)}, bf16[768,128]{1,0:T(8,128)(2,1)S(1)}, u32[]{:S(2)}, u32[]{:S(2)}) collective-permute-start(bf16[768,128]{1,0:T(8,128)(2,1)S(1)} %get-tuple-element.30), channel_id=1, source_target_pairs={{0,4},{1,5},{2,6},{3,7},{4,0},{5,1},{6,2},{7,3},{8,12},{9,13},{10,... | collective-permute-start | bytes 589832 | tf_op jit(solution)/shard_map/ppermute | solution.py:515
  71.4 28.1 %collective-permute-start.2 = (bf16[768,128]{1,0:T(8,128)(2,1)}, bf16[768,128]{1,0:T(8,128)(2,1)S(1)}, u32[]{:S(2)}, u32[]{:S(2)}) collective-permute-start(bf16[768,128]{1,0:T(8,128)(2,1)} %copy-done.7), channel_id=1, source_target_pairs={{0,8},{1,9},{2,10},{3,11},{4,12},{5,13},{6,14},{7,15},{8,0},{9,1},... | collective-permute-start | bytes 589832 | tf_op jit(solution)/shard_map/ppermute | solution.py:515
  84.9 15.2 %collective-permute-start.3 = (bf16[768,128]{1,0:T(8,128)(2,1)}, bf16[768,128]{1,0:T(8,128)(2,1)S(1)}, u32[]{:S(2)}, u32[]{:S(2)}) collective-permute-start(bf16[768,128]{1,0:T(8,128)(2,1)} %copy-done.6), channel_id=1, source_target_pairs={{0,12},{1,13},{2,14},{3,15},{4,8},{5,9},{6,10},{7,11},{8,4},{9,5},... | collective-permute-start | bytes 589832 | tf_op jit(solution)/shard_map/ppermute | solution.py:515
  98.5 1.0 copy-start
  99.5 0.7 copy-start.1
  100.2 0.7 copy-start.3
  100.9 5.7 %copy-start.2 = (bf16[768,128]{1,0:T(8,128)(2,1)S(1)}, bf16[768,128]{1,0:T(8,128)(2,1)}, u32[]{:S(2)}) copy-start(bf16[768,128]{1,0:T(8,128)(2,1)} %copy-done.1) | copy-start | bytes 589828
  100.9 38.1 %all-to-all-start.1 = ((bf16[16,256,128]{2,1,0:T(8,128)(2,1)}), bf16[16,256,128]{2,1,0:T(8,128)(2,1)S(1)}, u32[]{:S(2)}, u32[]{:S(2)}) async-start(bf16[16,256,128]{2,1,0:T(8,128)(2,1)} %copy-done), calls=%async_computation.1 | async-start | bytes 2097152 | tf_op jit(solution)/shard_map/all_to_all | solution.py:510
  106.6 0.9 copy-start.4
  109.0 2.0 %collective-permute-start.4 = (bf16[8,256,128]{2,1,0:T(8,128)(2,1)S(1)}, bf16[8,256,128]{2,1,0:T(8,128)(2,1)S(1)}, u32[]{:S(2)}, u32[]{:S(2)}) collective-permute-start(bf16[8,256,128]{2,1,0:T(8,128)(2,1)S(1)} %join_keys_values.1), channel_id=1, source_target_pairs={{0,1},{1,0},{2,3},{3,2},{4,5},{5,4},{6,7},{7,6},{8,9},{9,8},{10,11... | collective-permute-start | bytes 1572872 | tf_op jit(solution)/shard_map/ppermute | solution.py:519
  117.2 7.4 %collective-permute-start.5 = (bf16[4,128,128]{2,1,0:T(8,128)(2,1)S(1)}, bf16[4,128,128]{2,1,0:T(8,128)(2,1)S(1)}, u32[]{:S(2)}, u32[]{:S(2)}) collective-permute-start(bf16[4,128,128]{2,1,0:T(8,128)(2,1)S(1)} %get-tuple-element.42), channel_id=1, source_target_pairs={{0,2},{1,3},{2,0},{3,1},{4,6},{5,7},{6,4},{7,5},{8,10},{9,11},{10,... | collective-permute-start | bytes 393224 | tf_op jit(solution)/shard_map/ppermute | solution.py:515
  125.4 6.1 %collective-permute-start.6 = (bf16[256,128]{1,0:T(8,128)(2,1)S(1)}, bf16[256,128]{1,0:T(8,128)(2,1)S(1)}, u32[]{:S(2)}, u32[]{:S(2)}) collective-permute-start(bf16[256,128]{1,0:T(8,128)(2,1)S(1)} %get-tuple-element.44), channel_id=1, source_target_pairs={{0,4},{1,5},{2,6},{3,7},{4,0},{5,1},{6,2},{7,3},{8,12},{9,13},{10,... | collective-permute-start | bytes 196616 | tf_op jit(solution)/shard_map/ppermute | solution.py:515
  127.7 10.2 %collective-permute-start.7 = (bf16[256,128]{1,0:T(8,128)(2,1)S(1)}, bf16[256,128]{1,0:T(8,128)(2,1)S(1)}, u32[]{:S(2)}, u32[]{:S(2)}) collective-permute-start(bf16[256,128]{1,0:T(8,128)(2,1)S(1)} %get-tuple-element.45), channel_id=1, source_target_pairs={{0,8},{1,9},{2,10},{3,11},{4,12},{5,13},{6,14},{7,15},{8,0},{9,1},... | collective-permute-start | bytes 196616 | tf_op jit(solution)/shard_map/ppermute | solution.py:515
  129.6 8.2 %collective-permute-start.8 = (bf16[256,128]{1,0:T(8,128)(2,1)S(1)}, bf16[256,128]{1,0:T(8,128)(2,1)S(1)}, u32[]{:S(2)}, u32[]{:S(2)}) collective-permute-start(bf16[256,128]{1,0:T(8,128)(2,1)S(1)} %get-tuple-element.46), channel_id=1, source_target_pairs={{0,12},{1,13},{2,14},{3,15},{4,8},{5,9},{6,10},{7,11},{8,4},{9,5},... | collective-permute-start | bytes 196616 | tf_op jit(solution)/shard_map/ppermute | solution.py:515

commit v5 on v4

--- a/solution.py
+++ b/solution.py
@@ -294,21 +294,21 @@
     )(own, other)
 
 
-TOGETHER = 2
-UNROLL = 8
-
-
-def key_marks(keys):
-    shape = (keys.shape[0], HEAD_DIM)
+UNROLL = 4
+
+
+def write_marks(marked):
+    shape = (marked.shape[0], HEAD_DIM)
     tile = lax.broadcasted_iota(jnp.int32, shape, 0) // TILE
     marks = jnp.where(lax.broadcasted_iota(jnp.int32, shape, 1) == tile, 1.0, 0.0)
-    return jnp.concatenate([keys, marks.astype(jnp.bfloat16)], axis=1)
+    marked[:, HEAD_DIM:] = marks.astype(jnp.bfloat16)
 
 
 def query_masks(queries, mask):
-    bit = jnp.minimum(lax.broadcasted_iota(jnp.int32, queries.shape, 1), 31)
+    bit = jnp.minimum(lax.broadcasted_iota(jnp.int32, (1, HEAD_DIM), 1), 31)
     offsets = jnp.where((mask >> bit) & 1 == 1, jnp.float32(0.0), jnp.float32(-1e30))
-    return jnp.concatenate([queries, offsets.astype(jnp.bfloat16)], axis=1)
+    offsets = jnp.broadcast_to(offsets, queries.shape).astype(jnp.bfloat16)
+    return jnp.concatenate([queries, offsets], axis=1)
 
 
 def attend_rows(queries, keys, values, masks):
@@ -336,19 +336,19 @@
     ]
 
 
-def attend_slot(mask_ref, slot, here, first, out, out_first, stride, marked):
+def attend_slot(mask_ref, slot, here, first, out, out_first, stride, together, marked):
     def part(tile, tensor):
         return here[tile, first + tensor * TILE : first + (tensor + 1) * TILE]
 
-    marked[...] = key_marks(part(slice(None), 1).reshape(-1, HEAD_DIM))
-
-    products = here.shape[0] // (stride * TOGETHER)
+    marked[:, :HEAD_DIM] = part(slice(None), 1).reshape(-1, HEAD_DIM)
+
+    products = here.shape[0] // (stride * together)
     unroll = math.gcd(products, UNROLL)
 
     def step(index, carry):
         for product in range(unroll):
-            at = (index * unroll + product) * TOGETHER
-            tiles = [(at + i) * stride for i in range(TOGETHER)]
+            at = (index * unroll + product) * together
+            tiles = [(at + i) * stride for i in range(together)]
             values = part(slice(None), 2).reshape(-1, HEAD_DIM)
             masks = [mask_ref[slot, tile] for tile in tiles]
             blocks = attend_rows([part(tile, 0) for tile in tiles], marked[...], values, masks)
@@ -365,8 +365,9 @@
 
 def attend_whole_kernel(full, mask_ref, here, outs, out, marked, sems):
     stores = copy_list(sems)
+    write_marks(marked)
     for slot in range(full):
-        attend_slot(mask_ref, slot, here, 3 * slot * TILE, out, slot * TILE, 1, marked)
+        attend_slot(mask_ref, slot, here, 3 * slot * TILE, out, slot * TILE, 1, 4, marked)
         rows = pl.ds(slot * TILE, TILE)
         start_copy(stores, out.at[:, rows], outs.at[:, rows])
     wait_copies(stores)
@@ -385,7 +386,7 @@
             marked_keys(here.shape[0]),
             pltpu.SemaphoreType.DMA((full,)),
         ],
-        compiler_params=LEAVE_ROOM,
+        compiler_params=PARAMS,
     )(masks, here)
 
 
@@ -399,8 +400,9 @@
             start_copy(loads, block.at[pl.ds(3 * odd * TILE, 3 * TILE)], here.at[2 * partner])
             target = here.at[2 * partner + 1, pl.ds(TILE, 2 * TILE)]
             start_copy(loads, other.at[partner], target)
+    write_marks(marked)
     wait_copies(loads)
-    attend_slot(mask_ref, full, here, 0, out, 0, 2, marked)
+    attend_slot(mask_ref, full, here, 0, out, 0, 2, 2, marked)
     for flip in range(len(blocks)):
         for odd in range(2):
             start_copy(stores, out.at[2 * (2 * flip + odd)], outs[odd].at[flip])
@@ -453,7 +455,7 @@
 
 
 def collect_shared_kernel(full, me_ref, *refs):
-    blocks, (out, rows, in_sems, out_sems) = refs[:-4], refs[-4:]
+    blocks, (_, out, rows, in_sems, out_sems) = refs[:-5], refs[-5:]
     loads, stores = copy_list(in_sems), copy_list(out_sems)
     for flip, block in enumerate(blocks):
         start_copy(loads, block, rows.at[flip])
@@ -466,24 +468,25 @@
     wait_copies(stores)
 
 
-def collect_shared(full, shape, me, blocks):
+def collect_shared(full, me, blocks, so_far):
     flips = len(blocks)
     return pl.pallas_call(
         functools.partial(collect_shared_kernel, full),
         name="collect_shared",
-        out_shape=bf16(*shape),
-        in_specs=[IN_SMEM] + [ANYWHERE] * flips,
+        out_shape=bf16(*so_far.shape),
+        in_specs=[IN_SMEM] + [ANYWHERE] * flips + [IN_HBM],
         out_specs=IN_HBM,
         scratch_shapes=[
             pltpu.VMEM((flips, 2 * TILE, HEAD_DIM), jnp.bfloat16),
             pltpu.SemaphoreType.DMA((flips,)),
             pltpu.SemaphoreType.DMA((2 * flips,)),
         ],
+        input_output_aliases={1 + flips: 0},
         compiler_params=LEAVE_ROOM,
-    )(me, *blocks)
-
-
-def collect_whole_kernel(full, here, _, out, sems):
+    )(me, *blocks, so_far)
+
+
+def collect_whole_kernel(full, here, out, sems):
     stores = copy_list(sems)
     for device in range(here.shape[0]):
         for slot in range(full):
@@ -493,17 +496,16 @@
     wait_copies(stores)
 
 
-def collect_whole(full, here, so_far):
+def collect_whole(full, shape, here):
     return pl.pallas_call(
         functools.partial(collect_whole_kernel, full),
         name="collect_whole",
-        out_shape=bf16(*so_far.shape),
-        in_specs=[IN_VMEM, IN_HBM],
+        out_shape=bf16(*shape),
+        in_specs=[IN_VMEM],
         out_specs=IN_HBM,
         scratch_shapes=[pltpu.SemaphoreType.DMA((full * here.shape[0],))],
-        input_output_aliases={1: 0},
         compiler_params=LEAVE_ROOM,
-    )(here, so_far)
+    )(here)
 
 
 def with_all(blocks):
@@ -565,8 +567,8 @@
     even, odd = attend_shared(full, masks, shared, other)
     shared_back = join_columns(even, with_partner(odd, 1))
     shared_back = [with_partner(block, 2 * flip) for flip, block in enumerate(shared_back)]
-    so_far = collect_shared(full, queries.shape, me, shared_back)
-    return collect_whole(full, whole_back, so_far)
+    so_far = collect_whole(full, queries.shape, whole_back)
+    return collect_shared(full, me, shared_back, so_far)
 
 
 def paired_fits(mesh, key_tiles_shape):

time: 141 us -> 139 us (0.986)
  local copies, waits for them, and re-layouts: 9.14 us -> 3.64 us
  starting transfers between devices: 35.8 us -> 37.5 us
    unnamed x20 -> x10, local copies, waits for them, and re-layouts: 6.79 us -> 1.29 us
  transfers between devices with their start and end apart: 11 -> 11, of which waited for: 7 -> 6; matrix products, arithmetic and copies ran while one was open for 3% -> 3% of each run, Pallas kernels for 21% -> 21%
where the time goes in v5:
time: 139 us; the launch traced here: 138 us
  waiting for transfers between devices  60.7 us (44%)
  starting transfers between devices  37.5 us (27%)
  Pallas kernels  35.2 us (25%)
  local copies, waits for them, and re-layouts  3.64 us (3%)
    ppermute x8, waiting for transfers between devices, with_partner(): lax.ppermute(block, 'seq', [(i, i ^ 2 * k) for i in range(devices)])  55.7 us
    ppermute x8, starting transfers between devices, with_partner(): lax.ppermute(block, 'seq', [(i, i ^ 2 * k) for i in range(devices)])  22.6 us
    all_to_all x2, starting transfers between devices, with_all(): lax.all_to_all(blocks, 'seq', split_axis=0, concat_axis=0, tiled=True)  14.4 us
    pallas_call x1, Pallas kernels, attend_whole(): pl.pallas_call(functools.partial(attend_whole_kernel, full), name='attend...  13.6 us
    pallas_call x1, Pallas kernels, attend_shared(): pl.pallas_call(functools.partial(attend_shared_kernel, full), name='atten...  6.38 us
    pallas_call x1, Pallas kernels, prepare_whole(): pl.pallas_call(functools.partial(prepare_whole_kernel, full), name='prepa...  4.69 us
    pallas_call x1, Pallas kernels, prepare_shared(): pl.pallas_call(functools.partial(prepare_shared_kernel, full), name='prep...  3.63 us
    all_to_all x2, waiting for transfers between devices, with_all(): lax.all_to_all(blocks, 'seq', split_axis=0, concat_axis=0, tiled=True)  3.47 us
  transfers between devices with their start and end apart: 11, of which 6 were waited for; matrix products, arithmetic and copies ran while one was open for 3% of the time, Pallas kernels for 21%

profile of v5, /device:TPU:0, one launch (start us, length us, event | category | flops | bytes accessed | tf_op | source)
XLA Modules:
  0.0 138.4 jit_solution(1445337463889237323)
XLA Ops:
  0.0 4.7 %prepare_whole.1 = bf16[16,768,128]{2,1,0:T(8,128)(2,1)} custom-call(bf16[128,5120]{1,0:T(8,128)(2,1)} %refs_0_.2, bf16[128,5120]{1,0:T(8,128)(2,1)} %refs_1_.3, bf16[128,5120]{1,0:T(8,128)(2,1)} %refs_2_.3, f32[5120]{0:T(1024)} %refs_3_.3, f32[5120]{0:T(1024)} %refs_4_.3), custom_call_target="tpu_custom_call" | custom-call | tf_op jit(solution)/shard_map/prepare_whole/pallas_call | solution.py:243
  4.7 7.6 %all-to-all-start = ((bf16[16,768,128]{2,1,0:T(8,128)(2,1)}), bf16[16,768,128]{2,1,0:T(8,128)(2,1)}, u32[]{:S(2)}, u32[]{:S(2)}) async-start(bf16[16,768,128]{2,1,0:T(8,128)(2,1)} %prepare_whole.1), calls=%async_computation | async-start | bytes 6291456 | tf_op jit(solution)/shard_map/all_to_all | solution.py:512
  12.4 0.1 reshape.116
  12.6 0.2 copy.12
  12.8 0.6 gather_fusion
  13.4 0.5 gather_fusion.1
  13.9 0.2 select_reduce_fusion
  14.2 1.1 gather_fusion.2
  15.3 0.7 fusion.6.mask_ref
  16.0 3.6 %prepare_shared.1 = (bf16[4,384,128]{2,1,0:T(8,128)(2,1)}, bf16[4,384,128]{2,1,0:T(8,128)(2,1)}) custom-call(s32[1]{0:T(128)} %bitcast.me_ref, bf16[128,5120]{1,0:T(8,128)(2,1)} %refs_0_.2, bf16[128,5120]{1,0:T(8,128)(2,1)} %refs_1_.3, bf16[128,5120]{1,0:T(8,128)(2,1)} %refs_2_.3, f32[5120]{0:T(1024)} %refs_3_.3, f32[5120]{0:T(1024)} %refs_4_.3), custom_call_target="tpu_custom_call" | custom-call | tf_op jit(solution)/shard_map/prepare_shared/pallas_call | solution.py:255
  19.6 1.9 %collective-permute-start = (bf16[4,384,128]{2,1,0:T(8,128)(2,1)}, bf16[4,384,128]{2,1,0:T(8,128)(2,1)S(1)}, u32[]{:S(2)}, u32[]{:S(2)}) collective-permute-start(bf16[4,384,128]{2,1,0:T(8,128)(2,1)} %get-tuple-element.28), channel_id=1, source_target_pairs={{0,2},{1,3},{2,0},{3,1},{4,6},{5,7},{6,4},{7,5},{8,10},{9,11},{10,... | collective-permute-start | bytes 1179656 | tf_op jit(solution)/shard_map/ppermute | solution.py:517
  21.5 25.3 %collective-permute-done.other = bf16[4,384,128]{2,1,0:T(8,128)(2,1)S(1)} collective-permute-done((bf16[4,384,128]{2,1,0:T(8,128)(2,1)}, bf16[4,384,128]{2,1,0:T(8,128)(2,1)S(1)}, u32[]{:S(2)}, u32[]{:S(2)}) %collective-permute-start) | collective-permute-done | bytes 393248 | tf_op jit(solution)/shard_map/ppermute | solution.py:517
  46.8 1.0 copy-done
  47.8 2.3 %join_columns.2 = (bf16[768,128]{1,0:T(8,128)(2,1)S(1)}, bf16[768,128]{1,0:T(8,128)(2,1)S(1)}, bf16[768,128]{1,0:T(8,128)(2,1)S(1)}, bf16[768,128]{1,0:T(8,128)(2,1)S(1)}) custom-call(bf16[4,384,128]{2,1,0:T(8,128)(2,1)S(1)} %copy-done, bf16[4,384,128]{2,1,0:T(8,128)(2,1)S(1)} %collective-permute-done.other), custom_call_target="tpu_custom_call" | custom-call | tf_op jit(solution)/shard_map/join_columns/pallas_call | solution.py:282
  50.2 18.1 %collective-permute-done.1.refs_1_ = bf16[768,128]{1,0:T(8,128)(2,1)S(1)} collective-permute-done((bf16[768,128]{1,0:T(8,128)(2,1)S(1)}, bf16[768,128]{1,0:T(8,128)(2,1)S(1)}, u32[]{:S(2)}, u32[]{:S(2)}) %collective-permute-start.1) | collective-permute-done | bytes 196640 | tf_op jit(solution)/shard_map/ppermute | solution.py:517
  68.3 3.5 %all-to-all-done.here = bf16[16,768,128]{2,1,0:T(8,128)(2,1)} async-done(((bf16[16,768,128]{2,1,0:T(8,128)(2,1)}), bf16[16,768,128]{2,1,0:T(8,128)(2,1)}, u32[]{:S(2)}, u32[]{:S(2)}) %all-to-all-start) | async-done | bytes 3145760 | tf_op jit(solution)/shard_map/all_to_all | solution.py:512
  71.8 13.5 %collective-permute-start.2 = (bf16[768,128]{1,0:T(8,128)(2,1)S(1)}, bf16[768,128]{1,0:T(8,128)(2,1)S(1)}, u32[]{:S(2)}, u32[]{:S(2)}) collective-permute-start(bf16[768,128]{1,0:T(8,128)(2,1)S(1)} %get-tuple-element.34), channel_id=1, source_target_pairs={{0,8},{1,9},{2,10},{3,11},{4,12},{5,13},{6,14},{7,15},{8,0},{9,1},... | collective-permute-start | bytes 589832 | tf_op jit(solution)/shard_map/ppermute | solution.py:517
  85.3 13.6 %attend_whole.1 = bf16[16,256,128]{2,1,0:T(8,128)(2,1)} custom-call(s32[3,16]{1,0:T(4,128)} %fusion.6.mask_ref, bf16[16,768,128]{2,1,0:T(8,128)(2,1)} %all-to-all-done.here), custom_call_target="tpu_custom_call" | custom-call | tf_op jit(solution)/shard_map/attend_whole/pallas_call | solution.py:378
  98.9 6.9 %all-to-all-start.1 = ((bf16[16,256,128]{2,1,0:T(8,128)(2,1)}), bf16[16,256,128]{2,1,0:T(8,128)(2,1)S(1)}, u32[]{:S(2)}, u32[]{:S(2)}) async-start(bf16[16,256,128]{2,1,0:T(8,128)(2,1)} %attend_whole.1), calls=%async_computation.1 | async-start | bytes 2097152 | tf_op jit(solution)/shard_map/all_to_all | solution.py:512
  105.8 1.5 %join_keys_values.1 = bf16[8,256,128]{2,1,0:T(8,128)(2,1)S(1)} custom-call(bf16[768,128]{1,0:T(8,128)(2,1)S(1)} %get-tuple-element.36.refs_0_, bf16[768,128]{1,0:T(8,128)(2,1)S(1)} %collective-permute-done.1.refs_1_, bf16[768,128]{1,0:T(8,128)(2,1)S(1)} %collective-permute-done.2.refs_2_, bf16[768,128]{1,0:T(8,128)(2,1)S(1)} %collective-permute-done.3.refs_3_), custom_call_target="tpu_custom_call" | custom-call | tf_op jit(solution)/shard_map/join_keys_values/pallas_call | solution.py:446
  107.3 0.5 collective-permute-start.4
  107.8 1.5 %collective-permute-done.4.refs_4_ = bf16[8,256,128]{2,1,0:T(8,128)(2,1)S(1)} collective-permute-done((bf16[8,256,128]{2,1,0:T(8,128)(2,1)S(1)}, bf16[8,256,128]{2,1,0:T(8,128)(2,1)S(1)}, u32[]{:S(2)}, u32[]{:S(2)}) %collective-permute-start.4) | collective-permute-done | bytes 524320 | tf_op jit(solution)/shard_map/ppermute | solution.py:521
  109.4 6.4 %attend_shared.1 = (bf16[4,128,128]{2,1,0:T(8,128)(2,1)S(1)}, bf16[4,128,128]{2,1,0:T(8,128)(2,1)S(1)}) custom-call(s32[3,16]{1,0:T(4,128)S(1)} %copy-done.1, bf16[768,128]{1,0:T(8,128)(2,1)S(1)} %get-tuple-element.36.refs_0_, bf16[768,128]{1,0:T(8,128)(2,1)S(1)} %collective-permute-done.1.refs_1_, bf16[768,128]{1,0:T(8,128)(2,1)S(1)} %collective-permute-done.2.refs_2_, ...), custom_call_target="tpu_custom_call" | custom-call | tf_op jit(solution)/shard_map/attend_shared/pallas_call | solution.py:414
  115.7 2.0 %collective-permute-start.5 = (bf16[4,128,128]{2,1,0:T(8,128)(2,1)S(1)}, bf16[4,128,128]{2,1,0:T(8,128)(2,1)S(1)}, u32[]{:S(2)}, u32[]{:S(2)}) collective-permute-start(bf16[4,128,128]{2,1,0:T(8,128)(2,1)S(1)} %get-tuple-element.41), channel_id=1, source_target_pairs={{0,2},{1,3},{2,0},{3,1},{4,6},{5,7},{6,4},{7,5},{8,10},{9,11},{10,... | collective-permute-start | bytes 393224 | tf_op jit(solution)/shard_map/ppermute | solution.py:517
  117.7 5.6 %collective-permute-done.5.other = bf16[4,128,128]{2,1,0:T(8,128)(2,1)S(1)} collective-permute-done((bf16[4,128,128]{2,1,0:T(8,128)(2,1)S(1)}, bf16[4,128,128]{2,1,0:T(8,128)(2,1)S(1)}, u32[]{:S(2)}, u32[]{:S(2)}) %collective-permute-start.5) | collective-permute-done | bytes 131104 | tf_op jit(solution)/shard_map/ppermute | solution.py:517
  123.3 0.8 join_columns.3
  124.1 1.4 %collective-permute-start.6 = (bf16[256,128]{1,0:T(8,128)(2,1)S(1)}, bf16[256,128]{1,0:T(8,128)(2,1)S(1)}, u32[]{:S(2)}, u32[]{:S(2)}) collective-permute-start(bf16[256,128]{1,0:T(8,128)(2,1)S(1)} %get-tuple-element.43), channel_id=1, source_target_pairs={{0,4},{1,5},{2,6},{3,7},{4,0},{5,1},{6,2},{7,3},{8,12},{9,13},{10,... | collective-permute-start | bytes 196616 | tf_op jit(solution)/shard_map/ppermute | solution.py:517
  125.5 3.2 %collective-permute-start.7 = (bf16[256,128]{1,0:T(8,128)(2,1)S(1)}, bf16[256,128]{1,0:T(8,128)(2,1)S(1)}, u32[]{:S(2)}, u32[]{:S(2)}) collective-permute-start(bf16[256,128]{1,0:T(8,128)(2,1)S(1)} %get-tuple-element.44), channel_id=1, source_target_pairs={{0,8},{1,9},{2,10},{3,11},{4,12},{5,13},{6,14},{7,15},{8,0},{9,1},... | collective-permute-start | bytes 196616 | tf_op jit(solution)/shard_map/ppermute | solution.py:517
  128.7 0.4 collective-permute-start.8
  129.1 1.2 collect_whole.1.refs_4_
  130.4 6.7 %collective-permute-done.7.refs_2_ = bf16[256,128]{1,0:T(8,128)(2,1)S(1)} collective-permute-done((bf16[256,128]{1,0:T(8,128)(2,1)S(1)}, bf16[256,128]{1,0:T(8,128)(2,1)S(1)}, u32[]{:S(2)}, u32[]{:S(2)}) %collective-permute-start.7) | collective-permute-done | bytes 65568 | tf_op jit(solution)/shard_map/ppermute | solution.py:517
  137.1 1.1 collect_shared.1
  (20 shorter events, 0.4 us)
Async XLA Ops:
  4.7 7.8 %copy-start.3 = (s32[40,16]{0,1:T(8,128)S(1)}, s32[40,16]{0,1:T(8,128)}, u32[]{:S(2)}) copy-start(s32[40,16]{0,1:T(8,128)} %param.13) | copy-start | bytes 7684
  4.7 7.9 %copy-start.2 = (s32[40,16,16]{0,2,1:T(8,128)S(1)}, s32[40,16,16]{0,2,1:T(8,128)}, u32[]{:S(2)}) copy-start(s32[40,16,16]{0,2,1:T(8,128)} %param.12) | copy-start | bytes 122884
  4.7 67.0 %all-to-all-start = ((bf16[16,768,128]{2,1,0:T(8,128)(2,1)}), bf16[16,768,128]{2,1,0:T(8,128)(2,1)}, u32[]{:S(2)}, u32[]{:S(2)}) async-start(bf16[16,768,128]{2,1,0:T(8,128)(2,1)} %prepare_whole.1), calls=%async_computation | async-start | bytes 6291456 | tf_op jit(solution)/shard_map/all_to_all | solution.py:512
  19.6 27.2 %collective-permute-start = (bf16[4,384,128]{2,1,0:T(8,128)(2,1)}, bf16[4,384,128]{2,1,0:T(8,128)(2,1)S(1)}, u32[]{:S(2)}, u32[]{:S(2)}) collective-permute-start(bf16[4,384,128]{2,1,0:T(8,128)(2,1)} %get-tuple-element.28), channel_id=1, source_target_pairs={{0,2},{1,3},{2,0},{3,1},{4,6},{5,7},{6,4},{7,5},{8,10},{9,11},{10,... | collective-permute-start | bytes 1179656 | tf_op jit(solution)/shard_map/ppermute | solution.py:517
  46.8 1.0 copy-start
  50.1 18.2 %collective-permute-start.1 = (bf16[768,128]{1,0:T(8,128)(2,1)S(1)}, bf16[768,128]{1,0:T(8,128)(2,1)S(1)}, u32[]{:S(2)}, u32[]{:S(2)}) collective-permute-start(bf16[768,128]{1,0:T(8,128)(2,1)S(1)} %get-tuple-element.30), channel_id=1, source_target_pairs={{0,4},{1,5},{2,6},{3,7},{4,0},{5,1},{6,2},{7,3},{8,12},{9,13},{10,... | collective-permute-start | bytes 589832 | tf_op jit(solution)/shard_map/ppermute | solution.py:517
  71.8 27.1 %collective-permute-start.2 = (bf16[768,128]{1,0:T(8,128)(2,1)S(1)}, bf16[768,128]{1,0:T(8,128)(2,1)S(1)}, u32[]{:S(2)}, u32[]{:S(2)}) collective-permute-start(bf16[768,128]{1,0:T(8,128)(2,1)S(1)} %get-tuple-element.34), channel_id=1, source_target_pairs={{0,8},{1,9},{2,10},{3,11},{4,12},{5,13},{6,14},{7,15},{8,0},{9,1},... | collective-permute-start | bytes 589832 | tf_op jit(solution)/shard_map/ppermute | solution.py:517
  85.3 13.6 %collective-permute-start.3 = (bf16[768,128]{1,0:T(8,128)(2,1)S(1)}, bf16[768,128]{1,0:T(8,128)(2,1)S(1)}, u32[]{:S(2)}, u32[]{:S(2)}) collective-permute-start(bf16[768,128]{1,0:T(8,128)(2,1)S(1)} %get-tuple-element.35), channel_id=1, source_target_pairs={{0,12},{1,13},{2,14},{3,15},{4,8},{5,9},{6,10},{7,11},{8,4},{9,5},... | collective-permute-start | bytes 589832 | tf_op jit(solution)/shard_map/ppermute | solution.py:517
  98.9 10.4 %copy-start.1 = (s32[3,16]{1,0:T(4,128)S(1)}, s32[3,16]{1,0:T(4,128)}, u32[]{:S(2)}) copy-start(s32[3,16]{1,0:T(4,128)} %fusion.6.mask_ref) | copy-start | bytes 580
  98.9 30.2 %all-to-all-start.1 = ((bf16[16,256,128]{2,1,0:T(8,128)(2,1)}), bf16[16,256,128]{2,1,0:T(8,128)(2,1)S(1)}, u32[]{:S(2)}, u32[]{:S(2)}) async-start(bf16[16,256,128]{2,1,0:T(8,128)(2,1)} %attend_whole.1), calls=%async_computation.1 | async-start | bytes 2097152 | tf_op jit(solution)/shard_map/all_to_all | solution.py:512
  107.3 2.0 %collective-permute-start.4 = (bf16[8,256,128]{2,1,0:T(8,128)(2,1)S(1)}, bf16[8,256,128]{2,1,0:T(8,128)(2,1)S(1)}, u32[]{:S(2)}, u32[]{:S(2)}) collective-permute-start(bf16[8,256,128]{2,1,0:T(8,128)(2,1)S(1)} %join_keys_values.1), channel_id=1, source_target_pairs={{0,1},{1,0},{2,3},{3,2},{4,5},{5,4},{6,7},{7,6},{8,9},{9,8},{10,11... | collective-permute-start | bytes 1572872 | tf_op jit(solution)/shard_map/ppermute | solution.py:521
  115.7 7.5 %collective-permute-start.5 = (bf16[4,128,128]{2,1,0:T(8,128)(2,1)S(1)}, bf16[4,128,128]{2,1,0:T(8,128)(2,1)S(1)}, u32[]{:S(2)}, u32[]{:S(2)}) collective-permute-start(bf16[4,128,128]{2,1,0:T(8,128)(2,1)S(1)} %get-tuple-element.41), channel_id=1, source_target_pairs={{0,2},{1,3},{2,0},{3,1},{4,6},{5,7},{6,4},{7,5},{8,10},{9,11},{10,... | collective-permute-start | bytes 393224 | tf_op jit(solution)/shard_map/ppermute | solution.py:517
  124.1 6.3 %collective-permute-start.6 = (bf16[256,128]{1,0:T(8,128)(2,1)S(1)}, bf16[256,128]{1,0:T(8,128)(2,1)S(1)}, u32[]{:S(2)}, u32[]{:S(2)}) collective-permute-start(bf16[256,128]{1,0:T(8,128)(2,1)S(1)} %get-tuple-element.43), channel_id=1, source_target_pairs={{0,4},{1,5},{2,6},{3,7},{4,0},{5,1},{6,2},{7,3},{8,12},{9,13},{10,... | collective-permute-start | bytes 196616 | tf_op jit(solution)/shard_map/ppermute | solution.py:517
  125.5 11.6 %collective-permute-start.7 = (bf16[256,128]{1,0:T(8,128)(2,1)S(1)}, bf16[256,128]{1,0:T(8,128)(2,1)S(1)}, u32[]{:S(2)}, u32[]{:S(2)}) collective-permute-start(bf16[256,128]{1,0:T(8,128)(2,1)S(1)} %get-tuple-element.44), channel_id=1, source_target_pairs={{0,8},{1,9},{2,10},{3,11},{4,12},{5,13},{6,14},{7,15},{8,0},{9,1},... | collective-permute-start | bytes 196616 | tf_op jit(solution)/shard_map/ppermute | solution.py:517
  128.7 8.3 %collective-permute-start.8 = (bf16[256,128]{1,0:T(8,128)(2,1)S(1)}, bf16[256,128]{1,0:T(8,128)(2,1)S(1)}, u32[]{:S(2)}, u32[]{:S(2)}) collective-permute-start(bf16[256,128]{1,0:T(8,128)(2,1)S(1)} %get-tuple-element.45), channel_id=1, source_target_pairs={{0,12},{1,13},{2,14},{3,15},{4,8},{5,9},{6,10},{7,11},{8,4},{9,5},... | collective-permute-start | bytes 196616 | tf_op jit(solution)/shard_map/ppermute | solution.py:517

commit v6 on v5

--- a/solution.py
+++ b/solution.py
@@ -336,7 +336,7 @@
     ]
 
 
-def attend_slot(mask_ref, slot, here, first, out, out_first, stride, together, marked):
+def attend_slot(mask_ref, slot, here, first, out, out_first, stride, together, marked, stored):
     def part(tile, tensor):
         return here[tile, first + tensor * TILE : first + (tensor + 1) * TILE]
 
@@ -354,9 +354,11 @@
             blocks = attend_rows([part(tile, 0) for tile in tiles], marked[...], values, masks)
             for tile, block in zip(tiles, blocks):
                 out[tile, out_first : out_first + TILE] = block
+            stored(at)
         return carry
 
-    lax.fori_loop(0, products // unroll, step, 0)
+    for index in range(products // unroll):
+        step(index, 0)
 
 
 def marked_keys(devices):
@@ -367,9 +369,13 @@
     stores = copy_list(sems)
     write_marks(marked)
     for slot in range(full):
-        attend_slot(mask_ref, slot, here, 3 * slot * TILE, out, slot * TILE, 1, 4, marked)
         rows = pl.ds(slot * TILE, TILE)
-        start_copy(stores, out.at[:, rows], outs.at[:, rows])
+
+        def stored(tile, rows=rows):
+            tiles = pl.ds(tile, 4)
+            start_copy(stores, out.at[tiles, rows], outs.at[tiles, rows])
+
+        attend_slot(mask_ref, slot, here, 3 * slot * TILE, out, slot * TILE, 1, 4, marked, stored)
     wait_copies(stores)
 
 
@@ -384,7 +390,7 @@
         scratch_shapes=[
             pltpu.VMEM(shape, jnp.bfloat16),
             marked_keys(here.shape[0]),
-            pltpu.SemaphoreType.DMA((full,)),
+            pltpu.SemaphoreType.DMA((full * here.shape[0] // 4,)),
         ],
         compiler_params=PARAMS,
     )(masks, here)
@@ -402,7 +408,7 @@
             start_copy(loads, other.at[partner], target)
     write_marks(marked)
     wait_copies(loads)
-    attend_slot(mask_ref, full, here, 0, out, 0, 2, 2, marked)
+    attend_slot(mask_ref, full, here, 0, out, 0, 2, 2, marked, lambda tile: None)
     for flip in range(len(blocks)):
         for odd in range(2):
             start_copy(stores, out.at[2 * (2 * flip + odd)], outs[odd].at[flip])

time: 139 us -> 139 us (level)
  no operation moved by 1% of the time
where the time goes in v6:
time: 139 us; the launch traced here: 138 us
  waiting for transfers between devices  60.7 us (44%)
  starting transfers between devices  37.6 us (27%)
  Pallas kernels  35.1 us (25%)
  local copies, waits for them, and re-layouts  3.64 us (3%)
    ppermute x8, waiting for transfers between devices, with_partner(): lax.ppermute(block, 'seq', [(i, i ^ 2 * k) for i in range(devices)])  55.7 us
    ppermute x8, starting transfers between devices, with_partner(): lax.ppermute(block, 'seq', [(i, i ^ 2 * k) for i in range(devices)])  22.6 us
    all_to_all x2, starting transfers between devices, with_all(): lax.all_to_all(blocks, 'seq', split_axis=0, concat_axis=0, tiled=True)  14.5 us
    pallas_call x1, Pallas kernels, attend_whole(): pl.pallas_call(functools.partial(attend_whole_kernel, full), name='attend...  13.5 us
    pallas_call x1, Pallas kernels, attend_shared(): pl.pallas_call(functools.partial(attend_shared_kernel, full), name='atten...  6.38 us
    pallas_call x1, Pallas kernels, prepare_whole(): pl.pallas_call(functools.partial(prepare_whole_kernel, full), name='prepa...  4.69 us
    pallas_call x1, Pallas kernels, prepare_shared(): pl.pallas_call(functools.partial(prepare_shared_kernel, full), name='prep...  3.63 us
    all_to_all x2, waiting for transfers between devices, with_all(): lax.all_to_all(blocks, 'seq', split_axis=0, concat_axis=0, tiled=True)  3.47 us
  transfers between devices with their start and end apart: 11, of which 6 were waited for; matrix products, arithmetic and copies ran while one was open for 3% of the time, Pallas kernels for 21%

profile of v6, /device:TPU:0, one launch (start us, length us, event | category | flops | bytes accessed | tf_op | source)
XLA Modules:
  0.0 138.4 jit_solution(12540794800337102860)
XLA Ops:
  0.0 4.7 %prepare_whole.1 = bf16[16,768,128]{2,1,0:T(8,128)(2,1)} custom-call(bf16[128,5120]{1,0:T(8,128)(2,1)} %refs_0_.2, bf16[128,5120]{1,0:T(8,128)(2,1)} %refs_1_.3, bf16[128,5120]{1,0:T(8,128)(2,1)} %refs_2_.3, f32[5120]{0:T(1024)} %refs_3_.3, f32[5120]{0:T(1024)} %refs_4_.3), custom_call_target="tpu_custom_call" | custom-call | tf_op jit(solution)/shard_map/prepare_whole/pallas_call | solution.py:243
  4.7 7.6 %all-to-all-start = ((bf16[16,768,128]{2,1,0:T(8,128)(2,1)}), bf16[16,768,128]{2,1,0:T(8,128)(2,1)}, u32[]{:S(2)}, u32[]{:S(2)}) async-start(bf16[16,768,128]{2,1,0:T(8,128)(2,1)} %prepare_whole.1), calls=%async_computation | async-start | bytes 6291456 | tf_op jit(solution)/shard_map/all_to_all | solution.py:518
  12.4 0.1 reshape.116
  12.6 0.2 copy.12
  12.8 0.6 gather_fusion
  13.4 0.5 gather_fusion.1
  13.9 0.2 select_reduce_fusion
  14.2 1.1 gather_fusion.2
  15.3 0.7 fusion.6.mask_ref
  16.0 3.6 %prepare_shared.1 = (bf16[4,384,128]{2,1,0:T(8,128)(2,1)}, bf16[4,384,128]{2,1,0:T(8,128)(2,1)}) custom-call(s32[1]{0:T(128)} %bitcast.me_ref, bf16[128,5120]{1,0:T(8,128)(2,1)} %refs_0_.2, bf16[128,5120]{1,0:T(8,128)(2,1)} %refs_1_.3, bf16[128,5120]{1,0:T(8,128)(2,1)} %refs_2_.3, f32[5120]{0:T(1024)} %refs_3_.3, f32[5120]{0:T(1024)} %refs_4_.3), custom_call_target="tpu_custom_call" | custom-call | tf_op jit(solution)/shard_map/prepare_shared/pallas_call | solution.py:255
  19.6 1.9 %collective-permute-start = (bf16[4,384,128]{2,1,0:T(8,128)(2,1)}, bf16[4,384,128]{2,1,0:T(8,128)(2,1)S(1)}, u32[]{:S(2)}, u32[]{:S(2)}) collective-permute-start(bf16[4,384,128]{2,1,0:T(8,128)(2,1)} %get-tuple-element.28), channel_id=1, source_target_pairs={{0,2},{1,3},{2,0},{3,1},{4,6},{5,7},{6,4},{7,5},{8,10},{9,11},{10,... | collective-permute-start | bytes 1179656 | tf_op jit(solution)/shard_map/ppermute | solution.py:523
  21.5 25.3 %collective-permute-done.other = bf16[4,384,128]{2,1,0:T(8,128)(2,1)S(1)} collective-permute-done((bf16[4,384,128]{2,1,0:T(8,128)(2,1)}, bf16[4,384,128]{2,1,0:T(8,128)(2,1)S(1)}, u32[]{:S(2)}, u32[]{:S(2)}) %collective-permute-start) | collective-permute-done | bytes 393248 | tf_op jit(solution)/shard_map/ppermute | solution.py:523
  46.8 1.0 copy-done
  47.8 2.3 %join_columns.2 = (bf16[768,128]{1,0:T(8,128)(2,1)S(1)}, bf16[768,128]{1,0:T(8,128)(2,1)S(1)}, bf16[768,128]{1,0:T(8,128)(2,1)S(1)}, bf16[768,128]{1,0:T(8,128)(2,1)S(1)}) custom-call(bf16[4,384,128]{2,1,0:T(8,128)(2,1)S(1)} %copy-done, bf16[4,384,128]{2,1,0:T(8,128)(2,1)S(1)} %collective-permute-done.other), custom_call_target="tpu_custom_call" | custom-call | tf_op jit(solution)/shard_map/join_columns/pallas_call | solution.py:282
  50.2 18.1 %collective-permute-done.1.refs_1_ = bf16[768,128]{1,0:T(8,128)(2,1)S(1)} collective-permute-done((bf16[768,128]{1,0:T(8,128)(2,1)S(1)}, bf16[768,128]{1,0:T(8,128)(2,1)S(1)}, u32[]{:S(2)}, u32[]{:S(2)}) %collective-permute-start.1) | collective-permute-done | bytes 196640 | tf_op jit(solution)/shard_map/ppermute | solution.py:523
  68.3 3.5 %all-to-all-done.here = bf16[16,768,128]{2,1,0:T(8,128)(2,1)} async-done(((bf16[16,768,128]{2,1,0:T(8,128)(2,1)}), bf16[16,768,128]{2,1,0:T(8,128)(2,1)}, u32[]{:S(2)}, u32[]{:S(2)}) %all-to-all-start) | async-done | bytes 3145760 | tf_op jit(solution)/shard_map/all_to_all | solution.py:518
  71.8 13.5 %collective-permute-start.2 = (bf16[768,128]{1,0:T(8,128)(2,1)S(1)}, bf16[768,128]{1,0:T(8,128)(2,1)S(1)}, u32[]{:S(2)}, u32[]{:S(2)}) collective-permute-start(bf16[768,128]{1,0:T(8,128)(2,1)S(1)} %get-tuple-element.34), channel_id=1, source_target_pairs={{0,8},{1,9},{2,10},{3,11},{4,12},{5,13},{6,14},{7,15},{8,0},{9,1},... | collective-permute-start | bytes 589832 | tf_op jit(solution)/shard_map/ppermute | solution.py:523
  85.3 13.5 %attend_whole.1 = bf16[16,256,128]{2,1,0:T(8,128)(2,1)} custom-call(s32[3,16]{1,0:T(4,128)} %fusion.6.mask_ref, bf16[16,768,128]{2,1,0:T(8,128)(2,1)} %all-to-all-done.here), custom_call_target="tpu_custom_call" | custom-call | tf_op jit(solution)/shard_map/attend_whole/pallas_call | solution.py:384
  98.9 7.0 %all-to-all-start.1 = ((bf16[16,256,128]{2,1,0:T(8,128)(2,1)}), bf16[16,256,128]{2,1,0:T(8,128)(2,1)S(1)}, u32[]{:S(2)}, u32[]{:S(2)}) async-start(bf16[16,256,128]{2,1,0:T(8,128)(2,1)} %attend_whole.1), calls=%async_computation.1 | async-start | bytes 2097152 | tf_op jit(solution)/shard_map/all_to_all | solution.py:518
  105.8 1.5 %join_keys_values.1 = bf16[8,256,128]{2,1,0:T(8,128)(2,1)S(1)} custom-call(bf16[768,128]{1,0:T(8,128)(2,1)S(1)} %get-tuple-element.36.refs_0_, bf16[768,128]{1,0:T(8,128)(2,1)S(1)} %collective-permute-done.1.refs_1_, bf16[768,128]{1,0:T(8,128)(2,1)S(1)} %collective-permute-done.2.refs_2_, bf16[768,128]{1,0:T(8,128)(2,1)S(1)} %collective-permute-done.3.refs_3_), custom_call_target="tpu_custom_call" | custom-call | tf_op jit(solution)/shard_map/join_keys_values/pallas_call | solution.py:452
  107.3 0.5 collective-permute-start.4
  107.8 1.5 %collective-permute-done.4.refs_4_ = bf16[8,256,128]{2,1,0:T(8,128)(2,1)S(1)} collective-permute-done((bf16[8,256,128]{2,1,0:T(8,128)(2,1)S(1)}, bf16[8,256,128]{2,1,0:T(8,128)(2,1)S(1)}, u32[]{:S(2)}, u32[]{:S(2)}) %collective-permute-start.4) | collective-permute-done | bytes 524320 | tf_op jit(solution)/shard_map/ppermute | solution.py:527
  109.4 6.4 %attend_shared.1 = (bf16[4,128,128]{2,1,0:T(8,128)(2,1)S(1)}, bf16[4,128,128]{2,1,0:T(8,128)(2,1)S(1)}) custom-call(s32[3,16]{1,0:T(4,128)S(1)} %copy-done.1, bf16[768,128]{1,0:T(8,128)(2,1)S(1)} %get-tuple-element.36.refs_0_, bf16[768,128]{1,0:T(8,128)(2,1)S(1)} %collective-permute-done.1.refs_1_, bf16[768,128]{1,0:T(8,128)(2,1)S(1)} %collective-permute-done.2.refs_2_, ...), custom_call_target="tpu_custom_call" | custom-call | tf_op jit(solution)/shard_map/attend_shared/pallas_call | solution.py:420
  115.7 2.0 %collective-permute-start.5 = (bf16[4,128,128]{2,1,0:T(8,128)(2,1)S(1)}, bf16[4,128,128]{2,1,0:T(8,128)(2,1)S(1)}, u32[]{:S(2)}, u32[]{:S(2)}) collective-permute-start(bf16[4,128,128]{2,1,0:T(8,128)(2,1)S(1)} %get-tuple-element.41), channel_id=1, source_target_pairs={{0,2},{1,3},{2,0},{3,1},{4,6},{5,7},{6,4},{7,5},{8,10},{9,11},{10,... | collective-permute-start | bytes 393224 | tf_op jit(solution)/shard_map/ppermute | solution.py:523
  117.7 5.6 %collective-permute-done.5.other = bf16[4,128,128]{2,1,0:T(8,128)(2,1)S(1)} collective-permute-done((bf16[4,128,128]{2,1,0:T(8,128)(2,1)S(1)}, bf16[4,128,128]{2,1,0:T(8,128)(2,1)S(1)}, u32[]{:S(2)}, u32[]{:S(2)}) %collective-permute-start.5) | collective-permute-done | bytes 131104 | tf_op jit(solution)/shard_map/ppermute | solution.py:523
  123.3 0.8 join_columns.3
  124.1 1.4 %collective-permute-start.6 = (bf16[256,128]{1,0:T(8,128)(2,1)S(1)}, bf16[256,128]{1,0:T(8,128)(2,1)S(1)}, u32[]{:S(2)}, u32[]{:S(2)}) collective-permute-start(bf16[256,128]{1,0:T(8,128)(2,1)S(1)} %get-tuple-element.43), channel_id=1, source_target_pairs={{0,4},{1,5},{2,6},{3,7},{4,0},{5,1},{6,2},{7,3},{8,12},{9,13},{10,... | collective-permute-start | bytes 196616 | tf_op jit(solution)/shard_map/ppermute | solution.py:523
  125.5 3.2 %collective-permute-start.7 = (bf16[256,128]{1,0:T(8,128)(2,1)S(1)}, bf16[256,128]{1,0:T(8,128)(2,1)S(1)}, u32[]{:S(2)}, u32[]{:S(2)}) collective-permute-start(bf16[256,128]{1,0:T(8,128)(2,1)S(1)} %get-tuple-element.44), channel_id=1, source_target_pairs={{0,8},{1,9},{2,10},{3,11},{4,12},{5,13},{6,14},{7,15},{8,0},{9,1},... | collective-permute-start | bytes 196616 | tf_op jit(solution)/shard_map/ppermute | solution.py:523
  128.7 0.4 collective-permute-start.8
  129.1 1.2 collect_whole.1.refs_4_
  130.4 6.7 %collective-permute-done.7.refs_2_ = bf16[256,128]{1,0:T(8,128)(2,1)S(1)} collective-permute-done((bf16[256,128]{1,0:T(8,128)(2,1)S(1)}, bf16[256,128]{1,0:T(8,128)(2,1)S(1)}, u32[]{:S(2)}, u32[]{:S(2)}) %collective-permute-start.7) | collective-permute-done | bytes 65568 | tf_op jit(solution)/shard_map/ppermute | solution.py:523
  137.1 1.1 collect_shared.1
  (20 shorter events, 0.4 us)
Async XLA Ops:
  4.7 7.8 %copy-start.3 = (s32[40,16]{0,1:T(8,128)S(1)}, s32[40,16]{0,1:T(8,128)}, u32[]{:S(2)}) copy-start(s32[40,16]{0,1:T(8,128)} %param.13) | copy-start | bytes 7684
  4.7 7.9 %copy-start.2 = (s32[40,16,16]{0,2,1:T(8,128)S(1)}, s32[40,16,16]{0,2,1:T(8,128)}, u32[]{:S(2)}) copy-start(s32[40,16,16]{0,2,1:T(8,128)} %param.12) | copy-start | bytes 122884
  4.7 67.0 %all-to-all-start = ((bf16[16,768,128]{2,1,0:T(8,128)(2,1)}), bf16[16,768,128]{2,1,0:T(8,128)(2,1)}, u32[]{:S(2)}, u32[]{:S(2)}) async-start(bf16[16,768,128]{2,1,0:T(8,128)(2,1)} %prepare_whole.1), calls=%async_computation | async-start | bytes 6291456 | tf_op jit(solution)/shard_map/all_to_all | solution.py:518
  19.6 27.2 %collective-permute-start = (bf16[4,384,128]{2,1,0:T(8,128)(2,1)}, bf16[4,384,128]{2,1,0:T(8,128)(2,1)S(1)}, u32[]{:S(2)}, u32[]{:S(2)}) collective-permute-start(bf16[4,384,128]{2,1,0:T(8,128)(2,1)} %get-tuple-element.28), channel_id=1, source_target_pairs={{0,2},{1,3},{2,0},{3,1},{4,6},{5,7},{6,4},{7,5},{8,10},{9,11},{10,... | collective-permute-start | bytes 1179656 | tf_op jit(solution)/shard_map/ppermute | solution.py:523
  46.8 1.0 copy-start
  50.1 18.2 %collective-permute-start.1 = (bf16[768,128]{1,0:T(8,128)(2,1)S(1)}, bf16[768,128]{1,0:T(8,128)(2,1)S(1)}, u32[]{:S(2)}, u32[]{:S(2)}) collective-permute-start(bf16[768,128]{1,0:T(8,128)(2,1)S(1)} %get-tuple-element.30), channel_id=1, source_target_pairs={{0,4},{1,5},{2,6},{3,7},{4,0},{5,1},{6,2},{7,3},{8,12},{9,13},{10,... | collective-permute-start | bytes 589832 | tf_op jit(solution)/shard_map/ppermute | solution.py:523
  71.8 27.1 %collective-permute-start.2 = (bf16[768,128]{1,0:T(8,128)(2,1)S(1)}, bf16[768,128]{1,0:T(8,128)(2,1)S(1)}, u32[]{:S(2)}, u32[]{:S(2)}) collective-permute-start(bf16[768,128]{1,0:T(8,128)(2,1)S(1)} %get-tuple-element.34), channel_id=1, source_target_pairs={{0,8},{1,9},{2,10},{3,11},{4,12},{5,13},{6,14},{7,15},{8,0},{9,1},... | collective-permute-start | bytes 589832 | tf_op jit(solution)/shard_map/ppermute | solution.py:523
  85.3 13.5 %collective-permute-start.3 = (bf16[768,128]{1,0:T(8,128)(2,1)S(1)}, bf16[768,128]{1,0:T(8,128)(2,1)S(1)}, u32[]{:S(2)}, u32[]{:S(2)}) collective-permute-start(bf16[768,128]{1,0:T(8,128)(2,1)S(1)} %get-tuple-element.35), channel_id=1, source_target_pairs={{0,12},{1,13},{2,14},{3,15},{4,8},{5,9},{6,10},{7,11},{8,4},{9,5},... | collective-permute-start | bytes 589832 | tf_op jit(solution)/shard_map/ppermute | solution.py:523
  98.8 10.5 %copy-start.1 = (s32[3,16]{1,0:T(4,128)S(1)}, s32[3,16]{1,0:T(4,128)}, u32[]{:S(2)}) copy-start(s32[3,16]{1,0:T(4,128)} %fusion.6.mask_ref) | copy-start | bytes 580
  98.9 30.3 %all-to-all-start.1 = ((bf16[16,256,128]{2,1,0:T(8,128)(2,1)}), bf16[16,256,128]{2,1,0:T(8,128)(2,1)S(1)}, u32[]{:S(2)}, u32[]{:S(2)}) async-start(bf16[16,256,128]{2,1,0:T(8,128)(2,1)} %attend_whole.1), calls=%async_computation.1 | async-start | bytes 2097152 | tf_op jit(solution)/shard_map/all_to_all | solution.py:518
  107.3 2.0 %collective-permute-start.4 = (bf16[8,256,128]{2,1,0:T(8,128)(2,1)S(1)}, bf16[8,256,128]{2,1,0:T(8,128)(2,1)S(1)}, u32[]{:S(2)}, u32[]{:S(2)}) collective-permute-start(bf16[8,256,128]{2,1,0:T(8,128)(2,1)S(1)} %join_keys_values.1), channel_id=1, source_target_pairs={{0,1},{1,0},{2,3},{3,2},{4,5},{5,4},{6,7},{7,6},{8,9},{9,8},{10,11... | collective-permute-start | bytes 1572872 | tf_op jit(solution)/shard_map/ppermute | solution.py:527
  115.7 7.5 %collective-permute-start.5 = (bf16[4,128,128]{2,1,0:T(8,128)(2,1)S(1)}, bf16[4,128,128]{2,1,0:T(8,128)(2,1)S(1)}, u32[]{:S(2)}, u32[]{:S(2)}) collective-permute-start(bf16[4,128,128]{2,1,0:T(8,128)(2,1)S(1)} %get-tuple-element.41), channel_id=1, source_target_pairs={{0,2},{1,3},{2,0},{3,1},{4,6},{5,7},{6,4},{7,5},{8,10},{9,11},{10,... | collective-permute-start | bytes 393224 | tf_op jit(solution)/shard_map/ppermute | solution.py:523
  124.1 6.3 %collective-permute-start.6 = (bf16[256,128]{1,0:T(8,128)(2,1)S(1)}, bf16[256,128]{1,0:T(8,128)(2,1)S(1)}, u32[]{:S(2)}, u32[]{:S(2)}) collective-permute-start(bf16[256,128]{1,0:T(8,128)(2,1)S(1)} %get-tuple-element.43), channel_id=1, source_target_pairs={{0,4},{1,5},{2,6},{3,7},{4,0},{5,1},{6,2},{7,3},{8,12},{9,13},{10,... | collective-permute-start | bytes 196616 | tf_op jit(solution)/shard_map/ppermute | solution.py:523
  125.5 11.6 %collective-permute-start.7 = (bf16[256,128]{1,0:T(8,128)(2,1)S(1)}, bf16[256,128]{1,0:T(8,128)(2,1)S(1)}, u32[]{:S(2)}, u32[]{:S(2)}) collective-permute-start(bf16[256,128]{1,0:T(8,128)(2,1)S(1)} %get-tuple-element.44), channel_id=1, source_target_pairs={{0,8},{1,9},{2,10},{3,11},{4,12},{5,13},{6,14},{7,15},{8,0},{9,1},... | collective-permute-start | bytes 196616 | tf_op jit(solution)/shard_map/ppermute | solution.py:523
  128.7 8.3 %collective-permute-start.8 = (bf16[256,128]{1,0:T(8,128)(2,1)S(1)}, bf16[256,128]{1,0:T(8,128)(2,1)S(1)}, u32[]{:S(2)}, u32[]{:S(2)}) collective-permute-start(bf16[256,128]{1,0:T(8,128)(2,1)S(1)} %get-tuple-element.45), channel_id=1, source_target_pairs={{0,12},{1,13},{2,14},{3,15},{4,8},{5,9},{6,10},{7,11},{8,4},{9,5},... | collective-permute-start | bytes 196616 | tf_op jit(solution)/shard_map/ppermute | solution.py:523

commit v7 on v6

--- a/solution.py
+++ b/solution.py
@@ -336,7 +336,7 @@
     ]
 
 
-def attend_slot(mask_ref, slot, here, first, out, out_first, stride, together, marked, stored):
+def attend_slot(mask_ref, slot, here, first, out, out_first, start, stride, together, marked, stored):
     def part(tile, tensor):
         return here[tile, first + tensor * TILE : first + (tensor + 1) * TILE]
 
@@ -348,7 +348,7 @@
     def step(index, carry):
         for product in range(unroll):
             at = (index * unroll + product) * together
-            tiles = [(at + i) * stride for i in range(together)]
+            tiles = [start + (at + i) * stride for i in range(together)]
             values = part(slice(None), 2).reshape(-1, HEAD_DIM)
             masks = [mask_ref[slot, tile] for tile in tiles]
             blocks = attend_rows([part(tile, 0) for tile in tiles], marked[...], values, masks)
@@ -375,7 +375,7 @@
             tiles = pl.ds(tile, 4)
             start_copy(stores, out.at[tiles, rows], outs.at[tiles, rows])
 
-        attend_slot(mask_ref, slot, here, 3 * slot * TILE, out, slot * TILE, 1, 4, marked, stored)
+        attend_slot(mask_ref, slot, here, 3 * slot * TILE, out, slot * TILE, 0, 1, 4, marked, stored)
     wait_copies(stores)
 
 
@@ -396,39 +396,38 @@
     )(masks, here)
 
 
-def attend_shared_kernel(full, mask_ref, *refs):
-    blocks, (other, *outs), scratch = refs[:-8], refs[-8:-5], refs[-5:]
+def attend_shared_kernel(full, odd, mask_ref, *refs):
+    blocks, (other, outs), scratch = refs[:-7], refs[-7:-5], refs[-5:]
     here, out, marked, in_sems, out_sems = scratch
     loads, stores = copy_list(in_sems), copy_list(out_sems)
     for flip, block in enumerate(blocks):
-        for odd in range(2):
-            partner = 2 * flip + odd
-            start_copy(loads, block.at[pl.ds(3 * odd * TILE, 3 * TILE)], here.at[2 * partner])
+        for second in range(2):
+            partner = 2 * flip + second
+            start_copy(loads, block.at[pl.ds(3 * second * TILE, 3 * TILE)], here.at[2 * partner])
             target = here.at[2 * partner + 1, pl.ds(TILE, 2 * TILE)]
             start_copy(loads, other.at[partner], target)
     write_marks(marked)
     wait_copies(loads)
-    attend_slot(mask_ref, full, here, 0, out, 0, 2, 2, marked, lambda tile: None)
+    attend_slot(mask_ref, full, here, 0, out, 0, 2 * odd, 4, 4, marked, lambda tile: None)
     for flip in range(len(blocks)):
-        for odd in range(2):
-            start_copy(stores, out.at[2 * (2 * flip + odd)], outs[odd].at[flip])
+        start_copy(stores, out.at[2 * (2 * flip + odd)], outs.at[flip])
     wait_copies(stores)
 
 
-def attend_shared(full, masks, blocks, other):
+def attend_shared(full, odd, masks, blocks, other):
     flips = len(blocks)
     return pl.pallas_call(
-        functools.partial(attend_shared_kernel, full),
+        functools.partial(attend_shared_kernel, full, odd),
         name="attend_shared",
-        out_shape=[bf16(flips, TILE, HEAD_DIM)] * 2,
+        out_shape=bf16(flips, TILE, HEAD_DIM),
         in_specs=[IN_SMEM] + [ANYWHERE] * (flips + 1),
-        out_specs=[ANYWHERE] * 2,
+        out_specs=ANYWHERE,
         scratch_shapes=[
             pltpu.VMEM((4 * flips, 3 * TILE, HEAD_DIM), jnp.bfloat16),
             pltpu.VMEM((4 * flips, TILE, HEAD_DIM), jnp.bfloat16),
             marked_keys(4 * flips),
             pltpu.SemaphoreType.DMA((4 * flips,)),
-            pltpu.SemaphoreType.DMA((2 * flips,)),
+            pltpu.SemaphoreType.DMA((flips,)),
         ],
         compiler_params=LEAVE_ROOM,
     )(masks, *blocks, other)
@@ -570,7 +569,8 @@
     shared = all_after(near + far, whole_out)
     whole_back = with_all(after(whole_out, *shared))
     other = with_sibling(join_keys_values(shared))
-    even, odd = attend_shared(full, masks, shared, other)
+    odd = attend_shared(full, 1, masks, shared, other)
+    even = attend_shared(full, 0, masks, shared, after(other, odd))
     shared_back = join_columns(even, with_partner(odd, 1))
     shared_back = [with_partner(block, 2 * flip) for flip, block in enumerate(shared_back)]
     so_far = collect_whole(full, queries.shape, whole_back)

time: 139 us -> 139 us (level)
  Pallas kernels: 35.1 us -> 39.9 us
  waiting for transfers between devices: 60.7 us -> 56.4 us
    ppermute x8, waiting for transfers between devices: 55.7 us -> 50.4 us  [with_partner(): lax.ppermute(block, 'seq', [(i, i ^ 2 * k) for i in range(devices)])]
    pallas_call x1 -> x2, Pallas kernels: 6.38 us -> 11.3 us  [attend_shared(): pl.pallas_call(functools.partial(attend_shared_kernel, full, odd), name='...]
  transfers between devices with their start and end apart: 11 -> 11, of which waited for: 6 -> 7; matrix products, arithmetic and copies ran while one was open for 3% -> 3% of each run, Pallas kernels for 21% -> 25%
where the time goes in v7:
time: 139 us; the launch traced here: 138 us
  waiting for transfers between devices  56.4 us (41%)
  Pallas kernels  39.9 us (29%)
  starting transfers between devices  36.9 us (27%)
  local copies, waits for them, and re-layouts  3.64 us (3%)
    ppermute x8, waiting for transfers between devices, with_partner(): lax.ppermute(block, 'seq', [(i, i ^ 2 * k) for i in range(devices)])  50.4 us
    ppermute x8, starting transfers between devices, with_partner(): lax.ppermute(block, 'seq', [(i, i ^ 2 * k) for i in range(devices)])  22 us
    all_to_all x2, starting transfers between devices, with_all(): lax.all_to_all(blocks, 'seq', split_axis=0, concat_axis=0, tiled=True)  14.5 us
    pallas_call x1, Pallas kernels, attend_whole(): pl.pallas_call(functools.partial(attend_whole_kernel, full), name='attend...  13.5 us
    pallas_call x2, Pallas kernels, attend_shared(): pl.pallas_call(functools.partial(attend_shared_kernel, full, odd), name='...  11.3 us
    pallas_call x1, Pallas kernels, prepare_whole(): pl.pallas_call(functools.partial(prepare_whole_kernel, full), name='prepa...  4.61 us
    all_to_all x2, waiting for transfers between devices, with_all(): lax.all_to_all(blocks, 'seq', split_axis=0, concat_axis=0, tiled=True)  4.46 us
    pallas_call x1, Pallas kernels, prepare_shared(): pl.pallas_call(functools.partial(prepare_shared_kernel, full), name='prep...  3.61 us
  transfers between devices with their start and end apart: 11, of which 7 were waited for; matrix products, arithmetic and copies ran while one was open for 3% of the time, Pallas kernels for 25%

profile of v7, /device:TPU:0, one launch (start us, length us, event | category | flops | bytes accessed | tf_op | source)
XLA Modules:
  0.0 138.3 jit_solution(14449116814918408492)
XLA Ops:
  0.0 4.6 %prepare_whole.1 = bf16[16,768,128]{2,1,0:T(8,128)(2,1)} custom-call(bf16[128,5120]{1,0:T(8,128)(2,1)} %refs_0_.2, bf16[128,5120]{1,0:T(8,128)(2,1)} %refs_1_.3, bf16[128,5120]{1,0:T(8,128)(2,1)} %refs_2_.3, f32[5120]{0:T(1024)} %refs_3_.3, f32[5120]{0:T(1024)} %refs_4_.3), custom_call_target="tpu_custom_call" | custom-call | tf_op jit(solution)/shard_map/prepare_whole/pallas_call | solution.py:243
  4.6 7.6 %all-to-all-start = ((bf16[16,768,128]{2,1,0:T(8,128)(2,1)}), bf16[16,768,128]{2,1,0:T(8,128)(2,1)}, u32[]{:S(2)}, u32[]{:S(2)}) async-start(bf16[16,768,128]{2,1,0:T(8,128)(2,1)} %prepare_whole.1), calls=%async_computation | async-start | bytes 6291456 | tf_op jit(solution)/shard_map/all_to_all | solution.py:517
  12.5 0.2 copy.12
  12.7 0.6 gather_fusion
  13.3 0.5 gather_fusion.1
  13.9 0.2 select_reduce_fusion
  14.1 1.1 gather_fusion.2
  15.2 0.7 fusion.6.mask_ref
  15.9 3.6 %prepare_shared.1 = (bf16[4,384,128]{2,1,0:T(8,128)(2,1)}, bf16[4,384,128]{2,1,0:T(8,128)(2,1)}) custom-call(s32[1]{0:T(128)} %bitcast.me_ref, bf16[128,5120]{1,0:T(8,128)(2,1)} %refs_0_.2, bf16[128,5120]{1,0:T(8,128)(2,1)} %refs_1_.3, bf16[128,5120]{1,0:T(8,128)(2,1)} %refs_2_.3, f32[5120]{0:T(1024)} %refs_3_.3, f32[5120]{0:T(1024)} %refs_4_.3), custom_call_target="tpu_custom_call" | custom-call | tf_op jit(solution)/shard_map/prepare_shared/pallas_call | solution.py:255
  19.5 1.9 %collective-permute-start = (bf16[4,384,128]{2,1,0:T(8,128)(2,1)}, bf16[4,384,128]{2,1,0:T(8,128)(2,1)S(1)}, u32[]{:S(2)}, u32[]{:S(2)}) collective-permute-start(bf16[4,384,128]{2,1,0:T(8,128)(2,1)} %get-tuple-element.27), channel_id=1, source_target_pairs={{0,2},{1,3},{2,0},{3,1},{4,6},{5,7},{6,4},{7,5},{8,10},{9,11},{10,... | collective-permute-start | bytes 1179656 | tf_op jit(solution)/shard_map/ppermute | solution.py:522
  21.4 25.3 %collective-permute-done.other = bf16[4,384,128]{2,1,0:T(8,128)(2,1)S(1)} collective-permute-done((bf16[4,384,128]{2,1,0:T(8,128)(2,1)}, bf16[4,384,128]{2,1,0:T(8,128)(2,1)S(1)}, u32[]{:S(2)}, u32[]{:S(2)}) %collective-permute-start) | collective-permute-done | bytes 393248 | tf_op jit(solution)/shard_map/ppermute | solution.py:522
  46.8 1.0 copy-done
  47.8 2.3 %join_columns.2 = (bf16[768,128]{1,0:T(8,128)(2,1)S(1)}, bf16[768,128]{1,0:T(8,128)(2,1)S(1)}, bf16[768,128]{1,0:T(8,128)(2,1)S(1)}, bf16[768,128]{1,0:T(8,128)(2,1)S(1)}) custom-call(bf16[4,384,128]{2,1,0:T(8,128)(2,1)S(1)} %copy-done, bf16[4,384,128]{2,1,0:T(8,128)(2,1)S(1)} %collective-permute-done.other), custom_call_target="tpu_custom_call" | custom-call | tf_op jit(solution)/shard_map/join_columns/pallas_call | solution.py:282
  50.1 18.1 %collective-permute-done.1.refs_1_ = bf16[768,128]{1,0:T(8,128)(2,1)S(1)} collective-permute-done((bf16[768,128]{1,0:T(8,128)(2,1)S(1)}, bf16[768,128]{1,0:T(8,128)(2,1)S(1)}, u32[]{:S(2)}, u32[]{:S(2)}) %collective-permute-start.1) | collective-permute-done | bytes 196640 | tf_op jit(solution)/shard_map/ppermute | solution.py:522
  68.2 3.5 %all-to-all-done.here = bf16[16,768,128]{2,1,0:T(8,128)(2,1)} async-done(((bf16[16,768,128]{2,1,0:T(8,128)(2,1)}), bf16[16,768,128]{2,1,0:T(8,128)(2,1)}, u32[]{:S(2)}, u32[]{:S(2)}) %all-to-all-start) | async-done | bytes 3145760 | tf_op jit(solution)/shard_map/all_to_all | solution.py:517
  71.7 13.5 %collective-permute-start.2 = (bf16[768,128]{1,0:T(8,128)(2,1)S(1)}, bf16[768,128]{1,0:T(8,128)(2,1)S(1)}, u32[]{:S(2)}, u32[]{:S(2)}) collective-permute-start(bf16[768,128]{1,0:T(8,128)(2,1)S(1)} %get-tuple-element.33), channel_id=1, source_target_pairs={{0,8},{1,9},{2,10},{3,11},{4,12},{5,13},{6,14},{7,15},{8,0},{9,1},... | collective-permute-start | bytes 589832 | tf_op jit(solution)/shard_map/ppermute | solution.py:522
  85.2 13.5 %attend_whole.1 = bf16[16,256,128]{2,1,0:T(8,128)(2,1)} custom-call(s32[3,16]{1,0:T(4,128)} %fusion.6.mask_ref, bf16[16,768,128]{2,1,0:T(8,128)(2,1)} %all-to-all-done.here), custom_call_target="tpu_custom_call" | custom-call | tf_op jit(solution)/shard_map/attend_whole/pallas_call | solution.py:384
  98.8 7.0 %all-to-all-start.1 = ((bf16[16,256,128]{2,1,0:T(8,128)(2,1)}), bf16[16,256,128]{2,1,0:T(8,128)(2,1)S(1)}, u32[]{:S(2)}, u32[]{:S(2)}) async-start(bf16[16,256,128]{2,1,0:T(8,128)(2,1)} %attend_whole.1), calls=%async_computation.1 | async-start | bytes 2097152 | tf_op jit(solution)/shard_map/all_to_all | solution.py:517
  105.7 1.5 %join_keys_values.1 = bf16[8,256,128]{2,1,0:T(8,128)(2,1)S(1)} custom-call(bf16[768,128]{1,0:T(8,128)(2,1)S(1)} %get-tuple-element.35.refs_0_, bf16[768,128]{1,0:T(8,128)(2,1)S(1)} %collective-permute-done.1.refs_1_, bf16[768,128]{1,0:T(8,128)(2,1)S(1)} %collective-permute-done.2.refs_2_, bf16[768,128]{1,0:T(8,128)(2,1)S(1)} %collective-permute-done.3.refs_3_), custom_call_target="tpu_custom_call" | custom-call | tf_op jit(solution)/shard_map/join_keys_values/pallas_call | solution.py:451
  107.3 0.5 collective-permute-start.4
  107.7 1.5 %collective-permute-done.4.refs_4_ = bf16[8,256,128]{2,1,0:T(8,128)(2,1)S(1)} collective-permute-done((bf16[8,256,128]{2,1,0:T(8,128)(2,1)S(1)}, bf16[8,256,128]{2,1,0:T(8,128)(2,1)S(1)}, u32[]{:S(2)}, u32[]{:S(2)}) %collective-permute-start.4) | collective-permute-done | bytes 524320 | tf_op jit(solution)/shard_map/ppermute | solution.py:526
  109.3 5.6 %attend_shared.2 = bf16[4,128,128]{2,1,0:T(8,128)(2,1)S(1)} custom-call(s32[3,16]{1,0:T(4,128)S(1)} %copy-done.1, bf16[768,128]{1,0:T(8,128)(2,1)S(1)} %get-tuple-element.35.refs_0_, bf16[768,128]{1,0:T(8,128)(2,1)S(1)} %collective-permute-done.1.refs_1_, bf16[768,128]{1,0:T(8,128)(2,1)S(1)} %collective-permute-done.2.refs_2_, ...), custom_call_target="tpu_custom_call" | custom-call | tf_op jit(solution)/shard_map/attend_shared/pallas_call | solution.py:419
  114.9 2.0 %collective-permute-start.5 = (bf16[4,128,128]{2,1,0:T(8,128)(2,1)S(1)}, bf16[4,128,128]{2,1,0:T(8,128)(2,1)S(1)}, u32[]{:S(2)}, u32[]{:S(2)}) collective-permute-start(bf16[4,128,128]{2,1,0:T(8,128)(2,1)S(1)} %attend_shared.2), channel_id=1, source_target_pairs={{0,2},{1,3},{2,0},{3,1},{4,6},{5,7},{6,4},{7,5},{8,10},{9,11},{10,... | collective-permute-start | bytes 393224 | tf_op jit(solution)/shard_map/ppermute | solution.py:522
  116.9 5.6 %attend_shared.3.own = bf16[4,128,128]{2,1,0:T(8,128)(2,1)S(1)} custom-call(s32[3,16]{1,0:T(4,128)S(1)} %copy-done.1, bf16[768,128]{1,0:T(8,128)(2,1)S(1)} %get-tuple-element.35.refs_0_, bf16[768,128]{1,0:T(8,128)(2,1)S(1)} %collective-permute-done.1.refs_1_, bf16[768,128]{1,0:T(8,128)(2,1)S(1)} %collective-permute-done.2.refs_2_, ...), custom_call_target="tpu_custom_call" | custom-call | tf_op jit(solution)/shard_map/attend_shared/pallas_call | solution.py:419
  122.5 0.4 collective-permute-done.5.other
  122.9 0.8 join_columns.3
  123.7 1.1 collective-permute-start.6
  124.8 3.3 %collective-permute-start.7 = (bf16[256,128]{1,0:T(8,128)(2,1)S(1)}, bf16[256,128]{1,0:T(8,128)(2,1)S(1)}, u32[]{:S(2)}, u32[]{:S(2)}) collective-permute-start(bf16[256,128]{1,0:T(8,128)(2,1)S(1)} %get-tuple-element.42), channel_id=1, source_target_pairs={{0,8},{1,9},{2,10},{3,11},{4,12},{5,13},{6,14},{7,15},{8,0},{9,1},... | collective-permute-start | bytes 196616 | tf_op jit(solution)/shard_map/ppermute | solution.py:522
  128.1 1.0 all-to-all-done.1.here
  129.1 1.2 collect_whole.1.refs_4_
  130.4 6.6 %collective-permute-done.7.refs_2_ = bf16[256,128]{1,0:T(8,128)(2,1)S(1)} collective-permute-done((bf16[256,128]{1,0:T(8,128)(2,1)S(1)}, bf16[256,128]{1,0:T(8,128)(2,1)S(1)}, u32[]{:S(2)}, u32[]{:S(2)}) %collective-permute-start.7) | collective-permute-done | bytes 65568 | tf_op jit(solution)/shard_map/ppermute | solution.py:522
  137.0 1.1 collect_shared.1
  (21 shorter events, 0.4 us)
Async XLA Ops:
  4.6 7.8 %copy-start.3 = (s32[40,16]{0,1:T(8,128)S(1)}, s32[40,16]{0,1:T(8,128)}, u32[]{:S(2)}) copy-start(s32[40,16]{0,1:T(8,128)} %param.13) | copy-start | bytes 7684
  4.6 7.9 %copy-start.2 = (s32[40,16,16]{0,2,1:T(8,128)S(1)}, s32[40,16,16]{0,2,1:T(8,128)}, u32[]{:S(2)}) copy-start(s32[40,16,16]{0,2,1:T(8,128)} %param.12) | copy-start | bytes 122884
  4.6 67.0 %all-to-all-start = ((bf16[16,768,128]{2,1,0:T(8,128)(2,1)}), bf16[16,768,128]{2,1,0:T(8,128)(2,1)}, u32[]{:S(2)}, u32[]{:S(2)}) async-start(bf16[16,768,128]{2,1,0:T(8,128)(2,1)} %prepare_whole.1), calls=%async_computation | async-start | bytes 6291456 | tf_op jit(solution)/shard_map/all_to_all | solution.py:517
  19.5 27.2 %collective-permute-start = (bf16[4,384,128]{2,1,0:T(8,128)(2,1)}, bf16[4,384,128]{2,1,0:T(8,128)(2,1)S(1)}, u32[]{:S(2)}, u32[]{:S(2)}) collective-permute-start(bf16[4,384,128]{2,1,0:T(8,128)(2,1)} %get-tuple-element.27), channel_id=1, source_target_pairs={{0,2},{1,3},{2,0},{3,1},{4,6},{5,7},{6,4},{7,5},{8,10},{9,11},{10,... | collective-permute-start | bytes 1179656 | tf_op jit(solution)/shard_map/ppermute | solution.py:522
  46.8 1.0 copy-start
  50.1 18.2 %collective-permute-start.1 = (bf16[768,128]{1,0:T(8,128)(2,1)S(1)}, bf16[768,128]{1,0:T(8,128)(2,1)S(1)}, u32[]{:S(2)}, u32[]{:S(2)}) collective-permute-start(bf16[768,128]{1,0:T(8,128)(2,1)S(1)} %get-tuple-element.29), channel_id=1, source_target_pairs={{0,4},{1,5},{2,6},{3,7},{4,0},{5,1},{6,2},{7,3},{8,12},{9,13},{10,... | collective-permute-start | bytes 589832 | tf_op jit(solution)/shard_map/ppermute | solution.py:522
  71.7 27.1 %collective-permute-start.2 = (bf16[768,128]{1,0:T(8,128)(2,1)S(1)}, bf16[768,128]{1,0:T(8,128)(2,1)S(1)}, u32[]{:S(2)}, u32[]{:S(2)}) collective-permute-start(bf16[768,128]{1,0:T(8,128)(2,1)S(1)} %get-tuple-element.33), channel_id=1, source_target_pairs={{0,8},{1,9},{2,10},{3,11},{4,12},{5,13},{6,14},{7,15},{8,0},{9,1},... | collective-permute-start | bytes 589832 | tf_op jit(solution)/shard_map/ppermute | solution.py:522
  85.2 13.5 %collective-permute-start.3 = (bf16[768,128]{1,0:T(8,128)(2,1)S(1)}, bf16[768,128]{1,0:T(8,128)(2,1)S(1)}, u32[]{:S(2)}, u32[]{:S(2)}) collective-permute-start(bf16[768,128]{1,0:T(8,128)(2,1)S(1)} %get-tuple-element.34), channel_id=1, source_target_pairs={{0,12},{1,13},{2,14},{3,15},{4,8},{5,9},{6,10},{7,11},{8,4},{9,5},... | collective-permute-start | bytes 589832 | tf_op jit(solution)/shard_map/ppermute | solution.py:522
  98.7 10.5 %copy-start.1 = (s32[3,16]{1,0:T(4,128)S(1)}, s32[3,16]{1,0:T(4,128)}, u32[]{:S(2)}) copy-start(s32[3,16]{1,0:T(4,128)} %fusion.6.mask_ref) | copy-start | bytes 580
  98.8 30.4 %all-to-all-start.1 = ((bf16[16,256,128]{2,1,0:T(8,128)(2,1)}), bf16[16,256,128]{2,1,0:T(8,128)(2,1)S(1)}, u32[]{:S(2)}, u32[]{:S(2)}) async-start(bf16[16,256,128]{2,1,0:T(8,128)(2,1)} %attend_whole.1), calls=%async_computation.1 | async-start | bytes 2097152 | tf_op jit(solution)/shard_map/all_to_all | solution.py:517
  107.3 2.0 %collective-permute-start.4 = (bf16[8,256,128]{2,1,0:T(8,128)(2,1)S(1)}, bf16[8,256,128]{2,1,0:T(8,128)(2,1)S(1)}, u32[]{:S(2)}, u32[]{:S(2)}) collective-permute-start(bf16[8,256,128]{2,1,0:T(8,128)(2,1)S(1)} %join_keys_values.1), channel_id=1, source_target_pairs={{0,1},{1,0},{2,3},{3,2},{4,5},{5,4},{6,7},{7,6},{8,9},{9,8},{10,11... | collective-permute-start | bytes 1572872 | tf_op jit(solution)/shard_map/ppermute | solution.py:526
  114.9 8.0 %collective-permute-start.5 = (bf16[4,128,128]{2,1,0:T(8,128)(2,1)S(1)}, bf16[4,128,128]{2,1,0:T(8,128)(2,1)S(1)}, u32[]{:S(2)}, u32[]{:S(2)}) collective-permute-start(bf16[4,128,128]{2,1,0:T(8,128)(2,1)S(1)} %attend_shared.2), channel_id=1, source_target_pairs={{0,2},{1,3},{2,0},{3,1},{4,6},{5,7},{6,4},{7,5},{8,10},{9,11},{10,... | collective-permute-start | bytes 393224 | tf_op jit(solution)/shard_map/ppermute | solution.py:522
  123.7 6.7 %collective-permute-start.6 = (bf16[256,128]{1,0:T(8,128)(2,1)S(1)}, bf16[256,128]{1,0:T(8,128)(2,1)S(1)}, u32[]{:S(2)}, u32[]{:S(2)}) collective-permute-start(bf16[256,128]{1,0:T(8,128)(2,1)S(1)} %get-tuple-element.41), channel_id=1, source_target_pairs={{0,4},{1,5},{2,6},{3,7},{4,0},{5,1},{6,2},{7,3},{8,12},{9,13},{10,... | collective-permute-start | bytes 196616 | tf_op jit(solution)/shard_map/ppermute | solution.py:522
  124.8 12.1 %collective-permute-start.7 = (bf16[256,128]{1,0:T(8,128)(2,1)S(1)}, bf16[256,128]{1,0:T(8,128)(2,1)S(1)}, u32[]{:S(2)}, u32[]{:S(2)}) collective-permute-start(bf16[256,128]{1,0:T(8,128)(2,1)S(1)} %get-tuple-element.42), channel_id=1, source_target_pairs={{0,8},{1,9},{2,10},{3,11},{4,12},{5,13},{6,14},{7,15},{8,0},{9,1},... | collective-permute-start | bytes 196616 | tf_op jit(solution)/shard_map/ppermute | solution.py:522
  128.1 8.8 %collective-permute-start.8 = (bf16[256,128]{1,0:T(8,128)(2,1)S(1)}, bf16[256,128]{1,0:T(8,128)(2,1)S(1)}, u32[]{:S(2)}, u32[]{:S(2)}) collective-permute-start(bf16[256,128]{1,0:T(8,128)(2,1)S(1)} %get-tuple-element.43), channel_id=1, source_target_pairs={{0,12},{1,13},{2,14},{3,15},{4,8},{5,9},{6,10},{7,11},{8,4},{9,5},... | collective-permute-start | bytes 196616 | tf_op jit(solution)/shard_map/ppermute | solution.py:522

commit v8 on v6

--- a/solution.py
+++ b/solution.py
@@ -563,7 +563,7 @@
     shared = join_columns(even, with_partner(odd, 1))
     near, far = shared[: pairs // 4], shared[pairs // 4 :]
     near = [with_partner(block, 2 * flip) for flip, block in enumerate(near)]
-    whole = after(whole, *near, *far)
+    whole = after(whole, *far)
     far = all_after(far, whole)
     far = [with_partner(block, 2 * flip + pairs // 2) for flip, block in enumerate(far)]
     whole_out = attend_whole(full, masks, whole)

time: 139 us -> 139 us (level)
    all_to_all x2, waiting for transfers between devices: 3.47 us -> 21.6 us  [with_all(): lax.all_to_all(blocks, 'seq', split_axis=0, concat_axis=0, tiled=True)]
    ppermute x8, waiting for transfers between devices: 55.7 us -> 37.6 us  [with_partner(): lax.ppermute(block, 'seq', [(i, i ^ 2 * k) for i in range(devices)])]
  transfers between devices with their start and end apart: 11 -> 11, of which waited for: 6 -> 5; matrix products, arithmetic and copies ran while one was open for 3% -> 3% of each run, Pallas kernels for 21% -> 21%
where the time goes in v8:
time: 139 us
  waiting for transfers between devices  60.7 us (44%)
  starting transfers between devices  37.7 us (27%)
  Pallas kernels  35.1 us (25%)
  local copies, waits for them, and re-layouts  3.64 us (3%)
    ppermute x8, waiting for transfers between devices, with_partner(): lax.ppermute(block, 'seq', [(i, i ^ 2 * k) for i in range(devices)])  37.6 us
    ppermute x8, starting transfers between devices, with_partner(): lax.ppermute(block, 'seq', [(i, i ^ 2 * k) for i in range(devices)])  22.6 us
    all_to_all x2, waiting for transfers between devices, with_all(): lax.all_to_all(blocks, 'seq', split_axis=0, concat_axis=0, tiled=True)  21.6 us
    all_to_all x2, starting transfers between devices, with_all(): lax.all_to_all(blocks, 'seq', split_axis=0, concat_axis=0, tiled=True)  14.7 us
    pallas_call x1, Pallas kernels, attend_whole(): pl.pallas_call(functools.partial(attend_whole_kernel, full), name='attend...  13.5 us
    pallas_call x1, Pallas kernels, attend_shared(): pl.pallas_call(functools.partial(attend_shared_kernel, full), name='atten...  6.38 us
    pallas_call x1, Pallas kernels, prepare_whole(): pl.pallas_call(functools.partial(prepare_whole_kernel, full), name='prepa...  4.69 us
    pallas_call x1, Pallas kernels, prepare_shared(): pl.pallas_call(functools.partial(prepare_shared_kernel, full), name='prep...  3.63 us
  transfers between devices with their start and end apart: 11, of which 5 were waited for; matrix products, arithmetic and copies ran while one was open for 3% of the time, Pallas kernels for 21%

profile of v8, /device:TPU:0, one launch (start us, length us, event | category | flops | bytes accessed | tf_op | source)
XLA Modules:
  0.0 138.5 jit_solution(2919231725771555634)
XLA Ops:
  0.0 4.7 %prepare_whole.1 = bf16[16,768,128]{2,1,0:T(8,128)(2,1)} custom-call(bf16[128,5120]{1,0:T(8,128)(2,1)} %refs_0_.2, bf16[128,5120]{1,0:T(8,128)(2,1)} %refs_1_.3, bf16[128,5120]{1,0:T(8,128)(2,1)} %refs_2_.3, f32[5120]{0:T(1024)} %refs_3_.3, f32[5120]{0:T(1024)} %refs_4_.3), custom_call_target="tpu_custom_call" | custom-call | tf_op jit(solution)/shard_map/prepare_whole/pallas_call | solution.py:243
  4.7 7.6 %all-to-all-start = ((bf16[16,768,128]{2,1,0:T(8,128)(2,1)}), bf16[16,768,128]{2,1,0:T(8,128)(2,1)}, u32[]{:S(2)}, u32[]{:S(2)}) async-start(bf16[16,768,128]{2,1,0:T(8,128)(2,1)} %prepare_whole.1), calls=%async_computation | async-start | bytes 6291456 | tf_op jit(solution)/shard_map/all_to_all | solution.py:518
  12.4 0.1 reshape.116
  12.6 0.2 copy.12
  12.8 0.6 gather_fusion
  13.4 0.5 gather_fusion.1
  13.9 0.2 select_reduce_fusion
  14.2 1.1 gather_fusion.2
  15.2 0.1 reshape.119
  15.3 0.7 fusion.6.mask_ref
  16.0 3.6 %prepare_shared.1 = (bf16[4,384,128]{2,1,0:T(8,128)(2,1)}, bf16[4,384,128]{2,1,0:T(8,128)(2,1)}) custom-call(s32[1]{0:T(128)} %bitcast.me_ref, bf16[128,5120]{1,0:T(8,128)(2,1)} %refs_0_.2, bf16[128,5120]{1,0:T(8,128)(2,1)} %refs_1_.3, bf16[128,5120]{1,0:T(8,128)(2,1)} %refs_2_.3, f32[5120]{0:T(1024)} %refs_3_.3, f32[5120]{0:T(1024)} %refs_4_.3), custom_call_target="tpu_custom_call" | custom-call | tf_op jit(solution)/shard_map/prepare_shared/pallas_call | solution.py:255
  19.6 1.9 %collective-permute-start = (bf16[4,384,128]{2,1,0:T(8,128)(2,1)}, bf16[4,384,128]{2,1,0:T(8,128)(2,1)S(1)}, u32[]{:S(2)}, u32[]{:S(2)}) collective-permute-start(bf16[4,384,128]{2,1,0:T(8,128)(2,1)} %get-tuple-element.28), channel_id=1, source_target_pairs={{0,2},{1,3},{2,0},{3,1},{4,6},{5,7},{6,4},{7,5},{8,10},{9,11},{10,... | collective-permute-start | bytes 1179656 | tf_op jit(solution)/shard_map/ppermute | solution.py:523
  21.5 25.3 %collective-permute-done.other = bf16[4,384,128]{2,1,0:T(8,128)(2,1)S(1)} collective-permute-done((bf16[4,384,128]{2,1,0:T(8,128)(2,1)}, bf16[4,384,128]{2,1,0:T(8,128)(2,1)S(1)}, u32[]{:S(2)}, u32[]{:S(2)}) %collective-permute-start) | collective-permute-done | bytes 393248 | tf_op jit(solution)/shard_map/ppermute | solution.py:523
  46.8 1.0 copy-done
  47.8 2.3 %join_columns.2 = (bf16[768,128]{1,0:T(8,128)(2,1)S(1)}, bf16[768,128]{1,0:T(8,128)(2,1)S(1)}, bf16[768,128]{1,0:T(8,128)(2,1)S(1)}, bf16[768,128]{1,0:T(8,128)(2,1)S(1)}) custom-call(bf16[4,384,128]{2,1,0:T(8,128)(2,1)S(1)} %copy-done, bf16[4,384,128]{2,1,0:T(8,128)(2,1)S(1)} %collective-permute-done.other), custom_call_target="tpu_custom_call" | custom-call | tf_op jit(solution)/shard_map/join_columns/pallas_call | solution.py:282
  50.2 21.6 %all-to-all-done.here = bf16[16,768,128]{2,1,0:T(8,128)(2,1)} async-done(((bf16[16,768,128]{2,1,0:T(8,128)(2,1)}), bf16[16,768,128]{2,1,0:T(8,128)(2,1)}, u32[]{:S(2)}, u32[]{:S(2)}) %all-to-all-start) | async-done | bytes 3145760 | tf_op jit(solution)/shard_map/all_to_all | solution.py:518
  71.8 13.5 %collective-permute-start.2 = (bf16[768,128]{1,0:T(8,128)(2,1)S(1)}, bf16[768,128]{1,0:T(8,128)(2,1)S(1)}, u32[]{:S(2)}, u32[]{:S(2)}) collective-permute-start(bf16[768,128]{1,0:T(8,128)(2,1)S(1)} %get-tuple-element.34), channel_id=1, source_target_pairs={{0,8},{1,9},{2,10},{3,11},{4,12},{5,13},{6,14},{7,15},{8,0},{9,1},... | collective-permute-start | bytes 589832 | tf_op jit(solution)/shard_map/ppermute | solution.py:523
  85.3 13.5 %attend_whole.1 = bf16[16,256,128]{2,1,0:T(8,128)(2,1)} custom-call(s32[3,16]{1,0:T(4,128)} %fusion.6.mask_ref, bf16[16,768,128]{2,1,0:T(8,128)(2,1)} %all-to-all-done.here), custom_call_target="tpu_custom_call" | custom-call | tf_op jit(solution)/shard_map/attend_whole/pallas_call | solution.py:384
  98.9 7.1 %all-to-all-start.1 = ((bf16[16,256,128]{2,1,0:T(8,128)(2,1)}), bf16[16,256,128]{2,1,0:T(8,128)(2,1)S(1)}, u32[]{:S(2)}, u32[]{:S(2)}) async-start(bf16[16,256,128]{2,1,0:T(8,128)(2,1)} %attend_whole.1), calls=%async_computation.1 | async-start | bytes 2097152 | tf_op jit(solution)/shard_map/all_to_all | solution.py:518
  106.0 1.5 %join_keys_values.1 = bf16[8,256,128]{2,1,0:T(8,128)(2,1)S(1)} custom-call(bf16[768,128]{1,0:T(8,128)(2,1)S(1)} %get-tuple-element.36.refs_0_, bf16[768,128]{1,0:T(8,128)(2,1)S(1)} %collective-permute-done.1.refs_1_, bf16[768,128]{1,0:T(8,128)(2,1)S(1)} %collective-permute-done.2.refs_2_, bf16[768,128]{1,0:T(8,128)(2,1)S(1)} %collective-permute-done.3.refs_3_), custom_call_target="tpu_custom_call" | custom-call | tf_op jit(solution)/shard_map/join_keys_values/pallas_call | solution.py:452
  107.5 0.5 collective-permute-start.4
  107.9 1.5 %collective-permute-done.4.refs_4_ = bf16[8,256,128]{2,1,0:T(8,128)(2,1)S(1)} collective-permute-done((bf16[8,256,128]{2,1,0:T(8,128)(2,1)S(1)}, bf16[8,256,128]{2,1,0:T(8,128)(2,1)S(1)}, u32[]{:S(2)}, u32[]{:S(2)}) %collective-permute-start.4) | collective-permute-done | bytes 524320 | tf_op jit(solution)/shard_map/ppermute | solution.py:527
  109.5 6.4 %attend_shared.1 = (bf16[4,128,128]{2,1,0:T(8,128)(2,1)S(1)}, bf16[4,128,128]{2,1,0:T(8,128)(2,1)S(1)}) custom-call(s32[3,16]{1,0:T(4,128)S(1)} %copy-done.1, bf16[768,128]{1,0:T(8,128)(2,1)S(1)} %get-tuple-element.36.refs_0_, bf16[768,128]{1,0:T(8,128)(2,1)S(1)} %collective-permute-done.1.refs_1_, bf16[768,128]{1,0:T(8,128)(2,1)S(1)} %collective-permute-done.2.refs_2_, ...), custom_call_target="tpu_custom_call" | custom-call | tf_op jit(solution)/shard_map/attend_shared/pallas_call | solution.py:420
  115.9 2.0 %collective-permute-start.5 = (bf16[4,128,128]{2,1,0:T(8,128)(2,1)S(1)}, bf16[4,128,128]{2,1,0:T(8,128)(2,1)S(1)}, u32[]{:S(2)}, u32[]{:S(2)}) collective-permute-start(bf16[4,128,128]{2,1,0:T(8,128)(2,1)S(1)} %get-tuple-element.41), channel_id=1, source_target_pairs={{0,2},{1,3},{2,0},{3,1},{4,6},{5,7},{6,4},{7,5},{8,10},{9,11},{10,... | collective-permute-start | bytes 393224 | tf_op jit(solution)/shard_map/ppermute | solution.py:523
  117.8 5.6 %collective-permute-done.5.other = bf16[4,128,128]{2,1,0:T(8,128)(2,1)S(1)} collective-permute-done((bf16[4,128,128]{2,1,0:T(8,128)(2,1)S(1)}, bf16[4,128,128]{2,1,0:T(8,128)(2,1)S(1)}, u32[]{:S(2)}, u32[]{:S(2)}) %collective-permute-start.5) | collective-permute-done | bytes 131104 | tf_op jit(solution)/shard_map/ppermute | solution.py:523
  123.4 0.8 join_columns.3
  124.2 1.4 %collective-permute-start.6 = (bf16[256,128]{1,0:T(8,128)(2,1)S(1)}, bf16[256,128]{1,0:T(8,128)(2,1)S(1)}, u32[]{:S(2)}, u32[]{:S(2)}) collective-permute-start(bf16[256,128]{1,0:T(8,128)(2,1)S(1)} %get-tuple-element.43), channel_id=1, source_target_pairs={{0,4},{1,5},{2,6},{3,7},{4,0},{5,1},{6,2},{7,3},{8,12},{9,13},{10,... | collective-permute-start | bytes 196616 | tf_op jit(solution)/shard_map/ppermute | solution.py:523
  125.6 3.2 %collective-permute-start.7 = (bf16[256,128]{1,0:T(8,128)(2,1)S(1)}, bf16[256,128]{1,0:T(8,128)(2,1)S(1)}, u32[]{:S(2)}, u32[]{:S(2)}) collective-permute-start(bf16[256,128]{1,0:T(8,128)(2,1)S(1)} %get-tuple-element.44), channel_id=1, source_target_pairs={{0,8},{1,9},{2,10},{3,11},{4,12},{5,13},{6,14},{7,15},{8,0},{9,1},... | collective-permute-start | bytes 196616 | tf_op jit(solution)/shard_map/ppermute | solution.py:523
  128.9 0.4 collective-permute-start.8
  129.3 1.2 collect_whole.1.refs_4_
  130.5 6.7 %collective-permute-done.7.refs_2_ = bf16[256,128]{1,0:T(8,128)(2,1)S(1)} collective-permute-done((bf16[256,128]{1,0:T(8,128)(2,1)S(1)}, bf16[256,128]{1,0:T(8,128)(2,1)S(1)}, u32[]{:S(2)}, u32[]{:S(2)}) %collective-permute-start.7) | collective-permute-done | bytes 65568 | tf_op jit(solution)/shard_map/ppermute | solution.py:523
  137.2 1.1 collect_shared.1
  (20 shorter events, 0.3 us)
Async XLA Ops:
  4.7 7.8 %copy-start.3 = (s32[40,16]{0,1:T(8,128)S(1)}, s32[40,16]{0,1:T(8,128)}, u32[]{:S(2)}) copy-start(s32[40,16]{0,1:T(8,128)} %param.13) | copy-start | bytes 7684
  4.7 7.9 %copy-start.2 = (s32[40,16,16]{0,2,1:T(8,128)S(1)}, s32[40,16,16]{0,2,1:T(8,128)}, u32[]{:S(2)}) copy-start(s32[40,16,16]{0,2,1:T(8,128)} %param.12) | copy-start | bytes 122884
  4.7 67.0 %all-to-all-start = ((bf16[16,768,128]{2,1,0:T(8,128)(2,1)}), bf16[16,768,128]{2,1,0:T(8,128)(2,1)}, u32[]{:S(2)}, u32[]{:S(2)}) async-start(bf16[16,768,128]{2,1,0:T(8,128)(2,1)} %prepare_whole.1), calls=%async_computation | async-start | bytes 6291456 | tf_op jit(solution)/shard_map/all_to_all | solution.py:518
  19.6 27.2 %collective-permute-start = (bf16[4,384,128]{2,1,0:T(8,128)(2,1)}, bf16[4,384,128]{2,1,0:T(8,128)(2,1)S(1)}, u32[]{:S(2)}, u32[]{:S(2)}) collective-permute-start(bf16[4,384,128]{2,1,0:T(8,128)(2,1)} %get-tuple-element.28), channel_id=1, source_target_pairs={{0,2},{1,3},{2,0},{3,1},{4,6},{5,7},{6,4},{7,5},{8,10},{9,11},{10,... | collective-permute-start | bytes 1179656 | tf_op jit(solution)/shard_map/ppermute | solution.py:523
  46.8 1.0 copy-start
  50.1 48.7 %collective-permute-start.1 = (bf16[768,128]{1,0:T(8,128)(2,1)S(1)}, bf16[768,128]{1,0:T(8,128)(2,1)S(1)}, u32[]{:S(2)}, u32[]{:S(2)}) collective-permute-start(bf16[768,128]{1,0:T(8,128)(2,1)S(1)} %get-tuple-element.30), channel_id=1, source_target_pairs={{0,4},{1,5},{2,6},{3,7},{4,0},{5,1},{6,2},{7,3},{8,12},{9,13},{10,... | collective-permute-start | bytes 589832 | tf_op jit(solution)/shard_map/ppermute | solution.py:523
  71.8 27.1 %collective-permute-start.2 = (bf16[768,128]{1,0:T(8,128)(2,1)S(1)}, bf16[768,128]{1,0:T(8,128)(2,1)S(1)}, u32[]{:S(2)}, u32[]{:S(2)}) collective-permute-start(bf16[768,128]{1,0:T(8,128)(2,1)S(1)} %get-tuple-element.34), channel_id=1, source_target_pairs={{0,8},{1,9},{2,10},{3,11},{4,12},{5,13},{6,14},{7,15},{8,0},{9,1},... | collective-permute-start | bytes 589832 | tf_op jit(solution)/shard_map/ppermute | solution.py:523
  85.3 13.5 %collective-permute-start.3 = (bf16[768,128]{1,0:T(8,128)(2,1)S(1)}, bf16[768,128]{1,0:T(8,128)(2,1)S(1)}, u32[]{:S(2)}, u32[]{:S(2)}) collective-permute-start(bf16[768,128]{1,0:T(8,128)(2,1)S(1)} %get-tuple-element.35), channel_id=1, source_target_pairs={{0,12},{1,13},{2,14},{3,15},{4,8},{5,9},{6,10},{7,11},{8,4},{9,5},... | collective-permute-start | bytes 589832 | tf_op jit(solution)/shard_map/ppermute | solution.py:523
  98.9 10.6 %copy-start.1 = (s32[3,16]{1,0:T(4,128)S(1)}, s32[3,16]{1,0:T(4,128)}, u32[]{:S(2)}) copy-start(s32[3,16]{1,0:T(4,128)} %fusion.6.mask_ref) | copy-start | bytes 580
  98.9 30.4 %all-to-all-start.1 = ((bf16[16,256,128]{2,1,0:T(8,128)(2,1)}), bf16[16,256,128]{2,1,0:T(8,128)(2,1)S(1)}, u32[]{:S(2)}, u32[]{:S(2)}) async-start(bf16[16,256,128]{2,1,0:T(8,128)(2,1)} %attend_whole.1), calls=%async_computation.1 | async-start | bytes 2097152 | tf_op jit(solution)/shard_map/all_to_all | solution.py:518
  107.5 2.0 %collective-permute-start.4 = (bf16[8,256,128]{2,1,0:T(8,128)(2,1)S(1)}, bf16[8,256,128]{2,1,0:T(8,128)(2,1)S(1)}, u32[]{:S(2)}, u32[]{:S(2)}) collective-permute-start(bf16[8,256,128]{2,1,0:T(8,128)(2,1)S(1)} %join_keys_values.1), channel_id=1, source_target_pairs={{0,1},{1,0},{2,3},{3,2},{4,5},{5,4},{6,7},{7,6},{8,9},{9,8},{10,11... | collective-permute-start | bytes 1572872 | tf_op jit(solution)/shard_map/ppermute | solution.py:527
  115.9 7.5 %collective-permute-start.5 = (bf16[4,128,128]{2,1,0:T(8,128)(2,1)S(1)}, bf16[4,128,128]{2,1,0:T(8,128)(2,1)S(1)}, u32[]{:S(2)}, u32[]{:S(2)}) collective-permute-start(bf16[4,128,128]{2,1,0:T(8,128)(2,1)S(1)} %get-tuple-element.41), channel_id=1, source_target_pairs={{0,2},{1,3},{2,0},{3,1},{4,6},{5,7},{6,4},{7,5},{8,10},{9,11},{10,... | collective-permute-start | bytes 393224 | tf_op jit(solution)/shard_map/ppermute | solution.py:523
  124.2 6.3 %collective-permute-start.6 = (bf16[256,128]{1,0:T(8,128)(2,1)S(1)}, bf16[256,128]{1,0:T(8,128)(2,1)S(1)}, u32[]{:S(2)}, u32[]{:S(2)}) collective-permute-start(bf16[256,128]{1,0:T(8,128)(2,1)S(1)} %get-tuple-element.43), channel_id=1, source_target_pairs={{0,4},{1,5},{2,6},{3,7},{4,0},{5,1},{6,2},{7,3},{8,12},{9,13},{10,... | collective-permute-start | bytes 196616 | tf_op jit(solution)/shard_map/ppermute | solution.py:523
  125.6 11.6 %collective-permute-start.7 = (bf16[256,128]{1,0:T(8,128)(2,1)S(1)}, bf16[256,128]{1,0:T(8,128)(2,1)S(1)}, u32[]{:S(2)}, u32[]{:S(2)}) collective-permute-start(bf16[256,128]{1,0:T(8,128)(2,1)S(1)} %get-tuple-element.44), channel_id=1, source_target_pairs={{0,8},{1,9},{2,10},{3,11},{4,12},{5,13},{6,14},{7,15},{8,0},{9,1},... | collective-permute-start | bytes 196616 | tf_op jit(solution)/shard_map/ppermute | solution.py:523
  128.9 8.3 %collective-permute-start.8 = (bf16[256,128]{1,0:T(8,128)(2,1)S(1)}, bf16[256,128]{1,0:T(8,128)(2,1)S(1)}, u32[]{:S(2)}, u32[]{:S(2)}) collective-permute-start(bf16[256,128]{1,0:T(8,128)(2,1)S(1)} %get-tuple-element.45), channel_id=1, source_target_pairs={{0,12},{1,13},{2,14},{3,15},{4,8},{5,9},{6,10},{7,11},{8,4},{9,5},... | collective-permute-start | bytes 196616 | tf_op jit(solution)/shard_map/ppermute | solution.py:523
